TPU v7x, 128 devices: a whole 4x4x4 slice. The times are simulated.
128 devices in a mesh: pipe: 4 (over z_hi, core), dp: 32 (over z_lo, y, x).
Axes of the slice: x: 4, y: 4, z: 4 (z_hi: 2, z_lo: 2; z = z_hi * 2 + z_lo), core: 2. Of those that a mesh axis runs over, the one named last changes fastest.
Arguments:
- batches: bfloat16 [2, 128, 8192], P(None, None, 'dp'), may hold values from -6 to 6
- cotangents: bfloat16 [2, 128, 8192], P(None, None, 'dp'), may hold values from -1.5 to 1.5
- weights: bfloat16 [2, 4, 8192, 8192], P(None, 'pipe', None, 'dp'), may hold values from -0.044194174 to 0.54419417
- gains: bfloat16 [2, 4, 8192], P(None, 'pipe', 'dp'), may hold values from 0.4 to 3
- exponents: int32 [4, 64, 64], P('pipe', None, 'dp'), may hold values from -1 to 2
Outputs:
- weight_grads: bfloat16 [4, 8192, 8192], P('pipe', None, 'dp')
- last_states: bfloat16 [4, 128, 8192], P('pipe', None, 'dp')
All inputs are finite; a program needn't handle non-finite values.
Results may differ from a plain program's by a relative error of at most 0.025.
Values may be sent and summed in bfloat16 or wider, within the bound.
No kernel may reach another device: no remote copies, remote signals or barrier semaphores. Data moves between devices by JAX's collectives and lax.ppermute only.
A program may use at most 128 MiB of HBM per device.

v0:
```python
import jax
import jax.numpy as jnp
from jax import lax
from jax.sharding import PartitionSpec as P

D = 8192
TILE = 128


def shifted(value, axis, by):
    count = lax.axis_size(axis)
    pairs = [(i, i + by) for i in range(count) if 0 <= i + by < count]
    return lax.ppermute(value, axis, pairs)


def from_partner(block, axis, distance):
    count = lax.axis_size(axis)
    route = []
    for low in range(count):
        high = low | 1 << distance
        if high != low and high < count:
            route += [(low, high), (high, low)]
    return lax.ppermute(block, axis, route)


def normalize(state, gain):
    state32 = state.astype(jnp.float32)
    squares = lax.psum(jnp.sum(state32 * state32, axis=1), "dp")
    scale = lax.rsqrt(squares / D + 1e-05)
    normed = state32 * scale[:, None]
    local = (normed * gain.astype(jnp.float32)).astype(jnp.bfloat16)
    whole = lax.all_gather(local, "dp", axis=1, tiled=True)
    return (normed, scale, whole)


def on_device(batches, cotangents, weights, gains, exponents):
    sections = lax.axis_size("pipe")
    index = lax.axis_index("pipe")
    bit_count = sections.bit_length() - 1
    bit_list = list(range(bit_count))
    weight_pair = weights[:, 0]
    gain_pair = gains[:, 0]
    state = jnp.where(index == 0, batches[0], batches[1])
    inputs = []
    last = jnp.zeros_like(state)
    final_tick = jnp.maximum(index, sections - 1 - index)
    for tick in range(sections):
        pick = jnp.where(index == tick, 0, 1)
        weight = weight_pair[pick]
        gain = gain_pair[pick]
        normed, scale, whole = normalize(state, gain)
        produced = jnp.dot(whole, weight, preferred_element_type=jnp.float32)
        result = (state.astype(jnp.float32) + produced).astype(jnp.bfloat16)
        inputs.append(state)
        last = jnp.where(final_tick == tick, result, last)
        if tick + 1 < sections:
            from_lower = shifted(result, "pipe", 1)
            from_upper = shifted(result, "pipe", -1)
            state = jnp.where(index == tick + 1, from_lower, from_upper)
    grad_out = jnp.where(index == sections - 1, cotangents[0], cotangents[1])
    own_grad = jnp.zeros(weights.shape[2:], jnp.float32)
    mirror_grad = jnp.zeros(weights.shape[2:], jnp.float32)
    for tick in reversed(range(sections)):
        pick = jnp.where(index == tick, 0, 1)
        weight = weight_pair[pick]
        gain = gain_pair[pick].astype(jnp.float32)
        normed, scale, whole = normalize(inputs[tick], gain_pair[pick])
        grad_w = jnp.einsum("md,mk->dk", whole, grad_out, preferred_element_type=jnp.float32)
        grad_feat = (
            lax.psum_scatter(
                jnp.einsum(
                    "dk,mk->dm", weight, grad_out, preferred_element_type=jnp.float32
                ).astype(jnp.bfloat16),
                "dp",
                scatter_dimension=0,
                tiled=True,
            )
            .astype(jnp.float32)
            .T
        )
        grad_norm = grad_feat * gain
        mix = lax.psum(jnp.sum(grad_norm * normed, axis=1), "dp") / D
        grad_in = (
            grad_out.astype(jnp.float32) + scale[:, None] * (grad_norm - normed * mix[:, None])
        ).astype(jnp.bfloat16)
        own_grad = jnp.where(index == tick, grad_w, own_grad)
        mirror_grad = jnp.where(index == sections - 1 - tick, grad_w, mirror_grad)
        if tick > 0:
            from_upper = shifted(grad_in, "pipe", -1)
            from_lower = shifted(grad_in, "pipe", 1)
            grad_out = jnp.where(index == tick - 1, from_upper, from_lower)
    returned = mirror_grad.astype(jnp.bfloat16)
    for bit in bit_list:
        returned = from_partner(returned, "pipe", bit)
    expanded = jnp.repeat(jnp.repeat(exponents[0], TILE, axis=0), TILE, axis=1)
    factor = jnp.exp2(-expanded.astype(jnp.float32))
    total = ((own_grad + returned.astype(jnp.float32)) * factor).astype(jnp.bfloat16)
    return (total[None], last[None])


def solution(mesh):
    return jax.shard_map(
        on_device,
        mesh=mesh,
        in_specs=(
            P(None, None, "dp"),
            P(None, None, "dp"),
            P(None, "pipe", None, "dp"),
            P(None, "pipe", "dp"),
            P("pipe", None, "dp"),
        ),
        out_specs=(P("pipe", None, "dp"), P("pipe", None, "dp")),
        check_vma=False,
    )
```

profile of v0, /device:TPU:0, one launch (start us, length us, event | category | flops | bytes accessed | tf_op | source)
XLA Modules:
  0.0 1596.7 jit_solution(14207274203376488401)
XLA Ops:
  8.2 83.5 %psum.46 = f32[128]{0:T(128)S(1)} all-reduce(f32[128]{0:T(128)S(1)} %get-tuple-element.8), channel_id=1, replica_groups=mesh['pipe'=4,'dp'=32] {'dp'}, use_global_device_ids=true, to_apply=%region_1.2 | all-reduce | flops 128 | bytes 1024 | tf_op jit(solution)/shard_map/psum | solution.py:28
  93.3 121.1 %all-gather.5.cloned.1.call-done = bf16[128,8192]{1,0:T(8,128)(2,1)} async-done(((bf16[128,256]{1,0:T(8,128)(2,1)}), bf16[128,8192]{1,0:T(8,128)(2,1)}) %all-gather.5.cloned.1.call-update) | async-done | bytes 2097168 | tf_op jit(solution)/shard_map/all_gather | solution.py:32
  214.4 3.5 fusion.41
  218.0 1.4 collective-permute-start.1
  219.4 3.0 collective-permute-start
  223.5 81.7 %psum.49 = f32[128]{0:T(128)S(1)} all-reduce(f32[128]{0:T(128)S(1)} %get-tuple-element.6), channel_id=1, replica_groups=mesh['pipe'=4,'dp'=32] {'dp'}, use_global_device_ids=true, to_apply=%region_3.4 | all-reduce | flops 128 | bytes 1024 | tf_op jit(solution)/shard_map/psum | solution.py:28
  306.0 124.6 %all-gather.7.cloned.1.call-done = bf16[128,8192]{1,0:T(8,128)(2,1)} async-done(((bf16[128,256]{1,0:T(8,128)(2,1)}), bf16[128,8192]{1,0:T(8,128)(2,1)}) %all-gather.7.cloned.1.call-update) | async-done | bytes 2097168 | tf_op jit(solution)/shard_map/all_gather | solution.py:32
  430.6 3.5 fusion.38
  434.1 1.3 collective-permute-start.3
  435.4 3.0 collective-permute-start.2
  439.5 81.7 %psum.50 = f32[128]{0:T(128)S(1)} all-reduce(f32[128]{0:T(128)S(1)} %get-tuple-element.4), channel_id=1, replica_groups=mesh['pipe'=4,'dp'=32] {'dp'}, use_global_device_ids=true, to_apply=%region_5.6 | all-reduce | flops 128 | bytes 1024 | tf_op jit(solution)/shard_map/psum | solution.py:28
  522.0 5.0 convolution_convert_fusion.2
  527.1 119.5 %all-gather.9.cloned.1.call-done = bf16[128,8192]{1,0:T(8,128)(2,1)} async-done(((bf16[128,256]{1,0:T(8,128)(2,1)}), bf16[128,8192]{1,0:T(8,128)(2,1)}) %all-gather.9.cloned.1.call-update) | async-done | bytes 2097168 | tf_op jit(solution)/shard_map/all_gather | solution.py:32
  646.6 3.5 fusion.35
  650.1 1.3 collective-permute-start.5
  651.4 3.0 collective-permute-start.4
  655.5 81.7 %psum.51 = f32[128]{0:T(128)S(1)} all-reduce(f32[128]{0:T(128)S(1)} %get-tuple-element.2), channel_id=1, replica_groups=mesh['pipe'=4,'dp'=32] {'dp'}, use_global_device_ids=true, to_apply=%region_7.8 | all-reduce | flops 128 | bytes 1024 | tf_op jit(solution)/shard_map/psum | solution.py:28
  737.2 76.1 %reduce-scatter.4.cloned.1.call-done = bf16[256,128]{0,1:T(8,128)(2,1)} async-done(((bf16[8192,128]{0,1:T(8,128)(2,1)}), bf16[256,128]{0,1:T(8,128)(2,1)}) %reduce-scatter.4.cloned.1.call-update) | async-done | bytes 65552 | tf_op jit(solution)/shard_map/reduce_scatter | solution.py:70
  813.3 1.6 fusion.64
  814.8 77.4 %psum.54 = f32[128]{0:T(128)S(1)} all-reduce(f32[128]{0:T(128)S(1)} %get-tuple-element.11), channel_id=1, replica_groups=mesh['pipe'=4,'dp'=32] {'dp'}, use_global_device_ids=true, to_apply=%region_10.11 | all-reduce | flops 128 | bytes 1024 | tf_op jit(solution)/shard_map/psum | solution.py:82
  893.2 1.3 collective-permute-start.7
  894.5 1.3 collective-permute-start.6
  895.8 5.4 collective-permute-done.6
  901.2 5.0 convolution_convert_fusion.1
  906.9 161.3 %reduce-scatter.6.cloned.1.call-done = bf16[256,128]{0,1:T(8,128)(2,1)} async-done(((bf16[8192,128]{0,1:T(8,128)(2,1)}), bf16[256,128]{0,1:T(8,128)(2,1)}) %reduce-scatter.6.cloned.1.call-update) | async-done | bytes 65552 | tf_op jit(solution)/shard_map/reduce_scatter | solution.py:70
  1068.1 1.0 fusion.66
  1069.1 77.4 %psum.66 = f32[128]{0:T(128)S(1)} all-reduce(f32[128]{0:T(128)S(1)} %fusion.66), channel_id=1, replica_groups=mesh['pipe'=4,'dp'=32] {'dp'}, use_global_device_ids=true, to_apply=%region_13.14 | all-reduce | flops 128 | bytes 1024 | tf_op jit(solution)/shard_map/psum | solution.py:82
  1147.5 1.3 collective-permute-start.9
  1148.8 1.3 collective-permute-start.8
  1150.1 5.3 collective-permute-done.8
  1155.5 5.1 convolution_convert_fusion
  1160.7 4.5 fusion.101
  1165.2 25.6 %all-gather.11.cloned.1.call-done = bf16[128,8192]{1,0:T(8,128)(2,1)} async-done(((bf16[128,256]{1,0:T(8,128)(2,1)}), bf16[128,8192]{1,0:T(8,128)(2,1)}) %all-gather.11.cloned.1.call-update) | async-done | bytes 2097168 | tf_op jit(solution)/shard_map/all_gather | solution.py:32
  1190.7 6.1 fusion.83
  1196.8 161.1 %reduce-scatter.8.cloned.1.call-done = bf16[256,128]{0,1:T(8,128)(2,1)} async-done(((bf16[8192,128]{0,1:T(8,128)(2,1)}), bf16[256,128]{0,1:T(8,128)(2,1)}) %reduce-scatter.8.cloned.1.call-update) | async-done | bytes 65552 | tf_op jit(solution)/shard_map/reduce_scatter | solution.py:70
  1357.9 1.0 fusion.72
  1358.9 77.6 %psum.67 = f32[128]{0:T(128)S(1)} all-reduce(f32[128]{0:T(128)S(1)} %fusion.72), channel_id=1, replica_groups=mesh['pipe'=4,'dp'=32] {'dp'}, use_global_device_ids=true, to_apply=%region_16.17 | all-reduce | flops 128 | bytes 1024 | tf_op jit(solution)/shard_map/psum | solution.py:82
  1437.5 1.6 collective-permute-start.11
  1439.1 1.7 collective-permute-start.10
  1440.8 4.5 fusion.100
  1445.4 5.8 select_convert_fusion
  1451.1 6.7 collective-permute-start.12
  1457.8 7.1 collective-permute-done.12
  1464.9 3.0 collective-permute-start.13
  1468.1 3.5 fusion.47
  1471.7 88.0 %collective-permute-done.13 = bf16[8192,256]{1,0:T(8,128)(2,1)} collective-permute-done((bf16[8192,256]{1,0:T(8,128)(2,1)}, bf16[8192,256]{1,0:T(8,128)(2,1)}, u32[]{:S(2)}, u32[]{:S(2)}) %collective-permute-start.13) | collective-permute-done | bytes 4194336 | tf_op jit(solution)/shard_map/ppermute | solution.py:23
  1559.9 19.7 %broadcast_in_dim.11 = f32[8192,2,128]{2,1,0:T(2,128)} broadcast(f32[8192,2]{1,0:T(8,128)S(1)} %bitcast.89), dimensions={0,1} | broadcast | bytes 8454144 | tf_op jit(solution)/shard_map/broadcast_in_dim | solution.py:95
  1579.5 10.3 fusion.1
  (61 shorter events, 11.1 us)
Async XLA Ops:
  7.2 207.3 %all-gather.5.cloned.1.call-start = ((), (), s32[]{:S(2)}) async-start(), calls=%async_computation.3 | async-start | bytes 2162688 | tf_op jit(solution)/shard_map/all_gather | solution.py:32
  93.3 337.3 %all-gather.7.cloned.1.call-start = ((), (), s32[]{:S(2)}) async-start(), calls=%async_computation.4 | async-start | bytes 2162688 | tf_op jit(solution)/shard_map/all_gather | solution.py:32
  218.0 304.0 %copy-start.5 = (bf16[2,128,256]{2,1,0:T(8,128)(2,1)S(1)}, bf16[2,128,256]{2,1,0:T(8,128)(2,1)}, u32[]{:S(2)}) copy-start(bf16[2,128,256]{2,1,0:T(8,128)(2,1)} %param.6) | copy-start | bytes 393220
  218.0 4.5 collective-permute-start.1
  219.4 3.9 collective-permute-start
  305.9 340.7 %all-gather.9.cloned.1.call-start = ((), (), s32[]{:S(2)}) async-start(), calls=%async_computation.5 | async-start | bytes 2162688 | tf_op jit(solution)/shard_map/all_gather | solution.py:32
  434.1 4.3 collective-permute-start.3
  435.4 3.9 collective-permute-start.2
  521.9 291.3 %reduce-scatter.4.cloned.1.call-start = ((), (), s32[]{:S(2)}) async-start(), calls=%async_computation.6 | async-start | bytes 2162688 | tf_op jit(solution)/shard_map/reduce_scatter | solution.py:70
  527.0 541.1 %reduce-scatter.6.cloned.1.call-start = ((), (), s32[]{:S(2)}) async-start(), calls=%async_computation.7 | async-start | bytes 2162688 | tf_op jit(solution)/shard_map/reduce_scatter | solution.py:70
  650.1 4.3 collective-permute-start.5
  651.4 3.9 collective-permute-start.4
  893.2 2.6 collective-permute-start.7
  894.5 6.7 collective-permute-start.6
  906.2 284.5 %all-gather.11.cloned.1.call-start = ((), (), s32[]{:S(2)}) async-start(), calls=%async_computation.9 | async-start | bytes 2162688 | tf_op jit(solution)/shard_map/all_gather | solution.py:32
  906.8 451.1 %reduce-scatter.8.cloned.1.call-start = ((), (), s32[]{:S(2)}) async-start(), calls=%async_computation.8 | async-start | bytes 2162688 | tf_op jit(solution)/shard_map/reduce_scatter | solution.py:70
  1147.5 2.6 collective-permute-start.9
  1148.8 6.7 collective-permute-start.8
  1155.5 5.2 copy-start.3
  1165.2 275.7 %copy-start.2 = (bf16[128,8192]{1,0:T(8,128)(2,1)S(1)}, bf16[128,8192]{1,0:T(8,128)(2,1)}, u32[]{:S(2)}) copy-start(bf16[128,8192]{1,0:T(8,128)(2,1)} %all-gather.7.cloned.1.call-done) | copy-start | bytes 6291460
  1437.5 7.9 copy-start
  1437.5 7.9 copy-start.4
  1437.5 7.8 collective-permute-start.11
  1439.1 6.3 collective-permute-start.10
  1445.3 22.7 %copy-start.6 = (s32[1,64,2]{1,2,0:T(2,128)S(1)}, s32[1,64,2]{1,2,0:T(2,128)}, u32[]{:S(2)}) copy-start(s32[1,64,2]{1,2,0:T(2,128)} %param.9) | copy-start | bytes 1540
  1445.3 22.8 %copy-start.1 = (bf16[128,8192]{1,0:T(8,128)(2,1)S(1)}, bf16[128,8192]{1,0:T(8,128)(2,1)}, u32[]{:S(2)}) copy-start(bf16[128,8192]{1,0:T(8,128)(2,1)} %all-gather.11.cloned.1.call-done) | copy-start | bytes 6291460
  1451.1 13.8 collective-permute-start.12
  1464.9 94.7 %collective-permute-start.13 = (bf16[8192,256]{1,0:T(8,128)(2,1)}, bf16[8192,256]{1,0:T(8,128)(2,1)}, u32[]{:S(2)}, u32[]{:S(2)}) collective-permute-start(bf16[8192,256]{1,0:T(8,128)(2,1)} %collective-permute-done.12), channel_id=1, source_target_pairs={{0,64},{64,0},{32,96},{96,32},{1,65},{65,1},{33,97},{97,33},{2,66}... | collective-permute-start | bytes 12582920 | tf_op jit(solution)/shard_map/ppermute | solution.py:23
Sparse Core Ops, SparseCore 0:
  93.4 121.0 all-gather.4
  306.1 124.4 all-gather.6
  522.0 124.4 all-gather.8
  649.4 163.8 reduce-scatter.3
  906.4 161.7 reduce-scatter.5
  1070.1 120.5 all-gather.10
  1193.7 164.2 reduce-scatter.7
where the time goes:
time: 1600 us
  waiting for transfers between devices  898 us (56%)
  blocking collectives  561 us (35%)
  matrix products  50.2 us (3%)
  starting transfers between devices  31.6 us (2%)
  other arithmetic  21.1 us (1%)
  local copies, waits for them, and re-layouts  20.1 us (1%)
    reduce_scatter x3, waiting for transfers between devices, on_device(): lax.psum_scatter(jnp.einsum('dk,mk->dm', weight, grad_out, preferred_elem...  398 us
    all_gather x4, waiting for transfers between devices, normalize(): whole = lax.all_gather(local, 'dp', axis=1, tiled=True)  391 us
    psum x4, blocking collectives, normalize(): squares = lax.psum(jnp.sum(state32 * state32, axis=1), 'dp')  329 us
    psum x3, blocking collectives, on_device(): mix = lax.psum(jnp.sum(grad_norm * normed, axis=1), 'dp') / D  232 us
    ppermute x2, waiting for transfers between devices, from_partner(): return lax.ppermute(block, axis, route)  95.1 us
  transfers between devices with their start and end apart: 21, of which 14 were waited for; matrix products, arithmetic and copies ran while one was open for 2% of the time, Pallas kernels for 0%

commit v1 on v0

v1 whole, which is shorter than its diff:
```python
import functools

import jax
import jax.numpy as jnp
from jax import lax
from jax.experimental import pallas as pl
from jax.experimental.pallas import tpu as pltpu
from jax.sharding import PartitionSpec as P

D = 8192
EPS = 1e-05
M = 128
H = 128
N = 32
R = M + 16
F32 = jnp.float32
BF16 = jnp.bfloat16
BOTH = ("pipe", "dp")
VM = pl.BlockSpec(memory_space=pltpu.VMEM)
HBM = pl.BlockSpec(memory_space=pl.ANY)
PARAMS = pltpu.CompilerParams(vmem_limit_bytes=56 * 1024 * 1024)


def pairs(fn):
    out = []
    for i in range(128):
        p, d = divmod(i, 32)
        zh, c = divmod(p, 2)
        zl, r = divmod(d, 16)
        y, x = divmod(r, 4)
        zh2, c2, zl2, y2, x2 = fn(zh, c, zl, y, x)
        out.append((i, (zh2 * 2 + c2) * 32 + zl2 * 16 + (y2 % 4) * 4 + x2 % 4))
    return out


def move(value, fn):
    return lax.ppermute(value, BOTH, pairs(fn))


def other_core(zh, c, zl, y, x):
    return (zh, 1 - c, zl, y, x)


def other_zh(zh, c, zl, y, x):
    return (1 - zh, c, zl, y, x)


def other_zl(zh, c, zl, y, x):
    return (zh, c, 1 - zl, y, x)


def first_axis(k):
    return lambda zh, c, zl, y, x: (zh, c, zl, y + (k if c else 0), x + (0 if c else k))


def second_axis(k):
    return lambda zh, c, zl, y, x: (zh, c, zl, y + (0 if c else k), x + (k if c else 0))


SHIFTS = (0, 1, 3, 2)


def place():
    p = lax.axis_index("pipe")
    return p // 2, p % 2


def to_rows(value):
    return jnp.sum(jnp.transpose(value), axis=0, keepdims=True)


def to_cols(row):
    return jnp.transpose(jnp.broadcast_to(row, (M, H)))


def extra_rows(row):
    high = row.astype(BF16)
    low = (row - high.astype(F32)).astype(BF16)
    i = lax.broadcasted_iota(jnp.int32, (16, M), 0)
    value = jnp.where(i == 0, high.astype(F32), jnp.where(i == 1, low.astype(F32), 0.0))
    return value.astype(BF16)


def read_extra(block):
    return jnp.sum(block.astype(F32), axis=0, keepdims=True)


def weight_copies(tick, w_ref, r_ref, buf, sem, start):
    zh, c = place()
    copy_index = zh if tick < 2 else 1 - zh
    e = zh ^ c
    own = (e == 0) if tick in (0, 3) else (e == 1)
    for ch in range(4):
        part = pl.ds(8 * ch, 8)
        received = pltpu.make_async_copy(r_ref.at[copy_index, part], buf.at[part], sem.at[ch])
        if start:

            @pl.when(own)
            def _():
                pltpu.make_async_copy(w_ref.at[copy_index, part, c], buf.at[part], sem.at[ch]).start()

            @pl.when(jnp.logical_not(own))
            def _():
                received.start()


def weight_wait(ch, w_ref, r_ref, buf, sem):
    part = pl.ds(8 * ch, 8)
    pltpu.make_async_copy(r_ref.at[0, part], buf.at[part], sem.at[ch]).wait()


def payload_kernel(x_ref, gain_ref, out_ref, f_ref):
    x = x_ref[...].astype(F32)
    f = (x * gain_ref[...].astype(F32)).astype(BF16)
    f_ref[...] = f
    extra = extra_rows(to_rows(x * x))
    for j in range(N):
        out_ref[j, 0:M, :] = f
        out_ref[j, M:R, :] = extra


def forward_kernel(tick, rows, g_ref, w_ref, r_ref, keep_ref, send_ref, buf, sem):
    weight_copies(tick, w_ref, r_ref, buf, sem, True)
    _, c = place()
    if rows == R:
        sums = jnp.sum(g_ref[:, M:R, :].astype(F32), axis=0)
        sums = jnp.sum(sums, axis=0, keepdims=True)
    else:
        sums = jnp.zeros((1, M), F32)
    sums = jnp.broadcast_to(sums, (8, M))
    total = jnp.zeros((M, 2 * H), F32)
    for ch in range(4):
        f = jnp.concatenate([g_ref[8 * ch + j, 0:M, :] for j in range(8)], axis=1)
        weight_wait(ch, w_ref, r_ref, buf, sem)
        w = buf[8 * ch : 8 * ch + 8].reshape(8 * 128, 2 * H)
        total = total + jnp.dot(f, w, preferred_element_type=F32)
    first = c == 0
    keep_ref[0:M, :] = jnp.where(first, total[:, :H], total[:, H:])
    send_ref[0:M, :] = jnp.where(first, total[:, H:], total[:, :H])
    keep_ref[M : M + 8, :] = sums
    send_ref[M : M + 8, :] = sums


def combine_kernel(keep_ref, recv_ref, x_ref, gain_ref, next_ref, p_ref, s_ref, out_ref=None, f_ref=None):
    squares = keep_ref[M : M + 8, :] + recv_ref[M : M + 8, :]
    scale = lax.rsqrt(squares / D + EPS)
    s_ref[...] = scale
    p = keep_ref[0:M, :] + recv_ref[0:M, :]
    p_ref[...] = p
    new = (x_ref[...].astype(F32) + to_cols(scale[0:1]) * p).astype(BF16)
    next_ref[...] = new
    if out_ref is not None:
        x = new.astype(F32)
        f = (x * gain_ref[...].astype(F32)).astype(BF16)
        f_ref[...] = f
        extra = extra_rows(to_rows(x * x))
        for j in range(N):
            out_ref[j, 0:M, :] = f
            out_ref[j, M:R, :] = extra


def last_combine_kernel(keep_ref, recv_ref, x_ref, s_ref, next_ref):
    p = keep_ref[0:M, :] + recv_ref[0:M, :]
    next_ref[...] = (x_ref[...].astype(F32) + to_cols(s_ref[0:1, :]) * p).astype(BF16)


def backward_kernel(tick, mine_ref, theirs_ref, s_ref, w_ref, r_ref, out_ref, gs_ref, buf, sem):
    weight_copies(tick, w_ref, r_ref, buf, sem, True)
    _, c = place()
    first = c == 0
    a = mine_ref[0:M, :]
    b = theirs_ref[0:M, :]
    left = jnp.where(first, a, b).astype(F32)
    right = jnp.where(first, b, a).astype(F32)
    scale = to_cols(s_ref[0:1, :])
    gs_ref[:, :H] = (left * scale).astype(BF16)
    gs_ref[:, H:] = (right * scale).astype(BF16)
    extra = extra_rows(read_extra(mine_ref[M:R, :]) + read_extra(theirs_ref[M:R, :]))
    gt = jnp.concatenate([jnp.transpose(left), jnp.transpose(right)], axis=0).astype(BF16)
    for ch in range(4):
        weight_wait(ch, w_ref, r_ref, buf, sem)
        w = buf[8 * ch : 8 * ch + 8].reshape(8 * 128, 2 * H)
        part = jnp.dot(w, gt, preferred_element_type=F32).astype(BF16).reshape(8, 128, M)
        out_ref[8 * ch : 8 * ch + 8, 0:M, :] = part
    for j in range(N):
        out_ref[j, M:R, :] = extra


def first_backward_kernel(g_ref, w_ref, r_ref, out_ref, buf, sem):
    weight_copies(3, w_ref, r_ref, buf, sem, True)
    g = g_ref[...].astype(F32)
    gt = jnp.concatenate([jnp.transpose(g[:, :H]), jnp.transpose(g[:, H:])], axis=0).astype(BF16)
    for ch in range(4):
        weight_wait(ch, w_ref, r_ref, buf, sem)
        w = buf[8 * ch : 8 * ch + 8].reshape(8 * 128, 2 * H)
        out_ref[8 * ch : 8 * ch + 8] = jnp.dot(w, gt, preferred_element_type=F32).astype(BF16).reshape(8, 128, M)


def sum_kernel(got_ref, gain_ref, gn_ref):
    total = jnp.sum(got_ref[...].astype(F32), axis=0)
    gn_ref[...] = jnp.transpose(total) * gain_ref[...].astype(F32)


def scalars_kernel(x_ref, gn_ref, out_ref):
    x = x_ref[...].astype(F32)
    i = lax.broadcasted_iota(jnp.int32, (8, M), 0)
    out_ref[...] = jnp.where(i == 0, to_rows(x * x), jnp.where(i == 1, to_rows(x * gn_ref[...]), 0.0))


def spread_kernel(a_ref, b_ref, out_ref):
    total = a_ref[...] + b_ref[...]
    for j in range(N):
        out_ref[j] = total


def last_grad_kernel(sums_ref, g_ref, gn_ref, x_ref, p_ref, out_ref, s_ref):
    total = jnp.sum(sums_ref[...], axis=0)
    scale = lax.rsqrt(total[0:1, :] / D + EPS)
    s_ref[...] = jnp.broadcast_to(scale, (8, M))
    mix = scale * scale * scale * total[1:2, :] / D
    g = g_ref[...].astype(F32) + to_cols(scale) * gn_ref[...] - to_cols(mix) * x_ref[...].astype(F32)
    g = g.astype(BF16)
    out_ref[0:M, :] = g
    out_ref[M:R, :] = extra_rows(to_rows(g.astype(F32) * p_ref[...]))


def grad_kernel(got_ref, gain_ref, g_ref, s_ref, x_ref, out_ref):
    total = jnp.sum(got_ref[:, 0:M, :].astype(F32), axis=0)
    dots = jnp.sum(jnp.sum(got_ref[:, M:R, :].astype(F32), axis=0), axis=0, keepdims=True)
    gn = jnp.transpose(total) * gain_ref[...].astype(F32)
    scale = s_ref[0:1, :]
    mix = scale * scale * scale * dots / D
    g = g_ref[0:M, :].astype(F32) + to_cols(scale) * gn - to_cols(mix) * x_ref[...].astype(F32)
    out_ref[...] = g.astype(BF16)


def dots_kernel(g_ref, p_ref, out_ref):
    g = g_ref[...]
    out_ref[0:M, :] = g
    out_ref[M:R, :] = extra_rows(to_rows(g.astype(F32) * p_ref[...]))


def order_kernel(v0, v1, v2, v3, f0, f1, f2, f3_ref, keep_ref, send_ref):
    zh, c = place()
    dp = lax.axis_index("dp")
    zl, y, x = dp // 16, (dp // 4) % 4, dp % 4
    a0 = jnp.where(c == 0, x, y)
    b0 = jnp.where(c == 0, y, x)
    sa = jnp.where(c == 0, 1, 4)
    sb = jnp.where(c == 0, 4, 1)
    second = c == 1

    def turn(v):
        return jnp.transpose(v.astype(F32)).astype(BF16)

    def put(j, q, down, up):
        pair = jnp.concatenate([turn(down), turn(up)], axis=1)

        @pl.when(c == q)
        def _():
            keep_ref[j] = pair

        @pl.when(c != q)
        def _():
            send_ref[j] = pair

    for ib, kb in enumerate(SHIFTS):
        ref = (v0, v1, v2, v3)[ib]
        jb = lax.rem(b0 + 4 - kb, 4) * sb
        for ia, ka in enumerate(SHIFTS):
            ja = lax.rem(a0 + 4 - ka, 4) * sa
            for iz in range(2):
                j = jb + ja + (zl if iz == 0 else 1 - zl) * 16
                at = ia * 2 + iz
                last = ref[at, 0]
                f3_ref[j] = last
                d0 = jnp.where(zh == 0, f0[j, 0:M, :], f2[j, 0:M, :])
                d1 = jnp.where(zh == 0, f1[j, 0:M, :], last)
                put(j, 0, d0, ref[at, 1])
                put(j, 1, d1, ref[at, 2])


def weight_grad_kernel(keep_ref, recv_ref, local_ref, far_ref, factor_ref, out_ref):
    _, c = place()
    g = jnp.concatenate([local_ref[...], far_ref[...]], axis=0)
    count = keep_ref.shape[0]
    a = jnp.dot(keep_ref[...].reshape(count * H, 2 * M), g, preferred_element_type=F32).reshape(count, H, 2 * H)
    b = jnp.dot(recv_ref[...].reshape(count * H, 2 * M), g, preferred_element_type=F32).reshape(count, H, 2 * H)
    first = c == 0
    out_ref[:, 0] = (jnp.where(first, a, b) * factor_ref[:, 0]).astype(BF16)
    out_ref[:, 1] = (jnp.where(first, b, a) * factor_ref[:, 1]).astype(BF16)


def call(kernel, out, specs, args, scratch=(), flops=0, bytes_accessed=0):
    return pl.pallas_call(
        kernel,
        out_shape=[jax.ShapeDtypeStruct(s, d) for s, d in out],
        in_specs=specs,
        out_specs=[VM] * len(out),
        scratch_shapes=list(scratch),
        compiler_params=PARAMS,
        cost_estimate=pl.CostEstimate(flops=flops, bytes_accessed=bytes_accessed, transcendentals=0),
    )(*args)


WEIGHT_SCRATCH = (pltpu.VMEM((N, H, 2 * H), BF16), pltpu.SemaphoreType.DMA((4,)))
MATMUL = dict(scratch=WEIGHT_SCRATCH, flops=2 * M * N * H * 2 * H, bytes_accessed=4 << 20)


def blocks_of(payload):
    return lax.all_to_all(payload, "dp", 0, 0)


def gather_relative(value):
    both = jnp.stack([value, move(value, other_zl)])
    row = jnp.concatenate([both] + [move(both, first_axis(k)) for k in SHIFTS[1:]])
    return [row] + [move(row, second_axis(k)) for k in SHIFTS[1:]]


def on_device(batches, cotangents, weights, gains, exponents):
    zh, c = place()
    e = zh ^ c
    w5 = weights.reshape(2, N, 2, H, 2 * H)

    def half(value, which):
        return lax.dynamic_slice_in_dim(value, which * H, H, axis=value.ndim - 1)

    own_gain = half(gains[:, 0], c)
    got_gain = move(half(gains[:, 0], 1 - c), other_core)
    gain = []
    for tick in range(4):
        copy_index = zh if tick < 2 else 1 - zh
        own = (e == 0) if tick in (0, 3) else (e == 1)
        both = jnp.where(own, own_gain, got_gain)
        gain.append(lax.dynamic_slice_in_dim(both, copy_index, 1, axis=0))

    send_w = lax.dynamic_index_in_dim(w5, 1 - c, axis=2, keepdims=False)
    r_w = move(send_w, other_core)

    x0 = half(lax.dynamic_index_in_dim(batches, zh, axis=0, keepdims=False), c)
    block = (M, H)
    wide = ((N, R, H), BF16)
    out0, f0 = call(payload_kernel, [wide, (block, BF16)], [VM] * 2, (x0, gain[0]))
    g0 = blocks_of(out0)

    def forward(tick, gathered):
        keep, send = call(
            functools.partial(forward_kernel, tick, gathered.shape[1]),
            [((M + 8, H), F32)] * 2,
            [VM, HBM, HBM],
            (gathered, w5, r_w),
            **MATMUL,
        )
        return keep, move(send, other_core)

    outs = [(block, BF16), (block, F32), ((8, M), F32)]
    keep, recv = forward(0, g0)
    x1, _, s0, out1, f1 = call(
        combine_kernel, outs + [wide, (block, BF16)], [VM] * 4, (keep, recv, x0, gain[1])
    )
    g1 = blocks_of(out1)
    keep, recv = forward(1, g1)
    x2, p1, s1 = call(combine_kernel, outs, [VM] * 4, (keep, recv, x1, gain[1]))
    x2 = move(x2, other_zh)
    out2, f2 = call(payload_kernel, [wide, (block, BF16)], [VM] * 2, (x2, gain[2]))
    g2 = blocks_of(out2)

    cot = lax.dynamic_index_in_dim(cotangents, 1 - zh, axis=0, keepdims=False)
    (part,) = call(
        first_backward_kernel, [((N, H, M), BF16)], [VM, HBM, HBM], (cot, w5, r_w), **MATMUL
    )
    (gn3,) = call(sum_kernel, [(block, F32)], [VM] * 2, (blocks_of(part), gain[3]))

    keep, recv = forward(2, g2)
    x3, p2, s2, _, f3 = call(
        combine_kernel, outs + [wide, (block, BF16)], [VM] * 4, (keep, recv, x2, gain[3])
    )

    (mine,) = call(scalars_kernel, [((8, M), F32)], [VM] * 2, (x3, gn3))
    theirs = move(mine, other_core)
    (spread,) = call(spread_kernel, [((N, 8, M), F32)], [VM] * 2, (mine, theirs))
    sums = blocks_of(spread)

    early = jnp.stack([f0, f1])
    late = jnp.stack([f2, f3])
    mirror = move(jnp.where(zh == 1, early, late), other_zh)
    v = gather_relative(jnp.concatenate([f3[None], mirror]))

    g3 = half(cot, c)
    mine2, s3 = call(
        last_grad_kernel, [((R, H), BF16), ((8, M), F32)], [VM] * 5, (sums, g3, gn3, x3, p2)
    )

    def backward(tick, mine, s):
        theirs = move(mine, other_core)
        part, gs = call(
            functools.partial(backward_kernel, tick),
            [wide, ((M, 2 * H), BF16)],
            [VM] * 3 + [HBM] * 2,
            (mine, theirs, s, w5, r_w),
            **MATMUL,
        )
        return blocks_of(part), gs

    got2, gs2 = backward(2, mine2, s2)
    (g1_,) = call(grad_kernel, [(block, BF16)], [VM] * 5, (got2, gain[2], mine2, s2, x2))
    g1_ = move(g1_, other_zh)
    (mine1,) = call(dots_kernel, [((R, H), BF16)], [VM] * 2, (g1_, p1))
    got1, gs1 = backward(1, mine1, s1)
    (g0_,) = call(grad_kernel, [(block, BF16)], [VM] * 5, (got1, gain[1], mine1, s1, x1))

    f3_all, keep_t, send_t = call(
        order_kernel,
        [((N, M, H), BF16), ((N, H, 2 * M), BF16), ((N, H, 2 * M), BF16)],
        [VM] * 7,
        (*v, g0, g1, g2),
    )
    recv_t = move(send_t, other_core)
    keep, recv = forward(3, f3_all)
    (x4,) = call(last_combine_kernel, [(block, BF16)], [VM] * 4, (keep, recv, x3, s3))
    is_first = e == 0
    shown = jnp.where(is_first, x4, x3)
    got = move(jnp.where(is_first, x3, x4), other_core)
    last = jnp.where(c == 0, jnp.concatenate([shown, got], 1), jnp.concatenate([got, shown], 1))

    def scaled(g, s):
        return (g.astype(F32) * s[0][:, None]).astype(BF16)

    mine0 = scaled(g0_, s0)
    theirs0 = move(mine0, other_core)
    gs0 = jnp.where(c == 0, jnp.concatenate([mine0, theirs0], 1), jnp.concatenate([theirs0, mine0], 1))
    gs3 = scaled(cot, s3)
    low = jnp.where(c == 0, gs0, gs1)
    high = jnp.where(c == 0, gs2, gs3)
    local = jnp.where(zh == 0, low, high)
    far = move(jnp.where(zh == 0, high, low), other_zh)
    factor = jnp.repeat(jnp.exp2(-exponents[0].astype(F32)), H, axis=1).reshape(N, 2, 1, 2 * H)
    step = 8
    total = pl.pallas_call(
        weight_grad_kernel,
        out_shape=jax.ShapeDtypeStruct((N, 2, H, 2 * H), BF16),
        grid=(N // step,),
        in_specs=[
            pl.BlockSpec((step, H, 2 * M), lambda i: (i, 0, 0)),
            pl.BlockSpec((step, H, 2 * M), lambda i: (i, 0, 0)),
            pl.BlockSpec((M, 2 * H), lambda i: (0, 0)),
            pl.BlockSpec((M, 2 * H), lambda i: (0, 0)),
            pl.BlockSpec((step, 2, 1, 2 * H), lambda i: (i, 0, 0, 0)),
        ],
        out_specs=pl.BlockSpec((step, 2, H, 2 * H), lambda i: (i, 0, 0, 0)),
        compiler_params=PARAMS,
        cost_estimate=pl.CostEstimate(flops=2 * 256 * 256 * D, bytes_accessed=8 << 20, transcendentals=0),
    )(keep_t, recv_t, local, far, factor)
    return (total.reshape(1, D, 2 * H), last[None])


def solution(mesh):
    return jax.shard_map(
        on_device,
        mesh=mesh,
        in_specs=(
            P(None, None, "dp"),
            P(None, None, "dp"),
            P(None, "pipe", None, "dp"),
            P(None, "pipe", "dp"),
            P("pipe", None, "dp"),
        ),
        out_specs=(P("pipe", None, "dp"), P("pipe", None, "dp")),
        check_vma=False,
    )
```

time: 1600 us -> 287 us (0.18)
  waiting for transfers between devices: 898 us -> 87.6 us
  blocking collectives: 561 us -> 52.6 us
  Pallas kernels: 0 us -> 72.4 us
  matrix products: 50.2 us -> 0 us
  other arithmetic: 21.1 us -> 4.57 us
    psum x7 -> x0, blocking collectives: 561 us -> none  [the longest x4 329 us: normalize(): squares = lax.psum(jnp.sum(state32 * state32, axis=1), 'dp')]
    reduce_scatter x3 -> x0, waiting for transfers between devices: 398 us -> none  [on_device(): lax.psum_scatter(jnp.einsum('dk,mk->dm', weight, grad_out, preferred_elem...]
    all_gather x4 -> x0, waiting for transfers between devices: 391 us -> none  [normalize(): whole = lax.all_gather(local, 'dp', axis=1, tiled=True)]
    pallas_call x0 -> x22, Pallas kernels: none -> 72.4 us  [the longest x21 66.6 us: call(): pl.pallas_call(kernel, out_shape=[jax.ShapeDtypeStruct(s, d) for s, d in...]
    ppermute x14 -> x23, waiting for transfers between devices: 108 us -> 48.9 us  [move(): return lax.ppermute(value, BOTH, pairs(fn))]
    all_to_all x0 -> x2, blocking collectives: none -> 52.6 us  [blocks_of(): return lax.all_to_all(payload, 'dp', 0, 0)]
    dot_general x11 -> x0, matrix products: 50.2 us -> none  [the longest x4 20.9 us: on_device(): jnp.einsum('md,mk->dk', whole, grad_out, preferred_element_type=jnp.float32)]
    all_to_all x0 -> x5, waiting for transfers between devices: none -> 38.7 us  [blocks_of(): return lax.all_to_all(payload, 'dp', 0, 0)]
  transfers between devices with their start and end apart: 21 -> 28, of which waited for: 14 -> 16; matrix products, arithmetic and copies ran while one was open for 2% -> 3% of each run, Pallas kernels for 0% -> 18%
where the time goes in v1:
time: 287 us; the launch traced here: 285 us
  waiting for transfers between devices  87.6 us (31%)
  Pallas kernels  72.4 us (25%)
  blocking collectives  52.6 us (18%)
  starting transfers between devices  45.9 us (16%)
  local copies, waits for them, and re-layouts  21.1 us (7%)
  other arithmetic  4.57 us (2%)
    pallas_call x21, Pallas kernels, call(): pl.pallas_call(kernel, out_shape=[jax.ShapeDtypeStruct(s, d) for s, d in...  66.6 us
    all_to_all x2, blocking collectives, blocks_of(): return lax.all_to_all(payload, 'dp', 0, 0)  52.6 us
    ppermute x23, waiting for transfers between devices, move(): return lax.ppermute(value, BOTH, pairs(fn))  48.9 us
    all_to_all x5, waiting for transfers between devices, blocks_of(): return lax.all_to_all(payload, 'dp', 0, 0)  38.7 us
    all_to_all x5, starting transfers between devices, blocks_of(): return lax.all_to_all(payload, 'dp', 0, 0)  24.9 us
    ppermute x23, starting transfers between devices, move(): return lax.ppermute(value, BOTH, pairs(fn))  21 us
    unnamed x67, local copies, waits for them, and re-layouts  10.7 us
    pallas_call x1, Pallas kernels, on_device(): pl.pallas_call(weight_grad_kernel, out_shape=jax.ShapeDtypeStruct((N, 2,...  5.78 us
  transfers between devices with their start and end apart: 28, of which 16 were waited for; matrix products, arithmetic and copies ran while one was open for 3% of the time, Pallas kernels for 18%

profile of v1, /device:TPU:0, one launch (start us, length us, event | category | flops | bytes accessed | tf_op | source)
XLA Modules:
  0.0 285.2 jit_solution(9900612523095874844)
XLA Ops:
  0.7 4.7 %dynamic-slice_bitcast_fusion = bf16[2,32,128,256]{3,2,1,0:T(8,128)(2,1)} fusion(bf16[2,32,2,128,256]{4,3,2,1,0:T(8,128)(2,1)} %bitcast.39, s32[]{:T(128)S(6)} %select_n.126), kind=kLoop, calls=%fused_computation | loop fusion | bytes 8388612 | tf_op jit(solution)/shard_map/jit(dynamic_index_in_dim)/squeeze | solution.py:337
  6.6 4.7 %collective-permute-done = bf16[2,128]{1,0:T(2,128)(2,1)S(1)} collective-permute-done((bf16[2,128]{1,0:T(2,128)(2,1)S(1)}, bf16[2,128]{1,0:T(2,128)(2,1)S(1)}, u32[]{:S(2)}, u32[]{:S(2)}) %collective-permute-start) | collective-permute-done | bytes 544 | tf_op jit(solution)/shard_map/ppermute | solution.py:37
  11.9 1.9 shard_map.68
  13.8 28.3 %all_to_all.35.g_ref.f0 = bf16[32,144,128]{2,1,0:T(8,128)(2,1)} all-to-all(bf16[32,144,128]{2,1,0:T(8,128)(2,1)} %get-tuple-element.34), channel_id=1, replica_groups=mesh['pipe'=4,'dp'=32] {'dp'}, dimensions={0} | all-to-all | bytes 2359296 | tf_op jit(solution)/shard_map/all_to_all | solution.py:311
  42.2 4.1 %shard_map.69 = (f32[136,128]{1,0:T(8,128)}, f32[136,128]{1,0:T(8,128)}) custom-call(bf16[32,144,128]{2,1,0:T(8,128)(2,1)} %all_to_all.35.g_ref.f0, bf16[2,32,2,128,256]{4,3,2,1,0:T(8,128)(2,1)} %bitcast.40, bf16[2,32,128,256]{3,2,1,0:T(8,128)(2,1)} %collective-permute-done.1.r_ref), custom_call_target="tpu_custom_call" | custom-call | flops 268435456 | bytes 4194304 | tf_op jit(solution)/shard_map/pallas_call | solution.py:295
  48.4 2.1 shard_map.70
  50.6 24.2 %all_to_all.36.g_ref.f1 = bf16[32,144,128]{2,1,0:T(8,128)(2,1)} all-to-all(bf16[32,144,128]{2,1,0:T(8,128)(2,1)} %get-tuple-element.37), channel_id=1, replica_groups=mesh['pipe'=4,'dp'=32] {'dp'}, dimensions={0} | all-to-all | bytes 2359296 | tf_op jit(solution)/shard_map/all_to_all | solution.py:311
  74.8 4.1 %shard_map.71 = (f32[136,128]{1,0:T(8,128)}, f32[136,128]{1,0:T(8,128)}) custom-call(bf16[32,144,128]{2,1,0:T(8,128)(2,1)} %all_to_all.36.g_ref.f1, bf16[2,32,2,128,256]{4,3,2,1,0:T(8,128)(2,1)} %bitcast.41, bf16[2,32,128,256]{3,2,1,0:T(8,128)(2,1)} %collective-permute-done.1.r_ref), custom_call_target="tpu_custom_call" | custom-call | flops 268435456 | bytes 4194304 | tf_op jit(solution)/shard_map/pallas_call | solution.py:295
  79.0 1.5 collective-permute-done.3.recv_ref
  81.1 1.6 shard_map.72
  82.7 3.6 %collective-permute-start.4 = (bf16[128,128]{1,0:T(8,128)(2,1)}, bf16[128,128]{1,0:T(8,128)(2,1)S(1)}, u32[]{:S(2)}, u32[]{:S(2)}) collective-permute-start(bf16[128,128]{1,0:T(8,128)(2,1)} %get-tuple-element.41), channel_id=1, source_target_pairs={{0,64},{1,65},{2,66},{3,67},{4,68},{5,69},{6,70},{7,71},{8,72},{9,... | collective-permute-start | bytes 98312 | tf_op jit(solution)/shard_map/ppermute | solution.py:37
  86.3 2.1 collective-permute-done.4.x_ref
  89.0 1.9 shard_map.73
  90.9 4.1 %all-to-all-start.2 = ((bf16[32,144,128]{2,1,0:T(8,128)(2,1)}), bf16[32,144,128]{2,1,0:T(8,128)(2,1)S(1)}, u32[]{:S(2)}, u32[]{:S(2)}) async-start(bf16[32,144,128]{2,1,0:T(8,128)(2,1)} %get-tuple-element.42), calls=%async_computation.2 | async-start | bytes 2359296 | tf_op jit(solution)/shard_map/all_to_all | solution.py:311
  95.7 4.6 %shard_map.77 = bf16[32,128,128]{2,1,0:T(8,128)(2,1)} custom-call(bf16[128,256]{1,0:T(8,128)(2,1)} %dynamic-slice_bitcast_fusion.1.g_ref, bf16[2,32,2,128,256]{4,3,2,1,0:T(8,128)(2,1)} %bitcast.42, bf16[2,32,128,256]{3,2,1,0:T(8,128)(2,1)} %collective-permute-done.1.r_ref), custom_call_target="tpu_custom_call" | custom-call | flops 268435456 | bytes 4194304 | tf_op jit(solution)/shard_map/pallas_call | solution.py:295
  100.3 12.7 %all-to-all-done.2.g_ref.f2 = bf16[32,144,128]{2,1,0:T(8,128)(2,1)S(1)} async-done(((bf16[32,144,128]{2,1,0:T(8,128)(2,1)}), bf16[32,144,128]{2,1,0:T(8,128)(2,1)S(1)}, u32[]{:S(2)}, u32[]{:S(2)}) %all-to-all-start.2) | async-done | bytes 1179680 | tf_op jit(solution)/shard_map/all_to_all | solution.py:311
  113.0 4.3 %all-to-all-start.3 = ((bf16[32,128,128]{2,1,0:T(8,128)(2,1)}), bf16[32,128,128]{2,1,0:T(8,128)(2,1)S(1)}, u32[]{:S(2)}, u32[]{:S(2)}) async-start(bf16[32,128,128]{2,1,0:T(8,128)(2,1)} %shard_map.77), calls=%async_computation.3 | async-start | bytes 2097152 | tf_op jit(solution)/shard_map/all_to_all | solution.py:311
  117.3 4.1 %shard_map.74 = (f32[136,128]{1,0:T(8,128)}, f32[136,128]{1,0:T(8,128)}) custom-call(bf16[32,144,128]{2,1,0:T(8,128)(2,1)} %copy-done.1, bf16[2,32,2,128,256]{4,3,2,1,0:T(8,128)(2,1)} %bitcast.43, bf16[2,32,128,256]{3,2,1,0:T(8,128)(2,1)} %collective-permute-done.1.r_ref), custom_call_target="tpu_custom_call" | custom-call | flops 268435456 | bytes 4194304 | tf_op jit(solution)/shard_map/pallas_call | solution.py:295
  121.5 11.0 %all-to-all-done.3.got_ref = bf16[32,128,128]{2,1,0:T(8,128)(2,1)S(1)} async-done(((bf16[32,128,128]{2,1,0:T(8,128)(2,1)}), bf16[32,128,128]{2,1,0:T(8,128)(2,1)S(1)}, u32[]{:S(2)}, u32[]{:S(2)}) %all-to-all-start.3) | async-done | bytes 1048608 | tf_op jit(solution)/shard_map/all_to_all | solution.py:311
  133.5 2.1 shard_map.78.gn_ref
  136.2 2.1 shard_map.75
  139.2 3.3 %collective-permute-start.6 = (bf16[2,128,128]{2,1,0:T(8,128)(2,1)S(1)}, bf16[2,128,128]{2,1,0:T(8,128)(2,1)S(1)}, u32[]{:S(2)}, u32[]{:S(2)}) collective-permute-start(bf16[2,128,128]{2,1,0:T(8,128)(2,1)S(1)} %maximum_select_fusion), channel_id=1, source_target_pairs={{0,64},{1,65},{2,66},{3,67},{4,68},{5,69},{6,70},{7,71},{8,72},{9,... | collective-permute-start | bytes 196616 | tf_op jit(solution)/shard_map/ppermute | solution.py:37
  142.5 1.6 shard_map.79.a_ref
  147.4 4.3 %all-to-all-start.4 = ((f32[32,8,128]{2,1,0:T(8,128)}), f32[32,8,128]{2,1,0:T(8,128)S(1)}, u32[]{:S(2)}, u32[]{:S(2)}) async-start(f32[32,8,128]{2,1,0:T(8,128)} %shard_map.80), calls=%async_computation.4 | async-start | bytes 262144 | tf_op jit(solution)/shard_map/all_to_all | solution.py:311
  152.5 1.9 collective-permute-start.7
  155.1 5.0 %all-to-all-done.4.sums_ref = f32[32,8,128]{2,1,0:T(8,128)S(1)} async-done(((f32[32,8,128]{2,1,0:T(8,128)}), f32[32,8,128]{2,1,0:T(8,128)S(1)}, u32[]{:S(2)}, u32[]{:S(2)}) %all-to-all-start.4) | async-done | bytes 131104 | tf_op jit(solution)/shard_map/all_to_all | solution.py:311
  160.8 1.8 shard_map.81
  163.3 2.7 collective-permute-start.9
  166.9 4.6 %shard_map.82 = (bf16[32,144,128]{2,1,0:T(8,128)(2,1)}, bf16[128,256]{1,0:T(8,128)(2,1)}) custom-call(bf16[144,128]{1,0:T(8,128)(2,1)} %get-tuple-element.53.mine_ref.g_ref, bf16[144,128]{1,0:T(8,128)(2,1)} %copy-done.23, f32[8,128]{1,0:T(8,128)} %get-tuple-element.54.s_ref, bf16[2,32,2,128,256]{4,3,2,1,0:T(8,128)(2,1)} %bitcast.44, ...), custom_call_target="tpu_custom_call" | custom-call | flops 268435456 | bytes 4194304 | tf_op jit(solution)/shard_map/pallas_call | solution.py:295
  171.4 6.1 %all-to-all-start.5 = ((bf16[32,144,128]{2,1,0:T(8,128)(2,1)}), bf16[32,144,128]{2,1,0:T(8,128)(2,1)S(1)}, u32[]{:S(2)}, u32[]{:S(2)}) async-start(bf16[32,144,128]{2,1,0:T(8,128)(2,1)} %get-tuple-element.55), calls=%async_computation.5 | async-start | bytes 2359296 | tf_op jit(solution)/shard_map/all_to_all | solution.py:311
  177.7 1.9 collective-permute-start.11
  179.6 1.4 collective-permute-start.12
  181.0 2.1 collective-permute-start.13
  183.1 18.8 %collective-permute-done.11.v1 = bf16[8,3,128,128]{3,2,1,0:T(8,128)(2,1)S(1)} collective-permute-done((bf16[8,3,128,128]{3,2,1,0:T(8,128)(2,1)S(1)}, bf16[8,3,128,128]{3,2,1,0:T(8,128)(2,1)S(1)}, u32[]{:S(2)}, u32[]{:S(2)}) %collective-permute-start.11) | collective-permute-done | bytes 786464 | tf_op jit(solution)/shard_map/ppermute | solution.py:37
  201.9 8.5 %collective-permute-done.13.v3 = bf16[8,3,128,128]{3,2,1,0:T(8,128)(2,1)S(1)} collective-permute-done((bf16[8,3,128,128]{3,2,1,0:T(8,128)(2,1)S(1)}, bf16[8,3,128,128]{3,2,1,0:T(8,128)(2,1)S(1)}, u32[]{:S(2)}, u32[]{:S(2)}) %collective-permute-start.13) | collective-permute-done | bytes 786464 | tf_op jit(solution)/shard_map/ppermute | solution.py:37
  211.3 12.3 %shard_map.76 = (bf16[32,128,128]{2,1,0:T(8,128)(2,1)}, bf16[32,128,256]{2,1,0:T(8,128)(2,1)}, bf16[32,128,256]{2,1,0:T(8,128)(2,1)}) custom-call(bf16[8,3,128,128]{3,2,1,0:T(8,128)(2,1)} %copy-done.6, bf16[8,3,128,128]{3,2,1,0:T(8,128)(2,1)} %copy-done.7, bf16[8,3,128,128]{3,2,1,0:T(8,128)(2,1)} %copy-done.8, bf16[8,3,128,128]{3,2,1,0:T(8,128)(2,1)} %copy-done.9, ...), custom_call_target="tpu_custom_call" | custom-call | tf_op jit(solution)/shard_map/pallas_call | solution.py:295
  224.8 2.2 shard_map.83
  227.8 4.8 %collective-permute-done.17.g_ref = bf16[128,128]{1,0:T(8,128)(2,1)S(1)} collective-permute-done((bf16[128,128]{1,0:T(8,128)(2,1)}, bf16[128,128]{1,0:T(8,128)(2,1)S(1)}, u32[]{:S(2)}, u32[]{:S(2)}) %collective-permute-start.17) | collective-permute-done | bytes 32800 | tf_op jit(solution)/shard_map/ppermute | solution.py:37
  233.2 1.6 shard_map.84.mine_ref.g_ref
  234.8 1.4 collective-permute-done.18.theirs_ref
  236.8 4.7 %shard_map.85 = (bf16[32,144,128]{2,1,0:T(8,128)(2,1)}, bf16[128,256]{1,0:T(8,128)(2,1)}) custom-call(bf16[144,128]{1,0:T(8,128)(2,1)} %shard_map.84.mine_ref.g_ref, bf16[144,128]{1,0:T(8,128)(2,1)} %copy-done.24, f32[8,128]{1,0:T(8,128)} %get-tuple-element.57.s_ref, bf16[2,32,2,128,256]{4,3,2,1,0:T(8,128)(2,1)} %bitcast.45, ...), custom_call_target="tpu_custom_call" | custom-call | flops 268435456 | bytes 4194304 | tf_op jit(solution)/shard_map/pallas_call | solution.py:295
  241.5 6.1 %all-to-all-start.6 = ((bf16[32,144,128]{2,1,0:T(8,128)(2,1)}), bf16[32,144,128]{2,1,0:T(8,128)(2,1)S(1)}, u32[]{:S(2)}, u32[]{:S(2)}) async-start(bf16[32,144,128]{2,1,0:T(8,128)(2,1)} %get-tuple-element.58), calls=%async_computation.6 | async-start | bytes 2359296 | tf_op jit(solution)/shard_map/all_to_all | solution.py:311
  248.4 4.0 %shard_map.88 = (f32[136,128]{1,0:T(8,128)}, f32[136,128]{1,0:T(8,128)}) custom-call(bf16[32,128,128]{2,1,0:T(8,128)(2,1)} %get-tuple-element.63.g_ref, bf16[2,32,2,128,256]{4,3,2,1,0:T(8,128)(2,1)} %bitcast.46, bf16[2,32,128,256]{3,2,1,0:T(8,128)(2,1)} %collective-permute-done.1.r_ref), custom_call_target="tpu_custom_call" | custom-call | flops 268435456 | bytes 4194304 | tf_op jit(solution)/shard_map/pallas_call | solution.py:295
  254.6 1.6 shard_map.89
  256.3 9.9 %all-to-all-done.6.got_ref = bf16[32,144,128]{2,1,0:T(8,128)(2,1)S(1)} async-done(((bf16[32,144,128]{2,1,0:T(8,128)(2,1)}), bf16[32,144,128]{2,1,0:T(8,128)(2,1)S(1)}, u32[]{:S(2)}, u32[]{:S(2)}) %all-to-all-start.6) | async-done | bytes 1179680 | tf_op jit(solution)/shard_map/all_to_all | solution.py:311
  267.2 2.2 shard_map.86
  273.8 4.2 %collective-permute-done.20.far_ref = bf16[128,256]{1,0:T(8,128)(2,1)S(1)} collective-permute-done((bf16[128,256]{1,0:T(8,128)(2,1)S(1)}, bf16[128,256]{1,0:T(8,128)(2,1)S(1)}, u32[]{:S(2)}, u32[]{:S(2)}) %collective-permute-start.20) | collective-permute-done | bytes 65568 | tf_op jit(solution)/shard_map/ppermute | solution.py:37
  279.4 5.8 %shard_map.87 = bf16[32,2,128,256]{3,2,1,0:T(8,128)(2,1)} custom-call(bf16[32,128,256]{2,1,0:T(8,128)(2,1)} %get-tuple-element.49.keep_ref, bf16[32,128,256]{2,1,0:T(8,128)(2,1)} %copy-done.5, bf16[128,256]{1,0:T(8,128)(2,1)} %get-tuple-element.67.local_ref, bf16[128,256]{1,0:T(8,128)(2,1)} %copy-done.20, f32[32,2,1,256]{3,2,1,0:T(1,128)} %bitcast.52), custom_call_target="tpu_custom_call" | custom-call | flops 1073741824 | bytes 8388608 | tf_op jit(solution)/shard_map/pallas_call | solution.py:439
  (121 shorter events, 29.3 us)
Async XLA Ops:
  0.6 5.3 %copy-start = (bf16[2,128,256]{2,1,0:T(8,128)(2,1)S(1)}, bf16[2,128,256]{2,1,0:T(8,128)(2,1)}, u32[]{:S(2)}) copy-start(bf16[2,128,256]{2,1,0:T(8,128)(2,1)} %param.5) | copy-start | bytes 393220
  0.7 4.8 %copy-start.31 = (bf16[2,1,256]{2,0,1:T(2,128)(2,1)S(1)}, bf16[2,1,256]{2,0,1:T(2,128)(2,1)}, u32[]{:S(2)}) copy-start(bf16[2,1,256]{2,0,1:T(2,128)(2,1)} %param.8) | copy-start | bytes 3076
  5.4 36.7 %collective-permute-start.1 = (bf16[2,32,128,256]{3,2,1,0:T(8,128)(2,1)}, bf16[2,32,128,256]{3,2,1,0:T(8,128)(2,1)}, u32[]{:S(2)}, u32[]{:S(2)}) collective-permute-start(bf16[2,32,128,256]{3,2,1,0:T(8,128)(2,1)} %dynamic-slice_bitcast_fusion), channel_id=1, source_target_pairs={{0,32},{1,33},{2,34},{3,35},{4,36},{5,37},{6,38},{7,39},{8,40},{9,... | collective-permute-start | bytes 12582920 | tf_op jit(solution)/shard_map/ppermute | solution.py:37
  5.4 5.9 %collective-permute-start = (bf16[2,128]{1,0:T(2,128)(2,1)S(1)}, bf16[2,128]{1,0:T(2,128)(2,1)S(1)}, u32[]{:S(2)}, u32[]{:S(2)}) collective-permute-start(bf16[2,128]{1,0:T(2,128)(2,1)S(1)} %fusion.3), channel_id=1, source_target_pairs={{0,32},{1,33},{2,34},{3,35},{4,36},{5,37},{6,38},{7,39},{8,40},{9,... | collective-permute-start | bytes 1544 | tf_op jit(solution)/shard_map/ppermute | solution.py:37
  46.3 1.6 collective-permute-start.2
  78.9 1.6 collective-permute-start.3
  82.7 5.7 %collective-permute-start.4 = (bf16[128,128]{1,0:T(8,128)(2,1)}, bf16[128,128]{1,0:T(8,128)(2,1)S(1)}, u32[]{:S(2)}, u32[]{:S(2)}) collective-permute-start(bf16[128,128]{1,0:T(8,128)(2,1)} %get-tuple-element.41), channel_id=1, source_target_pairs={{0,64},{1,65},{2,66},{3,67},{4,68},{5,69},{6,70},{7,71},{8,72},{9,... | collective-permute-start | bytes 98312 | tf_op jit(solution)/shard_map/ppermute | solution.py:37
  90.9 4.1 %copy-start.13 = (bf16[2,128,256]{2,1,0:T(8,128)(2,1)S(1)}, bf16[2,128,256]{2,1,0:T(8,128)(2,1)}, u32[]{:S(2)}) copy-start(bf16[2,128,256]{2,1,0:T(8,128)(2,1)} %param.6) | copy-start | bytes 393220
  90.9 22.0 %all-to-all-start.2 = ((bf16[32,144,128]{2,1,0:T(8,128)(2,1)}), bf16[32,144,128]{2,1,0:T(8,128)(2,1)S(1)}, u32[]{:S(2)}, u32[]{:S(2)}) async-start(bf16[32,144,128]{2,1,0:T(8,128)(2,1)} %get-tuple-element.42), calls=%async_computation.2 | async-start | bytes 2359296 | tf_op jit(solution)/shard_map/all_to_all | solution.py:311
  113.0 4.3 %copy-start.1 = (bf16[32,144,128]{2,1,0:T(8,128)(2,1)}, bf16[32,144,128]{2,1,0:T(8,128)(2,1)S(1)}, u32[]{:S(2)}) copy-start(bf16[32,144,128]{2,1,0:T(8,128)(2,1)S(1)} %all-to-all-done.2.g_ref.f2) | copy-start | bytes 3538948
  113.0 19.6 %all-to-all-start.3 = ((bf16[32,128,128]{2,1,0:T(8,128)(2,1)}), bf16[32,128,128]{2,1,0:T(8,128)(2,1)S(1)}, u32[]{:S(2)}, u32[]{:S(2)}) async-start(bf16[32,128,128]{2,1,0:T(8,128)(2,1)} %shard_map.77), calls=%async_computation.3 | async-start | bytes 2097152 | tf_op jit(solution)/shard_map/all_to_all | solution.py:311
  121.4 17.0 %copy-start.25 = (bf16[128,128]{1,0:T(8,128)(2,1)S(1)}, bf16[128,128]{1,0:T(8,128)(2,1)}, u32[]{:S(2)}) copy-start(bf16[128,128]{1,0:T(8,128)(2,1)} %get-tuple-element.46) | copy-start | bytes 98308
  121.4 17.0 %copy-start.26 = (bf16[128,128]{1,0:T(8,128)(2,1)S(1)}, bf16[128,128]{1,0:T(8,128)(2,1)}, u32[]{:S(2)}) copy-start(bf16[128,128]{1,0:T(8,128)(2,1)} %get-tuple-element.47) | copy-start | bytes 98308
  121.4 17.0 %copy-start.27 = (bf16[128,128]{1,0:T(8,128)(2,1)S(1)}, bf16[128,128]{1,0:T(8,128)(2,1)}, u32[]{:S(2)}) copy-start(bf16[128,128]{1,0:T(8,128)(2,1)} %get-tuple-element.48) | copy-start | bytes 98308
  121.4 14.2 %collective-permute-start.5 = (f32[136,128]{1,0:T(8,128)}, f32[136,128]{1,0:T(8,128)S(1)}, u32[]{:S(2)}, u32[]{:S(2)}) collective-permute-start(f32[136,128]{1,0:T(8,128)} %get-tuple-element.44), channel_id=1, source_target_pairs={{0,32},{1,33},{2,34},{3,35},{4,36},{5,37},{6,38},{7,39},{8,40},{9,... | collective-permute-start | bytes 208904 | tf_op jit(solution)/shard_map/ppermute | solution.py:37
  132.6 1.0 copy-start.4
  139.2 12.5 %collective-permute-start.6 = (bf16[2,128,128]{2,1,0:T(8,128)(2,1)S(1)}, bf16[2,128,128]{2,1,0:T(8,128)(2,1)S(1)}, u32[]{:S(2)}, u32[]{:S(2)}) collective-permute-start(bf16[2,128,128]{2,1,0:T(8,128)(2,1)S(1)} %maximum_select_fusion), channel_id=1, source_target_pairs={{0,64},{1,65},{2,66},{3,67},{4,68},{5,69},{6,70},{7,71},{8,72},{9,... | collective-permute-start | bytes 196616 | tf_op jit(solution)/shard_map/ppermute | solution.py:37
  144.0 1.4 collective-permute-start.15
  147.4 12.8 %all-to-all-start.4 = ((f32[32,8,128]{2,1,0:T(8,128)}), f32[32,8,128]{2,1,0:T(8,128)S(1)}, u32[]{:S(2)}, u32[]{:S(2)}) async-start(f32[32,8,128]{2,1,0:T(8,128)} %shard_map.80), calls=%async_computation.4 | async-start | bytes 262144 | tf_op jit(solution)/shard_map/all_to_all | solution.py:311
  152.5 10.2 %collective-permute-start.7 = (bf16[3,128,128]{2,1,0:T(8,128)(2,1)S(1)}, bf16[3,128,128]{2,1,0:T(8,128)(2,1)S(1)}, u32[]{:S(2)}, u32[]{:S(2)}) collective-permute-start(bf16[3,128,128]{2,1,0:T(8,128)(2,1)S(1)} %get-tuple-element.69), channel_id=1, source_target_pairs={{0,16},{1,17},{2,18},{3,19},{4,20},{5,21},{6,22},{7,23},{8,24},{9,... | collective-permute-start | bytes 294920 | tf_op jit(solution)/shard_map/ppermute | solution.py:37
  162.6 3.6 %collective-permute-start.16 = (bf16[144,128]{1,0:T(8,128)(2,1)}, bf16[144,128]{1,0:T(8,128)(2,1)S(1)}, u32[]{:S(2)}, u32[]{:S(2)}) collective-permute-start(bf16[144,128]{1,0:T(8,128)(2,1)} %get-tuple-element.53.mine_ref.g_ref), channel_id=1, source_target_pairs={{0,32},{1,33},{2,34},{3,35},{4,36},{5,37},{6,38},{7,39},{8,40},{9,... | collective-permute-start | bytes 110600 | tf_op jit(solution)/shard_map/ppermute | solution.py:37
  162.7 14.9 %collective-permute-start.8 = (bf16[2,3,128,128]{3,2,1,0:T(8,128)(2,1)S(1)}, bf16[2,3,128,128]{3,2,1,0:T(8,128)(2,1)S(1)}, u32[]{:S(2)}, u32[]{:S(2)}) collective-permute-start(bf16[2,3,128,128]{3,2,1,0:T(8,128)(2,1)S(1)} %pad_maximum_fusion), channel_id=1, source_target_pairs={{0,1},{1,2},{2,3},{3,0},{4,5},{5,6},{6,7},{7,4},{8,9},{9,10},{10,1... | collective-permute-start | bytes 589832 | tf_op jit(solution)/shard_map/ppermute | solution.py:37
  163.3 14.3 %collective-permute-start.9 = (bf16[2,3,128,128]{3,2,1,0:T(8,128)(2,1)S(1)}, bf16[2,3,128,128]{3,2,1,0:T(8,128)(2,1)S(1)}, u32[]{:S(2)}, u32[]{:S(2)}) collective-permute-start(bf16[2,3,128,128]{3,2,1,0:T(8,128)(2,1)S(1)} %pad_maximum_fusion), channel_id=1, source_target_pairs={{0,3},{1,0},{2,1},{3,2},{4,7},{5,4},{6,5},{7,6},{8,11},{9,8},{10,9... | collective-permute-start | bytes 589832 | tf_op jit(solution)/shard_map/ppermute | solution.py:37
  166.0 11.7 %collective-permute-start.10 = (bf16[2,3,128,128]{3,2,1,0:T(8,128)(2,1)S(1)}, bf16[2,3,128,128]{3,2,1,0:T(8,128)(2,1)S(1)}, u32[]{:S(2)}, u32[]{:S(2)}) collective-permute-start(bf16[2,3,128,128]{3,2,1,0:T(8,128)(2,1)S(1)} %pad_maximum_fusion), channel_id=1, source_target_pairs={{0,2},{1,3},{2,0},{3,1},{4,6},{5,7},{6,4},{7,5},{8,10},{9,11},{10,... | collective-permute-start | bytes 589832 | tf_op jit(solution)/shard_map/ppermute | solution.py:37
  171.4 52.2 %all-to-all-start.5 = ((bf16[32,144,128]{2,1,0:T(8,128)(2,1)}), bf16[32,144,128]{2,1,0:T(8,128)(2,1)S(1)}, u32[]{:S(2)}, u32[]{:S(2)}) async-start(bf16[32,144,128]{2,1,0:T(8,128)(2,1)} %get-tuple-element.55), calls=%async_computation.5 | async-start | bytes 2359296 | tf_op jit(solution)/shard_map/all_to_all | solution.py:311
  177.7 32.7 %copy-start.6 = (bf16[8,3,128,128]{3,2,1,0:T(8,128)(2,1)}, bf16[8,3,128,128]{3,2,1,0:T(8,128)(2,1)S(1)}, u32[]{:S(2)}) copy-start(bf16[8,3,128,128]{3,2,1,0:T(8,128)(2,1)S(1)} %constant_dynamic-update-slice_fusion.v0) | copy-start | bytes 2359300
  177.7 24.2 %collective-permute-start.11 = (bf16[8,3,128,128]{3,2,1,0:T(8,128)(2,1)S(1)}, bf16[8,3,128,128]{3,2,1,0:T(8,128)(2,1)S(1)}, u32[]{:S(2)}, u32[]{:S(2)}) collective-permute-start(bf16[8,3,128,128]{3,2,1,0:T(8,128)(2,1)S(1)} %constant_dynamic-update-slice_fusion.v0), channel_id=1, source_target_pairs={{0,4},{1,5},{2,6},{3,7},{4,8},{5,9},{6,10},{7,11},{8,12},{9,13},{1... | collective-permute-start | bytes 2359304 | tf_op jit(solution)/shard_map/ppermute | solution.py:37
  179.6 22.4 %collective-permute-start.12 = (bf16[8,3,128,128]{3,2,1,0:T(8,128)(2,1)S(1)}, bf16[8,3,128,128]{3,2,1,0:T(8,128)(2,1)S(1)}, u32[]{:S(2)}, u32[]{:S(2)}) collective-permute-start(bf16[8,3,128,128]{3,2,1,0:T(8,128)(2,1)S(1)} %constant_dynamic-update-slice_fusion.v0), channel_id=1, source_target_pairs={{0,12},{1,13},{2,14},{3,15},{4,0},{5,1},{6,2},{7,3},{8,4},{9,5},{1... | collective-permute-start | bytes 2359304 | tf_op jit(solution)/shard_map/ppermute | solution.py:37
  181.0 29.4 %collective-permute-start.13 = (bf16[8,3,128,128]{3,2,1,0:T(8,128)(2,1)S(1)}, bf16[8,3,128,128]{3,2,1,0:T(8,128)(2,1)S(1)}, u32[]{:S(2)}, u32[]{:S(2)}) collective-permute-start(bf16[8,3,128,128]{3,2,1,0:T(8,128)(2,1)S(1)} %constant_dynamic-update-slice_fusion.v0), channel_id=1, source_target_pairs={{0,8},{1,9},{2,10},{3,11},{4,12},{5,13},{6,14},{7,15},{8,0},{9,1},... | collective-permute-start | bytes 2359304 | tf_op jit(solution)/shard_map/ppermute | solution.py:37
  201.9 8.5 %copy-start.7 = (bf16[8,3,128,128]{3,2,1,0:T(8,128)(2,1)}, bf16[8,3,128,128]{3,2,1,0:T(8,128)(2,1)S(1)}, u32[]{:S(2)}) copy-start(bf16[8,3,128,128]{3,2,1,0:T(8,128)(2,1)S(1)} %collective-permute-done.11.v1) | copy-start | bytes 2359300
  201.9 8.5 %copy-start.8 = (bf16[8,3,128,128]{3,2,1,0:T(8,128)(2,1)}, bf16[8,3,128,128]{3,2,1,0:T(8,128)(2,1)S(1)}, u32[]{:S(2)}) copy-start(bf16[8,3,128,128]{3,2,1,0:T(8,128)(2,1)S(1)} %collective-permute-done.12.v2) | copy-start | bytes 2359300
  223.6 54.5 %collective-permute-start.14 = (bf16[32,128,256]{2,1,0:T(8,128)(2,1)}, bf16[32,128,256]{2,1,0:T(8,128)(2,1)S(1)}, u32[]{:S(2)}, u32[]{:S(2)}) collective-permute-start(bf16[32,128,256]{2,1,0:T(8,128)(2,1)} %get-tuple-element.50), channel_id=1, source_target_pairs={{0,32},{1,33},{2,34},{3,35},{4,36},{5,37},{6,38},{7,39},{8,40},{9,... | collective-permute-start | bytes 6291464 | tf_op jit(solution)/shard_map/ppermute | solution.py:37
  223.7 1.1 copy-start.2
  227.0 5.6 %collective-permute-start.17 = (bf16[128,128]{1,0:T(8,128)(2,1)}, bf16[128,128]{1,0:T(8,128)(2,1)S(1)}, u32[]{:S(2)}, u32[]{:S(2)}) collective-permute-start(bf16[128,128]{1,0:T(8,128)(2,1)} %shard_map.83), channel_id=1, source_target_pairs={{0,64},{1,65},{2,66},{3,67},{4,68},{5,69},{6,70},{7,71},{8,72},{9,... | collective-permute-start | bytes 98312 | tf_op jit(solution)/shard_map/ppermute | solution.py:37
  234.8 1.4 collective-permute-start.18
  241.5 6.1 %copy-start.30 = (s32[1,64,2]{1,2,0:T(2,128)S(1)}, s32[1,64,2]{1,2,0:T(2,128)}, u32[]{:S(2)}) copy-start(s32[1,64,2]{1,2,0:T(2,128)} %param.9) | copy-start | bytes 1540
  241.5 24.7 %all-to-all-start.6 = ((bf16[32,144,128]{2,1,0:T(8,128)(2,1)}), bf16[32,144,128]{2,1,0:T(8,128)(2,1)S(1)}, u32[]{:S(2)}, u32[]{:S(2)}) async-start(bf16[32,144,128]{2,1,0:T(8,128)(2,1)} %get-tuple-element.58), calls=%async_computation.6 | async-start | bytes 2359296 | tf_op jit(solution)/shard_map/all_to_all | solution.py:311
  252.5 17.9 %copy-start.10 = (bf16[128,128]{1,0:T(8,128)(2,1)S(1)}, bf16[128,128]{1,0:T(8,128)(2,1)}, u32[]{:S(2)}) copy-start(bf16[128,128]{1,0:T(8,128)(2,1)} %get-tuple-element.51.x_ref) | copy-start | bytes 98308
  252.5 1.6 collective-permute-start.21
  256.3 14.1 %copy-start.15 = (bf16[128,128]{1,0:T(8,128)(2,1)S(1)}, bf16[128,128]{1,0:T(8,128)(2,1)}, u32[]{:S(2)}) copy-start(bf16[128,128]{1,0:T(8,128)(2,1)} %shard_map.89) | copy-start | bytes 98308
  266.2 1.0 copy-start.3
  267.2 4.3 %copy-start.14 = (bf16[2,128,256]{2,1,0:T(8,128)(2,1)S(1)}, bf16[2,128,256]{2,1,0:T(8,128)(2,1)}, u32[]{:S(2)}) copy-start(bf16[2,128,256]{2,1,0:T(8,128)(2,1)} %param.6) | copy-start | bytes 393220
  267.2 4.3 %copy-start.21 = (bf16[128,256]{1,0:T(8,128)(2,1)S(1)}, bf16[128,256]{1,0:T(8,128)(2,1)}, u32[]{:S(2)}) copy-start(bf16[128,256]{1,0:T(8,128)(2,1)} %get-tuple-element.61) | copy-start | bytes 196612
  267.2 4.3 %copy-start.22 = (bf16[128,256]{1,0:T(8,128)(2,1)S(1)}, bf16[128,256]{1,0:T(8,128)(2,1)}, u32[]{:S(2)}) copy-start(bf16[128,256]{1,0:T(8,128)(2,1)} %get-tuple-element.60) | copy-start | bytes 196612
  270.3 1.3 collective-permute-start.19
  270.4 2.8 collective-permute-start.22
  272.3 5.8 %collective-permute-start.20 = (bf16[128,256]{1,0:T(8,128)(2,1)S(1)}, bf16[128,256]{1,0:T(8,128)(2,1)S(1)}, u32[]{:S(2)}, u32[]{:S(2)}) collective-permute-start(bf16[128,256]{1,0:T(8,128)(2,1)S(1)} %get-tuple-element.66), channel_id=1, source_target_pairs={{0,64},{1,65},{2,66},{3,67},{4,68},{5,69},{6,70},{7,71},{8,72},{9,... | collective-permute-start | bytes 196616 | tf_op jit(solution)/shard_map/ppermute | solution.py:37
  278.1 1.4 copy-start.5
  (12 other events, 8.1 us)

commit v2 on v1

v2 whole, which is shorter than its diff:
```python
import functools

import jax
import jax.numpy as jnp
from jax import lax
from jax.experimental import pallas as pl
from jax.experimental.pallas import tpu as pltpu
from jax.sharding import PartitionSpec as P

D = 8192
EPS = 1e-05
M = 128
H = 128
N = 32
R = M + 16
F32 = jnp.float32
BF16 = jnp.bfloat16
BOTH = ("pipe", "dp")
VM = pl.BlockSpec(memory_space=pltpu.VMEM)
HBM = pl.BlockSpec(memory_space=pltpu.HBM)
MIB = 1 << 20


def pairs(fn):
    out = []
    for i in range(128):
        p, d = divmod(i, 32)
        zh, c = divmod(p, 2)
        zl, r = divmod(d, 16)
        y, x = divmod(r, 4)
        zh2, c2, zl2, y2, x2 = fn(zh, c, zl, y, x)
        out.append((i, (zh2 * 2 + c2) * 32 + zl2 * 16 + (y2 % 4) * 4 + x2 % 4))
    return out


def move(value, fn):
    return lax.ppermute(value, BOTH, pairs(fn))


def move_some(value, fn, keep):
    return lax.ppermute(value, BOTH, [(i, j) for i, j in pairs(fn) if (i // 64, i // 32 % 2) in keep])


def other_core(zh, c, zl, y, x):
    return (zh, 1 - c, zl, y, x)


def other_zh(zh, c, zl, y, x):
    return (1 - zh, c, zl, y, x)


def other_both(zh, c, zl, y, x):
    return (1 - zh, 1 - c, zl, y, x)


def other_zl(zh, c, zl, y, x):
    return (zh, c, 1 - zl, y, x)


def first_axis(k):
    return lambda zh, c, zl, y, x: (zh, c, zl, y + (k if c else 0), x + (0 if c else k))


def second_axis(k):
    return lambda zh, c, zl, y, x: (zh, c, zl, y + (0 if c else k), x + (k if c else 0))


def along_y(k):
    return lambda zh, c, zl, y, x: (zh, c, zl, y + k, x)


SHIFTS = (0, 1, 3, 2)


def place():
    p = lax.axis_index("pipe")
    return p // 2, p % 2


def block_index(sign):
    _, c = place()
    dp = lax.axis_index("dp")
    y, x = (dp // 4) % 4, dp % 4
    b = jnp.where(c == 0, y, x)
    sa = jnp.where(c == 0, 1, 4)
    sb = jnp.where(c == 0, 4, 1)

    def index(ib, i):
        return lax.rem(b + 4 + sign * SHIFTS[ib], 4) * sb + (i % 4) * sa + (i // 4) * 16

    return index


def step_index():
    _, c = place()
    dp = lax.axis_index("dp")
    zl, y, x = dp // 16, (dp // 4) % 4, dp % 4
    a = jnp.where(c == 0, x, y)
    b = jnp.where(c == 0, y, x)
    sa = jnp.where(c == 0, 1, 4)
    sb = jnp.where(c == 0, 4, 1)

    def index(ib, ia, iz):
        jb = lax.rem(b + 4 - SHIFTS[ib], 4) * sb
        ja = lax.rem(a + 4 - SHIFTS[ia], 4) * sa
        return jb + ja + (zl if iz == 0 else 1 - zl) * 16

    return index


def to_rows(value):
    return jnp.sum(jnp.transpose(value), axis=0, keepdims=True)


def to_cols(row):
    return jnp.transpose(jnp.broadcast_to(row, (M, H)))


def extra_rows(row):
    high = row.astype(BF16)
    low = (row - high.astype(F32)).astype(BF16)
    i = lax.broadcasted_iota(jnp.int32, (16, M), 0)
    value = jnp.where(i == 0, high.astype(F32), jnp.where(i == 1, low.astype(F32), 0.0))
    return value.astype(BF16)


def read_extra(block):
    return jnp.sum(block.astype(F32), axis=0, keepdims=True)


def split_kernel(w_ref, own_ref, send_ref, sem):
    _, c = place()
    copies = [pltpu.make_async_copy(w_ref.at[b, :, 1 - c], send_ref.at[b], sem.at[b]) for b in range(2)]
    copies += [pltpu.make_async_copy(w_ref.at[b, :, c], own_ref.at[b], sem.at[2 + b]) for b in range(2)]
    for copy in copies:
        copy.start()
    for copy in copies:
        copy.wait()


def pick_kernel(own_ref, other_ref, out_ref, sem):
    zh, c = place()

    def run(own_ticks, other_ticks):
        copies = []
        for i in range(2):
            b = zh if i == 0 else 1 - zh
            copies.append(pltpu.make_async_copy(own_ref.at[b], out_ref.at[own_ticks[i]], sem.at[i]))
            copies.append(pltpu.make_async_copy(other_ref.at[b], out_ref.at[other_ticks[i]], sem.at[2 + i]))
        for copy in copies:
            copy.start()
        for copy in copies:
            copy.wait()

    pl.when((zh ^ c) == 0)(lambda: run((0, 3), (1, 2)))
    pl.when((zh ^ c) == 1)(lambda: run((1, 2), (0, 3)))


def load_kernel(tick, w_ref, out_ref, sem):
    parts = [pl.ds(N // 8 * i, N // 8) for i in range(8)]
    copies = [pltpu.make_async_copy(w_ref.at[tick, q], out_ref.at[q], sem.at[i]) for i, q in enumerate(parts)]
    for copy in copies:
        copy.start()
    for copy in copies:
        copy.wait()


def payload_kernel(x_ref, gain_ref, out_ref, ft_ref):
    x = x_ref[...].astype(F32)
    f = (x * gain_ref[...].astype(F32)).astype(BF16)
    ft_ref[...] = jnp.transpose(f)
    extra = extra_rows(to_rows(x * x))
    for j in range(out_ref.shape[0]):
        out_ref[j, 0:M, :] = f
        out_ref[j, M:R, :] = extra


def forward_kernel(v0, v1, v2, v3, w_ref, keep_ref, send_ref):
    _, c = place()
    index = block_index(-1)
    sums = jnp.zeros((16, M), F32)
    total = jnp.zeros((M, 2 * H), F32)
    for ref in (v0, v1, v2, v3):
        sums = sums + jnp.sum(ref[:, M:R, :].astype(F32), axis=0)
    for ib, ref in enumerate((v0, v1, v2, v3)):
        f = jnp.concatenate([ref[i, 0:M, :] for i in range(8)], axis=1)
        w = jnp.concatenate([w_ref[index(ib, i)] for i in range(8)], axis=0)
        total = total + jnp.dot(f, w, preferred_element_type=F32)
    sums = jnp.broadcast_to(jnp.sum(sums, axis=0, keepdims=True), (8, M))
    first = c == 0
    keep_ref[0:M, :] = jnp.where(first, total[:, :H], total[:, H:])
    send_ref[0:M, :] = jnp.where(first, total[:, H:], total[:, :H])
    keep_ref[M : M + 8, :] = sums
    send_ref[M : M + 8, :] = sums


def last_forward_kernel(f_ref, w_ref, keep_ref, send_ref):
    _, c = place()
    total = jnp.zeros((M, 2 * H), F32)
    for ch in range(4):
        f = jnp.concatenate([f_ref[8 * ch + j] for j in range(8)], axis=1)
        w = w_ref[8 * ch : 8 * ch + 8].reshape(8 * 128, 2 * H)
        total = total + jnp.dot(f, w, preferred_element_type=F32)
    first = c == 0
    keep_ref[...] = jnp.where(first, total[:, :H], total[:, H:])
    send_ref[...] = jnp.where(first, total[:, H:], total[:, :H])


def combine_kernel(keep_ref, recv_ref, x_ref, gain_ref, next_ref, p_ref, s_ref, out_ref=None, ft_ref=None):
    squares = keep_ref[M : M + 8, :] + recv_ref[M : M + 8, :]
    scale = lax.rsqrt(squares / D + EPS)
    s_ref[...] = scale
    p = keep_ref[0:M, :] + recv_ref[0:M, :]
    p_ref[...] = p
    new = (x_ref[...].astype(F32) + to_cols(scale[0:1]) * p).astype(BF16)
    next_ref[...] = new
    if out_ref is not None:
        x = new.astype(F32)
        f = (x * gain_ref[...].astype(F32)).astype(BF16)
        ft_ref[...] = jnp.transpose(f)
        extra = extra_rows(to_rows(x * x))
        for j in range(out_ref.shape[0]):
            out_ref[j, 0:M, :] = f
            out_ref[j, M:R, :] = extra


def third_combine_kernel(keep_ref, recv_ref, x_ref, gain_ref, gn_ref, next_ref, p_ref, s_ref, f_ref, ft_ref, sums_ref):
    squares = keep_ref[M : M + 8, :] + recv_ref[M : M + 8, :]
    scale = lax.rsqrt(squares / D + EPS)
    s_ref[...] = scale
    p = keep_ref[0:M, :] + recv_ref[0:M, :]
    p_ref[...] = p
    new = (x_ref[...].astype(F32) + to_cols(scale[0:1]) * p).astype(BF16)
    next_ref[...] = new
    x = new.astype(F32)
    f = (x * gain_ref[...].astype(F32)).astype(BF16)
    f_ref[...] = f
    ft_ref[...] = jnp.transpose(f)
    i = lax.broadcasted_iota(jnp.int32, (8, M), 0)
    sums = jnp.where(i == 0, to_rows(x * x), jnp.where(i == 1, to_rows(x * gn_ref[...]), 0.0))
    for j in range(16):
        sums_ref[j] = sums


def last_combine_kernel(keep_ref, recv_ref, x_ref, s_ref, next_ref):
    p = keep_ref[...] + recv_ref[...]
    next_ref[...] = (x_ref[...].astype(F32) + to_cols(s_ref[0:1, :]) * p).astype(BF16)


def turned(left, right):
    return jnp.concatenate([jnp.transpose(left), jnp.transpose(right)], axis=0)


def backward_kernel(mine_ref, theirs_ref, s_ref, w_ref, o0, o1, o2, o3, gs_ref):
    _, c = place()
    first = c == 0
    a = mine_ref[0:M, :]
    b = theirs_ref[0:M, :]
    left = jnp.where(first, a, b)
    right = jnp.where(first, b, a)
    scale = to_cols(s_ref[0:1, :])
    gs_ref[:, :H] = (left.astype(F32) * scale).astype(BF16)
    gs_ref[:, H:] = (right.astype(F32) * scale).astype(BF16)
    extra = extra_rows(read_extra(mine_ref[M:R, :]) + read_extra(theirs_ref[M:R, :]))
    gt = turned(left, right)
    index = block_index(1)
    for ib, ref in enumerate((o0, o1, o2, o3)):
        w = jnp.concatenate([w_ref[index(ib, i)] for i in range(8)], axis=0)
        ref[:, 0:M, :] = jnp.dot(w, gt, preferred_element_type=F32).astype(BF16).reshape(8, H, M)
        for i in range(8):
            ref[i, M:R, :] = extra


def first_backward_kernel(g_ref, w_ref, o0, o1, o2, o3):
    gt = turned(g_ref[:, :H], g_ref[:, H:])
    index = block_index(1)
    for ib, ref in enumerate((o0, o1, o2, o3)):
        w = jnp.concatenate([w_ref[index(ib, i)] for i in range(8)], axis=0)
        ref[...] = jnp.dot(w, gt, preferred_element_type=F32).astype(BF16).reshape(8, H, M)


def sum_kernel(r0, r1, r2, r3, out):
    total = r0[...].astype(F32) + r1[...].astype(F32) + r2[...].astype(F32) + r3[...].astype(F32)
    out[:, 0:M, :] = total[:, 0:M, :].astype(BF16)
    if total.shape[1] == R:
        for i in range(8):
            out[i, M:R, :] = extra_rows(jnp.sum(total[i, M:R, :], axis=0, keepdims=True))


def last_sum_kernel(got_ref, gain_ref, gn_ref):
    total = jnp.sum(got_ref[...].astype(F32), axis=0)
    gn_ref[...] = jnp.transpose(total) * gain_ref[...].astype(F32)


def choose_kernel(a_ref, b_ref, out):
    zh, _ = place()
    out[...] = jnp.where(zh == 0, a_ref[...], b_ref[...])


def join_kernel(r0, r1, r2, r3, out):
    n = r0.shape[0]
    for i, ref in enumerate((r0, r1, r2, r3)):
        out[i * n : (i + 1) * n] = ref[...]


def turned(left, right):
    return jnp.concatenate([jnp.transpose(left), jnp.transpose(right)], axis=0)


def add_kernel(r, out):
    out[...] = jnp.sum(r[...], axis=0)


def last_grad_kernel(s0, s1, s2, s3, g_ref, gn_ref, x_ref, p_ref, out_ref, s_ref):
    total = s0[...] + s1[...] + s2[...] + s3[...]
    scale = lax.rsqrt(total[0:1, :] / D + EPS)
    s_ref[...] = jnp.broadcast_to(scale, (8, M))
    mix = scale * scale * scale * total[1:2, :] / D
    g = g_ref[...].astype(F32) + to_cols(scale) * gn_ref[...] - to_cols(mix) * x_ref[...].astype(F32)
    g = g.astype(BF16)
    out_ref[0:M, :] = g
    out_ref[M:R, :] = extra_rows(to_rows(g.astype(F32) * p_ref[...]))


def grad_kernel(got_ref, gain_ref, g_ref, s_ref, x_ref, *rest):
    out_ref = rest[-1]
    total = jnp.sum(got_ref[:, 0:M, :].astype(F32), axis=0)
    dots = jnp.sum(jnp.sum(got_ref[:, M:R, :].astype(F32), axis=0), axis=0, keepdims=True)
    gn = jnp.transpose(total) * gain_ref[...].astype(F32)
    scale = s_ref[0:1, :]
    mix = scale * scale * scale * dots / D
    g = g_ref[0:M, :].astype(F32) + to_cols(scale) * gn - to_cols(mix) * x_ref[...].astype(F32)
    if len(rest) == 2:
        g = g.astype(BF16).astype(F32) * to_cols(rest[0][0:1, :])
    out_ref[...] = g.astype(BF16)


def dots_kernel(g_ref, p_ref, out_ref):
    g = g_ref[...]
    out_ref[0:M, :] = g
    out_ref[M:R, :] = extra_rows(to_rows(g.astype(F32) * p_ref[...]))


def order_kernel(*refs):
    v, g0, g1, g2 = refs[0:4], refs[4:8], refs[8:12], refs[12:16]
    f3_ref, keep_ref, send_ref = refs[16:]
    zh, c = place()
    index = step_index()
    other = block_index(-1)

    def fill(first, second, q0_ref, q1_ref):
        for ib in range(4):
            for ia in range(4):
                for iz in range(2):
                    j = index(ib, ia, iz)
                    at = ia * 2 + iz
                    last = v[ib][at, 0]
                    f3_ref[j] = last
                    q0_ref[j, :, M:] = v[ib][at, 1]
                    q1_ref[j, :, M:] = v[ib][at, 2]
                    if second is None:
                        q1_ref[j, :, :M] = jnp.transpose(last)
            for i in range(8):
                j = other(ib, i)
                q0_ref[j, :, :M] = jnp.transpose(first[ib][i, 0:M, :])
                if second is not None:
                    q1_ref[j, :, :M] = jnp.transpose(second[ib][i, 0:M, :])

    for a in range(2):
        for b in range(2):
            q0, q1 = (keep_ref, send_ref) if b == 0 else (send_ref, keep_ref)
            first, second = (g0, g1) if a == 0 else (g2, None)
            pl.when(jnp.logical_and(zh == a, c == b))(functools.partial(fill, first, second, q0, q1))


def weight_grad_kernel(
    keep_ref, recv_ref, local_ref, far_ref, mine_ref, core_ref, far0_ref, far1_ref, factor_ref, out_ref, buf, sem
):
    zh, c = place()
    late = (zh + c) == 0
    local = jnp.where(late, jnp.concatenate([mine_ref[...], core_ref[...]], axis=1), local_ref[...])
    far = jnp.where(late, jnp.concatenate([far0_ref[...], far1_ref[...]], axis=1), far_ref[...])
    g = jnp.concatenate([local, far], axis=0)
    count = 4
    copies = []
    for i in range(N // count):
        part = pl.ds(i * count, count)
        for ref, which in ((keep_ref, c), (recv_ref, 1 - c)):
            value = jnp.dot(ref[part].reshape(count * H, 2 * M), g, preferred_element_type=F32)
            value = value.reshape(count, H, 2 * H) * factor_ref[part, which]
            buf[part, which] = value.astype(BF16)
        copies.append(pltpu.make_async_copy(buf.at[part], out_ref.at[part], sem.at[i]))
        copies[-1].start()
    for copy in copies:
        copy.wait()


def call(kernel, out, specs, args, scratch=(), flops=0, bytes_accessed=0, limit=4, out_specs=None, deps=()):
    count = len(args)

    def body(*refs):
        kernel(*refs[:count], *refs[count + len(deps) :])

    return pl.pallas_call(
        body,
        out_shape=[jax.ShapeDtypeStruct(s, d) for s, d in out],
        in_specs=list(specs) + [pl.BlockSpec(memory_space=pl.ANY)] * len(deps),
        out_specs=out_specs or [VM] * len(out),
        scratch_shapes=list(scratch),
        compiler_params=pltpu.CompilerParams(vmem_limit_bytes=limit * MIB),
        cost_estimate=pl.CostEstimate(flops=flops, bytes_accessed=bytes_accessed, transcendentals=0),
    )(*args, *deps)


MATMUL = dict(
    flops=2 * M * N * H * 2 * H,
    bytes_accessed=4 << 20,
    limit=6,
)


def plane_groups():
    groups = {}
    for i in range(128):
        p, d = divmod(i, 32)
        c = p % 2
        y, x = (d // 4) % 4, d % 4
        groups.setdefault((p, y if c == 0 else x), []).append((d // 16, x if c == 0 else y, i))
    return [[i for _, _, i in sorted(g)] for g in groups.values()]


PLANES = plane_groups()


def core_groups():
    groups = {}
    for i in range(128):
        p, d = divmod(i, 32)
        groups.setdefault((p // 2, (d // 4) % 4), []).append(i)
    return list(groups.values())


CORES = core_groups()


def exchange(value):
    return lax.all_to_all(value, BOTH, 0, 0, axis_index_groups=PLANES)


def along_second(parts):
    return [parts[0]] + [move(parts[i], second_axis(SHIFTS[i])) for i in (1, 2, 3)]


def gather(payload):
    row = exchange(payload)
    return along_second([row] * 4)


def scatter(parts, *deps):
    shape = parts[0].shape
    (total,) = call(sum_kernel, [(shape, BF16)], [VM] * 4, along_second(parts), deps=deps)
    return exchange(total), total


def gather_z(value):
    return jnp.stack([value, move(value, other_zl)])


def gather_first(both, dep):
    rows = [both] + [move(both, first_axis(k)) for k in SHIFTS[1:]]
    return call(join_kernel, [((8,) + both.shape[1:], BF16)], [VM] * 4, rows, deps=(dep,))[0]


def on_device(batches, cotangents, weights, gains, exponents):
    zh, c = place()
    e = zh ^ c
    w5 = weights.reshape(2, N, 2, H, 2 * H)

    def half(value, which):
        return lax.dynamic_slice_in_dim(value, which * H, H, axis=value.ndim - 1)

    own_gain = half(gains[:, 0], c)
    got_gain = move(half(gains[:, 0], 1 - c), other_core)
    gain = []
    for tick in range(4):
        copy_index = zh if tick < 2 else 1 - zh
        own = (e == 0) if tick in (0, 3) else (e == 1)
        both = jnp.where(own, own_gain, got_gain)
        gain.append(lax.dynamic_slice_in_dim(both, copy_index, 1, axis=0))

    x0 = half(lax.dynamic_index_in_dim(batches, zh, axis=0, keepdims=False), c)
    block = (M, H)
    wide = ((8, R, H), BF16)
    out0, ft0 = call(payload_kernel, [wide, (block, BF16)], [VM] * 2, (x0, gain[0]))
    g0 = gather(out0)

    started = move(ft0, other_core)
    own_w, send_w = call(
        split_kernel,
        [((2, N, H, 2 * H), BF16)] * 2,
        [VM],
        (w5,),
        scratch=[pltpu.SemaphoreType.DMA((4,))],
        out_specs=[HBM] * 2,
        limit=10,
        deps=(started,),
    )
    (all_w,) = call(
        pick_kernel,
        [((24, N, H, 2 * H), BF16)],
        [VM] * 2,
        (own_w, move(send_w, other_core)),
        scratch=[pltpu.SemaphoreType.DMA((4,))],
        out_specs=[HBM],
        limit=10,
    )

    def load(tick, *deps):
        return call(
            functools.partial(load_kernel, tick),
            [((N, H, 2 * H), BF16)],
            [HBM],
            (all_w,),
            scratch=[pltpu.SemaphoreType.DMA((8,))],
            deps=deps,
        )[0]

    cot = lax.dynamic_index_in_dim(cotangents, 1 - zh, axis=0, keepdims=False)
    first_parts = call(first_backward_kernel, [((8, H, M), BF16)] * 4, [VM] * 2, (cot, load(3)), **MATMUL)
    parts = along_second(first_parts)

    def forward(weight, gathered, deps):
        keep, send = call(
            forward_kernel, [((M + 8, H), F32)] * 2, [VM] * 5, (*gathered, weight), deps=deps, **MATMUL
        )
        return keep, move(send, other_core)

    outs = [(block, BF16), (block, F32), ((8, M), F32)]
    keep, recv = forward(load(0), g0, first_parts)
    x1, _, s0, out1, ft1 = call(
        combine_kernel, outs + [wide, (block, BF16)], [VM] * 4, (keep, recv, x0, gain[1])
    )
    g1 = gather(out1)
    (row3,) = call(sum_kernel, [((8, H, M), BF16)], [VM] * 4, parts)
    (gn3,) = call(last_sum_kernel, [(block, F32)], [VM] * 2, (exchange(row3), gain[3]))
    keep, recv = forward(load(1, out1), g1, ())
    x2, p1, s1 = call(combine_kernel, outs, [VM] * 4, (keep, recv, x1, gain[1]), deps=(gn3,))
    x2 = move(x2, other_zh)
    out2, ft2 = call(payload_kernel, [wide, (block, BF16)], [VM] * 2, (x2, gain[2]))
    g2 = gather(out2)
    mirror0 = move(jnp.where(zh == 1, ft0, ft2), other_zh)
    keep, recv = forward(load(2, out2), g2, (mirror0,))
    x3, p2, s2, f3, ft3, spread = call(
        third_combine_kernel,
        outs + [(block, BF16), (block, BF16), ((16, 8, M), F32)],
        [VM] * 5,
        (keep, recv, x2, gain[3], gn3),
    )
    (send3,) = call(choose_kernel, [(block, BF16)], [VM] * 2, (ft3, ft1), deps=(x3,))
    mirror1 = move(send3, other_zh)
    (sums,) = call(add_kernel, [((8, M), F32)], [VM], (lax.all_to_all(spread, BOTH, 0, 0, axis_index_groups=CORES),), deps=(mirror1,))
    first_rows = gather_z(jnp.stack([f3, mirror0, mirror1]))
    w2 = load(2, x3)
    sums = [sums] + [move(sums, along_y(k)) for k in SHIFTS[1:]]

    g3 = half(cot, c)
    mine2, s3 = call(
        last_grad_kernel,
        [((R, H), BF16), ((8, M), F32)],
        [VM] * 8,
        (*sums, g3, gn3, x3, p2),
        deps=(w2, first_rows),
    )

    def backward(weight, mine, s):
        theirs = move(mine, other_core)
        *parts, gs = call(
            backward_kernel, [wide] * 4 + [((M, 2 * H), BF16)], [VM] * 4, (mine, theirs, s, weight), **MATMUL
        )
        return parts, gs

    parts2, gs2 = backward(w2, mine2, s2)
    got2, row2 = scatter(parts2)
    w1 = load(1, row2)
    joined = gather_first(first_rows, row2)
    v = along_second([joined] * 4)
    (back1,) = call(
        grad_kernel,
        [(block, BF16)],
        [VM] * 5,
        (got2, gain[2], mine2, s2, x2),
        deps=(w1, joined),
    )
    back1 = move(back1, other_zh)
    (mine1,) = call(dots_kernel, [((R, H), BF16)], [VM] * 2, (back1, p1))
    parts1, gs1 = backward(w1, mine1, s1)

    f3_all, keep_t, send_t = call(
        order_kernel,
        [((N, M, H), BF16), ((N, H, 2 * M), BF16), ((N, H, 2 * M), BF16)],
        [VM] * 16,
        (*v, *g0, *g1, *g2),
        limit=14,
        deps=(gs1,),
    )
    recv_t = move(send_t, other_core)
    keep, send = call(last_forward_kernel, [(block, F32)] * 2, [VM] * 2, (f3_all, load(3, gs1)), **MATMUL)
    got1, row1 = scatter(parts1, send)
    recv = move(send, other_core)
    (x4,) = call(last_combine_kernel, [(block, BF16)], [VM] * 4, (keep, recv, x3, s3))
    is_first = e == 0
    shown = jnp.where(is_first, x4, x3)
    got = move(jnp.where(is_first, x3, x4), other_core)
    last = jnp.where(c == 0, jnp.concatenate([shown, got], 1), jnp.concatenate([got, shown], 1))

    gs3 = (cot.astype(F32) * s3[0][:, None]).astype(BF16)
    high = jnp.where(c == 0, gs2, gs3)
    local = jnp.where(zh == 0, gs1, high)
    far = move(jnp.where(zh == 0, high, gs1), other_zh)
    factor = jnp.repeat(jnp.exp2(-exponents[0].astype(F32)), H, axis=1).reshape(N, 2, 1, 2 * H)
    (mine0,) = call(
        grad_kernel,
        [(block, BF16)],
        [VM] * 6,
        (got1, gain[1], mine1, s1, x1, s0),
        deps=(factor, local),
    )
    far0 = move_some(mine0, other_zh, [(1, 0)])
    far1 = move_some(mine0, other_both, [(1, 1)])
    core = move_some(mine0, other_core, [(0, 1)])
    (total,) = call(
        weight_grad_kernel,
        [((N, 2, H, 2 * H), BF16)],
        [VM] * 9,
        (keep_t, recv_t, local, far, mine0, core, far0, far1, factor),
        scratch=[pltpu.VMEM((N, 2, H, 2 * H), BF16), pltpu.SemaphoreType.DMA((8,))],
        out_specs=[HBM],
        flops=2 * 256 * 256 * D,
        bytes_accessed=8 << 20,
        limit=11,
    )
    return (total.reshape(1, D, 2 * H), last[None])


def solution(mesh):
    return jax.shard_map(
        on_device,
        mesh=mesh,
        in_specs=(
            P(None, None, "dp"),
            P(None, None, "dp"),
            P(None, "pipe", None, "dp"),
            P(None, "pipe", "dp"),
            P("pipe", None, "dp"),
        ),
        out_specs=(P("pipe", None, "dp"), P("pipe", None, "dp")),
        check_vma=False,
    )
```

time: 287 us -> 218 us (0.76)
  Pallas kernels: 72.4 us -> 36.6 us
  blocking collectives: 52.6 us -> 23.4 us
  starting transfers between devices: 45.9 us -> 72.3 us
  waiting for transfers between devices: 87.6 us -> 65.3 us
  local copies, waits for them, and re-layouts: 21.1 us -> 15 us
    pallas_call x22 -> x35, Pallas kernels: 72.4 us -> 36.6 us  [call(): pl.pallas_call(body, out_shape=[jax.ShapeDtypeStruct(s, d) for s, d in ou...]
    all_to_all x2, blocking collectives: 52.6 us -> 23.4 us  [exchange(): return lax.all_to_all(value, BOTH, 0, 0, axis_index_groups=PLANES)]
    ppermute x23 -> x44, starting transfers between devices: 21 us -> 50 us  [move(): return lax.ppermute(value, BOTH, pairs(fn))]
    ppermute x23 -> x44, waiting for transfers between devices: 48.9 us -> 34.2 us  [move(): return lax.ppermute(value, BOTH, pairs(fn))]
    all_to_all x5, waiting for transfers between devices: 38.7 us -> 26.3 us  [the longest x4 23.8 us: exchange(): return lax.all_to_all(value, BOTH, 0, 0, axis_index_groups=PLANES)]
    all_to_all x5, starting transfers between devices: 24.9 us -> 18.4 us  [the longest x4 14.9 us: exchange(): return lax.all_to_all(value, BOTH, 0, 0, axis_index_groups=PLANES)]
    ppermute x0 -> x3, waiting for transfers between devices: none -> 4.79 us  [move_some(): lax.ppermute(value, BOTH, [(i, j) for i, j in pairs(fn) if (i // 64, i //...]
    squeeze x1 -> x0, local copies, waits for them, and re-layouts: 4.75 us -> none  [on_device(): send_w = lax.dynamic_index_in_dim(w5, 1 - c, axis=2, keepdims=False)]
  transfers between devices with their start and end apart: 28 -> 52, of which waited for: 16 -> 28; matrix products, arithmetic and copies ran while one was open for 3% -> 2% of each run, Pallas kernels for 18% -> 12%
where the time goes in v2:
time: 218 us; the launch traced here: 216 us
  starting transfers between devices  72.3 us (33%)
  waiting for transfers between devices  65.3 us (30%)
  Pallas kernels  36.6 us (17%)
  blocking collectives  23.4 us (11%)
  local copies, waits for them, and re-layouts  15 us (7%)
  other arithmetic  2.3 us (1%)
    ppermute x44, starting transfers between devices, move(): return lax.ppermute(value, BOTH, pairs(fn))  50 us
    pallas_call x35, Pallas kernels, call(): pl.pallas_call(body, out_shape=[jax.ShapeDtypeStruct(s, d) for s, d in ou...  36.6 us
    ppermute x44, waiting for transfers between devices, move(): return lax.ppermute(value, BOTH, pairs(fn))  34.2 us
    all_to_all x4, waiting for transfers between devices, exchange(): return lax.all_to_all(value, BOTH, 0, 0, axis_index_groups=PLANES)  23.8 us
    all_to_all x2, blocking collectives, exchange(): return lax.all_to_all(value, BOTH, 0, 0, axis_index_groups=PLANES)  23.4 us
    all_to_all x4, starting transfers between devices, exchange(): return lax.all_to_all(value, BOTH, 0, 0, axis_index_groups=PLANES)  14.9 us
    unnamed x92, local copies, waits for them, and re-layouts  11.1 us
    ppermute x3, waiting for transfers between devices, move_some(): lax.ppermute(value, BOTH, [(i, j) for i, j in pairs(fn) if (i // 64, i //...  4.79 us
  transfers between devices with their start and end apart: 52, of which 28 were waited for; matrix products, arithmetic and copies ran while one was open for 2% of the time, Pallas kernels for 12%

profile of v2, /device:TPU:0, one launch (start us, length us, event | category | flops | bytes accessed | tf_op | source)
XLA Modules:
  0.0 216.4 jit_solution(18244703717796414219)
XLA Ops:
  4.6 3.4 %copy-done.2 = bf16[2,1,8192,256]{3,2,1,0:T(8,128)(2,1)S(1)} copy-done((bf16[2,1,8192,256]{3,2,1,0:T(8,128)(2,1)S(1)}, bf16[2,1,8192,256]{3,2,1,0:T(8,128)(2,1)}, u32[]{:S(2)}) %copy-start.2) | copy-done | bytes 8388632
  9.2 13.2 %all_to_all.35.refs_0_.refs_4_ = bf16[8,144,128]{2,1,0:T(8,128)(2,1)S(1)} all-to-all(bf16[8,144,128]{2,1,0:T(8,128)(2,1)S(1)} %get-tuple-element.48), channel_id=1, replica_groups={{0,1,2,3,16,17,18,19},{4,5,6,7,20,21,22,23},{8,9,10,11,24,25,26,27},{12..., dimensions={0} | all-to-all | bytes 589824 | tf_op jit(solution)/shard_map/all_to_all | solution.py:447
  22.4 1.6 collective-permute-start.1
  23.9 1.7 collective-permute-start.2
  25.6 2.0 collective-permute-start.3
  27.6 3.4 %shard_map.70.refs_0_ = bf16[24,32,128,256]{3,2,1,0:T(8,128)(2,1)} custom-call(bf16[2,32,128,256]{3,2,1,0:T(8,128)(2,1)S(1)} %get-tuple-element.50.refs_0_, bf16[2,32,128,256]{3,2,1,0:T(8,128)(2,1)S(1)} %collective-permute-done.5.refs_1_), custom_call_target="tpu_custom_call" | custom-call | tf_op jit(solution)/shard_map/pallas_call | solution.py:404
  31.0 1.6 shard_map.72.refs_1_
  32.6 1.6 shard_map.71.refs_4_
  39.4 3.4 %all-to-all-start.1 = ((bf16[8,144,128]{2,1,0:T(8,128)(2,1)}), bf16[8,144,128]{2,1,0:T(8,128)(2,1)S(1)}, u32[]{:S(2)}, u32[]{:S(2)}) async-start(bf16[8,144,128]{2,1,0:T(8,128)(2,1)} %get-tuple-element.58.refs_1_), calls=%async_computation.1 | async-start | bytes 589824 | tf_op jit(solution)/shard_map/all_to_all | solution.py:447
  42.8 2.6 %collective-permute-start.12 = (bf16[8,128,128]{2,1,0:T(8,128)(2,1)S(1)}, bf16[8,128,128]{2,1,0:T(8,128)(2,1)S(1)}, u32[]{:S(2)}, u32[]{:S(2)}) collective-permute-start(bf16[8,128,128]{2,1,0:T(8,128)(2,1)S(1)} %get-tuple-element.54.refs_7_), channel_id=1, source_target_pairs={{0,12},{1,13},{2,14},{3,15},{4,0},{5,1},{6,2},{7,3},{8,4},{9,5},{1... | collective-permute-start | bytes 786440 | tf_op jit(solution)/shard_map/ppermute | solution.py:37
  45.8 5.3 %all-to-all-done.1.refs_0_.refs_8_ = bf16[8,144,128]{2,1,0:T(8,128)(2,1)S(1)} async-done(((bf16[8,144,128]{2,1,0:T(8,128)(2,1)}), bf16[8,144,128]{2,1,0:T(8,128)(2,1)S(1)}, u32[]{:S(2)}, u32[]{:S(2)}) %all-to-all-start.1) | async-done | bytes 294944 | tf_op jit(solution)/shard_map/all_to_all | solution.py:447
  51.2 3.1 %collective-permute-start.8 = (bf16[8,144,128]{2,1,0:T(8,128)(2,1)S(1)}, bf16[8,144,128]{2,1,0:T(8,128)(2,1)S(1)}, u32[]{:S(2)}, u32[]{:S(2)}) collective-permute-start(bf16[8,144,128]{2,1,0:T(8,128)(2,1)S(1)} %all-to-all-done.1.refs_0_.refs_8_), channel_id=1, source_target_pairs={{0,12},{1,13},{2,14},{3,15},{4,0},{5,1},{6,2},{7,3},{8,4},{9,5},{1... | collective-permute-start | bytes 884744 | tf_op jit(solution)/shard_map/ppermute | solution.py:37
  55.8 4.0 %all-to-all-start.2 = ((bf16[8,128,128]{2,1,0:T(8,128)(2,1)}), bf16[8,128,128]{2,1,0:T(8,128)(2,1)S(1)}, u32[]{:S(2)}, u32[]{:S(2)}) async-start(bf16[8,128,128]{2,1,0:T(8,128)(2,1)} %shard_map.78), calls=%async_computation.2 | async-start | bytes 524288 | tf_op jit(solution)/shard_map/all_to_all | solution.py:447
  59.8 1.6 shard_map.76.refs_4_
  61.4 1.7 collective-permute-done.8.refs_2_.refs_10_
  64.1 3.0 %all-to-all-done.2.refs_0_ = bf16[8,128,128]{2,1,0:T(8,128)(2,1)S(1)} async-done(((bf16[8,128,128]{2,1,0:T(8,128)(2,1)}), bf16[8,128,128]{2,1,0:T(8,128)(2,1)S(1)}, u32[]{:S(2)}, u32[]{:S(2)}) %all-to-all-start.2) | async-done | bytes 262176 | tf_op jit(solution)/shard_map/all_to_all | solution.py:447
  68.0 3.5 %collective-permute-start.14 = (bf16[128,128]{1,0:T(8,128)(2,1)S(1)}, bf16[128,128]{1,0:T(8,128)(2,1)S(1)}, u32[]{:S(2)}, u32[]{:S(2)}) collective-permute-start(bf16[128,128]{1,0:T(8,128)(2,1)S(1)} %get-tuple-element.62), channel_id=1, source_target_pairs={{0,64},{1,65},{2,66},{3,67},{4,68},{5,69},{6,70},{7,71},{8,72},{9,... | collective-permute-start | bytes 98312 | tf_op jit(solution)/shard_map/ppermute | solution.py:37
  71.5 1.9 collective-permute-done.14.refs_0_.refs_2_.refs_4_
  73.5 10.2 %all_to_all.36.refs_0_.refs_12_ = bf16[8,144,128]{2,1,0:T(8,128)(2,1)S(1)} all-to-all(bf16[8,144,128]{2,1,0:T(8,128)(2,1)S(1)} %get-tuple-element.63.refs_1_), channel_id=1, replica_groups={{0,1,2,3,16,17,18,19},{4,5,6,7,20,21,22,23},{8,9,10,11,24,25,26,27},{12..., dimensions={0} | all-to-all | bytes 589824 | tf_op jit(solution)/shard_map/all_to_all | solution.py:447
  84.7 2.3 %collective-permute-start.16 = (bf16[8,144,128]{2,1,0:T(8,128)(2,1)S(1)}, bf16[8,144,128]{2,1,0:T(8,128)(2,1)S(1)}, u32[]{:S(2)}, u32[]{:S(2)}) collective-permute-start(bf16[8,144,128]{2,1,0:T(8,128)(2,1)S(1)} %all_to_all.36.refs_0_.refs_12_), channel_id=1, source_target_pairs={{0,12},{1,13},{2,14},{3,15},{4,0},{5,1},{6,2},{7,3},{8,4},{9,5},{1... | collective-permute-start | bytes 884744 | tf_op jit(solution)/shard_map/ppermute | solution.py:37
  88.0 3.5 %collective-permute-start.18 = (bf16[128,128]{1,0:T(8,128)(2,1)S(1)}, bf16[128,128]{1,0:T(8,128)(2,1)S(1)}, u32[]{:S(2)}, u32[]{:S(2)}) collective-permute-start(bf16[128,128]{1,0:T(8,128)(2,1)S(1)} %broadcast_select_fusion.3), channel_id=1, source_target_pairs={{0,64},{1,65},{2,66},{3,67},{4,68},{5,69},{6,70},{7,71},{8,72},{9,... | collective-permute-start | bytes 98312 | tf_op jit(solution)/shard_map/ppermute | solution.py:37
  91.6 1.6 shard_map.82.refs_4_
  98.3 3.6 %collective-permute-start.20 = (bf16[128,128]{1,0:T(8,128)(2,1)S(1)}, bf16[128,128]{1,0:T(8,128)(2,1)S(1)}, u32[]{:S(2)}, u32[]{:S(2)}) collective-permute-start(bf16[128,128]{1,0:T(8,128)(2,1)S(1)} %shard_map.85), channel_id=1, source_target_pairs={{0,64},{1,65},{2,66},{3,67},{4,68},{5,69},{6,70},{7,71},{8,72},{9,... | collective-permute-start | bytes 98312 | tf_op jit(solution)/shard_map/ppermute | solution.py:37
  101.9 3.5 %all-to-all-start.4 = ((f32[16,8,128]{2,1,0:T(8,128)}), f32[16,8,128]{2,1,0:T(8,128)S(1)}, u32[]{:S(2)}, u32[]{:S(2)}) async-start(f32[16,8,128]{2,1,0:T(8,128)} %get-tuple-element.71), calls=%async_computation.4 | async-start | bytes 131072 | tf_op jit(solution)/shard_map/all_to_all | solution.py:561
  105.4 1.9 collective-permute-start.21
  107.4 1.6 shard_map.87.refs_8_.refs_3_
  109.0 2.4 %all-to-all-done.4.refs_0_ = f32[16,8,128]{2,1,0:T(8,128)S(1)} async-done(((f32[16,8,128]{2,1,0:T(8,128)}), f32[16,8,128]{2,1,0:T(8,128)S(1)}, u32[]{:S(2)}, u32[]{:S(2)}) %all-to-all-start.4) | async-done | bytes 65568 | tf_op jit(solution)/shard_map/all_to_all | solution.py:561
  111.5 1.5 collective-permute-start.25
  113.0 1.8 collective-permute-start.26
  116.6 3.3 %collective-permute-done.27.refs_3_ = f32[8,128]{1,0:T(8,128)S(1)} collective-permute-done((f32[8,128]{1,0:T(8,128)S(1)}, f32[8,128]{1,0:T(8,128)S(1)}, u32[]{:S(2)}, u32[]{:S(2)}) %collective-permute-start.27) | collective-permute-done | bytes 4128 | tf_op jit(solution)/shard_map/ppermute | solution.py:37
  122.5 3.0 %collective-permute-start.30 = (bf16[8,144,128]{2,1,0:T(8,128)(2,1)S(1)}, bf16[8,144,128]{2,1,0:T(8,128)(2,1)S(1)}, u32[]{:S(2)}, u32[]{:S(2)}) collective-permute-start(bf16[8,144,128]{2,1,0:T(8,128)(2,1)S(1)} %get-tuple-element.77), channel_id=1, source_target_pairs={{0,12},{1,13},{2,14},{3,15},{4,0},{5,1},{6,2},{7,3},{8,4},{9,5},{1... | collective-permute-start | bytes 884744 | tf_op jit(solution)/shard_map/ppermute | solution.py:37
  126.1 2.7 %collective-permute-start.23 = (bf16[2,3,128,128]{3,2,1,0:T(8,128)(2,1)S(1)}, bf16[2,3,128,128]{3,2,1,0:T(8,128)(2,1)S(1)}, u32[]{:S(2)}, u32[]{:S(2)}) collective-permute-start(bf16[2,3,128,128]{3,2,1,0:T(8,128)(2,1)S(1)} %pad_maximum_fusion.refs_9_.refs_0_), channel_id=1, source_target_pairs={{0,3},{1,0},{2,1},{3,2},{4,7},{5,4},{6,5},{7,6},{8,11},{9,8},{10,9... | collective-permute-start | bytes 589832 | tf_op jit(solution)/shard_map/ppermute | solution.py:37
  128.8 3.1 %collective-permute-done.29.refs_1_ = bf16[8,144,128]{2,1,0:T(8,128)(2,1)S(1)} collective-permute-done((bf16[8,144,128]{2,1,0:T(8,128)(2,1)S(1)}, bf16[8,144,128]{2,1,0:T(8,128)(2,1)S(1)}, u32[]{:S(2)}, u32[]{:S(2)}) %collective-permute-start.29) | collective-permute-done | bytes 294944 | tf_op jit(solution)/shard_map/ppermute | solution.py:37
  131.9 4.5 %collective-permute-done.30.refs_2_ = bf16[8,144,128]{2,1,0:T(8,128)(2,1)S(1)} collective-permute-done((bf16[8,144,128]{2,1,0:T(8,128)(2,1)S(1)}, bf16[8,144,128]{2,1,0:T(8,128)(2,1)S(1)}, u32[]{:S(2)}, u32[]{:S(2)}) %collective-permute-start.30) | collective-permute-done | bytes 294944 | tf_op jit(solution)/shard_map/ppermute | solution.py:37
  137.3 1.7 collective-permute-done.24.refs_3_
  139.2 3.2 %collective-permute-start.33 = (bf16[8,3,128,128]{3,2,1,0:T(8,128)(2,1)S(1)}, bf16[8,3,128,128]{3,2,1,0:T(8,128)(2,1)}, u32[]{:S(2)}, u32[]{:S(2)}) collective-permute-start(bf16[8,3,128,128]{3,2,1,0:T(8,128)(2,1)S(1)} %shard_map.91.refs_6_.refs_0_), channel_id=1, source_target_pairs={{0,12},{1,13},{2,14},{3,15},{4,0},{5,1},{6,2},{7,3},{8,4},{9,5},{1... | collective-permute-start | bytes 2359304 | tf_op jit(solution)/shard_map/ppermute | solution.py:37
  142.8 4.1 %all-to-all-start.5 = ((bf16[8,144,128]{2,1,0:T(8,128)(2,1)}), bf16[8,144,128]{2,1,0:T(8,128)(2,1)}, u32[]{:S(2)}, u32[]{:S(2)}) async-start(bf16[8,144,128]{2,1,0:T(8,128)(2,1)} %shard_map.90.refs_4_.refs_1_), calls=%async_computation.5 | async-start | bytes 589824 | tf_op jit(solution)/shard_map/all_to_all | solution.py:447
  146.8 1.6 shard_map.92.refs_5_.refs_3_
  148.4 12.0 %all-to-all-done.5.refs_0_ = bf16[8,144,128]{2,1,0:T(8,128)(2,1)} async-done(((bf16[8,144,128]{2,1,0:T(8,128)(2,1)}), bf16[8,144,128]{2,1,0:T(8,128)(2,1)}, u32[]{:S(2)}, u32[]{:S(2)}) %all-to-all-start.5) | async-done | bytes 294944 | tf_op jit(solution)/shard_map/all_to_all | solution.py:447
  162.7 5.4 %collective-permute-done.35.refs_0_ = bf16[128,128]{1,0:T(8,128)(2,1)S(1)} collective-permute-done((bf16[128,128]{1,0:T(8,128)(2,1)S(1)}, bf16[128,128]{1,0:T(8,128)(2,1)S(1)}, u32[]{:S(2)}, u32[]{:S(2)}) %collective-permute-start.35) | collective-permute-done | bytes 32800 | tf_op jit(solution)/shard_map/ppermute | solution.py:37
  169.5 1.7 shard_map.95
  172.0 4.0 %shard_map.96 = (bf16[32,128,128]{2,1,0:T(8,128)(2,1)S(1)}, bf16[32,128,256]{2,1,0:T(8,128)(2,1)S(1)}, bf16[32,128,256]{2,1,0:T(8,128)(2,1)}) custom-call(bf16[8,3,128,128]{3,2,1,0:T(8,128)(2,1)S(1)} %shard_map.91.refs_6_.refs_0_, bf16[8,3,128,128]{3,2,1,0:T(8,128)(2,1)} %collective-permute-done.32.refs_1_, ...), custom_call_target="tpu_custom_call" | custom-call | tf_op jit(solution)/shard_map/pallas_call | solution.py:404
  178.2 2.6 %collective-permute-start.40 = (bf16[8,144,128]{2,1,0:T(8,128)(2,1)}, bf16[8,144,128]{2,1,0:T(8,128)(2,1)S(1)}, u32[]{:S(2)}, u32[]{:S(2)}) collective-permute-start(bf16[8,144,128]{2,1,0:T(8,128)(2,1)} %get-tuple-element.88), channel_id=1, source_target_pairs={{0,12},{1,13},{2,14},{3,15},{4,0},{5,1},{6,2},{7,3},{8,4},{9,5},{1... | collective-permute-start | bytes 884744 | tf_op jit(solution)/shard_map/ppermute | solution.py:37
  183.5 1.6 shard_map.97.refs_1_
  190.9 3.4 %all-to-all-start.6 = ((bf16[8,144,128]{2,1,0:T(8,128)(2,1)}), bf16[8,144,128]{2,1,0:T(8,128)(2,1)S(1)}, u32[]{:S(2)}, u32[]{:S(2)}) async-start(bf16[8,144,128]{2,1,0:T(8,128)(2,1)} %shard_map.99), calls=%async_computation.6 | async-start | bytes 589824 | tf_op jit(solution)/shard_map/all_to_all | solution.py:447
  198.3 3.5 %all-to-all-done.6.refs_0_ = bf16[8,144,128]{2,1,0:T(8,128)(2,1)S(1)} async-done(((bf16[8,144,128]{2,1,0:T(8,128)(2,1)}), bf16[8,144,128]{2,1,0:T(8,128)(2,1)S(1)}, u32[]{:S(2)}, u32[]{:S(2)}) %all-to-all-start.6) | async-done | bytes 294944 | tf_op jit(solution)/shard_map/all_to_all | solution.py:447
  207.4 4.0 %collective-permute-done.43.refs_6_ = bf16[128,128]{1,0:T(8,128)(2,1)S(1)} collective-permute-done((bf16[128,128]{1,0:T(8,128)(2,1)S(1)}, bf16[128,128]{1,0:T(8,128)(2,1)S(1)}, u32[]{:S(2)}, u32[]{:S(2)}) %collective-permute-start.43) | collective-permute-done | bytes 32800 | tf_op jit(solution)/shard_map/ppermute | solution.py:41
  212.2 4.0 %shard_map.101 = bf16[32,2,128,256]{3,2,1,0:T(8,128)(2,1)} custom-call(bf16[32,128,256]{2,1,0:T(8,128)(2,1)S(1)} %copy-done.6, bf16[32,128,256]{2,1,0:T(8,128)(2,1)} %collective-permute-done.37.refs_1_, bf16[128,256]{1,0:T(8,128)(2,1)S(1)} %get-tuple-element.95.refs_7_.refs_2_, bf16[128,256]{1,0:T(8,128)(2,1)S(1)} %collective-permute-done.38.refs_3_, ...), custom_call_target="tpu_custom_call" | custom-call | flops 1073741824 | bytes 8388608 | tf_op jit(solution)/shard_map/pallas_call | solution.py:404
  (202 shorter events, 52.9 us)
Async XLA Ops:
  8.9 18.7 %collective-permute-start.5 = (bf16[2,32,128,256]{3,2,1,0:T(8,128)(2,1)S(1)}, bf16[2,32,128,256]{3,2,1,0:T(8,128)(2,1)S(1)}, u32[]{:S(2)}, u32[]{:S(2)}) collective-permute-start(bf16[2,32,128,256]{3,2,1,0:T(8,128)(2,1)S(1)} %get-tuple-element.51), channel_id=1, source_target_pairs={{0,32},{1,33},{2,34},{3,35},{4,36},{5,37},{6,38},{7,39},{8,40},{9,... | collective-permute-start | bytes 12582920 | tf_op jit(solution)/shard_map/ppermute | solution.py:37
  22.4 13.3 %collective-permute-start.1 = (bf16[8,144,128]{2,1,0:T(8,128)(2,1)S(1)}, bf16[8,144,128]{2,1,0:T(8,128)(2,1)S(1)}, u32[]{:S(2)}, u32[]{:S(2)}) collective-permute-start(bf16[8,144,128]{2,1,0:T(8,128)(2,1)S(1)} %all_to_all.35.refs_0_.refs_4_), channel_id=1, source_target_pairs={{0,4},{1,5},{2,6},{3,7},{4,8},{5,9},{6,10},{7,11},{8,12},{9,13},{1... | collective-permute-start | bytes 884744 | tf_op jit(solution)/shard_map/ppermute | solution.py:37
  23.9 11.8 %collective-permute-start.2 = (bf16[8,144,128]{2,1,0:T(8,128)(2,1)S(1)}, bf16[8,144,128]{2,1,0:T(8,128)(2,1)S(1)}, u32[]{:S(2)}, u32[]{:S(2)}) collective-permute-start(bf16[8,144,128]{2,1,0:T(8,128)(2,1)S(1)} %all_to_all.35.refs_0_.refs_4_), channel_id=1, source_target_pairs={{0,12},{1,13},{2,14},{3,15},{4,0},{5,1},{6,2},{7,3},{8,4},{9,5},{1... | collective-permute-start | bytes 884744 | tf_op jit(solution)/shard_map/ppermute | solution.py:37
  25.6 10.1 %collective-permute-start.3 = (bf16[8,144,128]{2,1,0:T(8,128)(2,1)S(1)}, bf16[8,144,128]{2,1,0:T(8,128)(2,1)S(1)}, u32[]{:S(2)}, u32[]{:S(2)}) collective-permute-start(bf16[8,144,128]{2,1,0:T(8,128)(2,1)S(1)} %all_to_all.35.refs_0_.refs_4_), channel_id=1, source_target_pairs={{0,8},{1,9},{2,10},{3,11},{4,12},{5,13},{6,14},{7,15},{8,0},{9,1},... | collective-permute-start | bytes 884744 | tf_op jit(solution)/shard_map/ppermute | solution.py:37
  34.9 19.4 %collective-permute-start.11 = (bf16[8,128,128]{2,1,0:T(8,128)(2,1)S(1)}, bf16[8,128,128]{2,1,0:T(8,128)(2,1)S(1)}, u32[]{:S(2)}, u32[]{:S(2)}) collective-permute-start(bf16[8,128,128]{2,1,0:T(8,128)(2,1)S(1)} %get-tuple-element.53.refs_6_), channel_id=1, source_target_pairs={{0,4},{1,5},{2,6},{3,7},{4,8},{5,9},{6,10},{7,11},{8,12},{9,13},{1... | collective-permute-start | bytes 786440 | tf_op jit(solution)/shard_map/ppermute | solution.py:37
  39.4 11.7 %all-to-all-start.1 = ((bf16[8,144,128]{2,1,0:T(8,128)(2,1)}), bf16[8,144,128]{2,1,0:T(8,128)(2,1)S(1)}, u32[]{:S(2)}, u32[]{:S(2)}) async-start(bf16[8,144,128]{2,1,0:T(8,128)(2,1)} %get-tuple-element.58.refs_1_), calls=%async_computation.1 | async-start | bytes 589824 | tf_op jit(solution)/shard_map/all_to_all | solution.py:447
  42.8 12.2 %collective-permute-start.12 = (bf16[8,128,128]{2,1,0:T(8,128)(2,1)S(1)}, bf16[8,128,128]{2,1,0:T(8,128)(2,1)S(1)}, u32[]{:S(2)}, u32[]{:S(2)}) collective-permute-start(bf16[8,128,128]{2,1,0:T(8,128)(2,1)S(1)} %get-tuple-element.54.refs_7_), channel_id=1, source_target_pairs={{0,12},{1,13},{2,14},{3,15},{4,0},{5,1},{6,2},{7,3},{8,4},{9,5},{1... | collective-permute-start | bytes 786440 | tf_op jit(solution)/shard_map/ppermute | solution.py:37
  45.4 9.6 %collective-permute-start.13 = (bf16[8,128,128]{2,1,0:T(8,128)(2,1)S(1)}, bf16[8,128,128]{2,1,0:T(8,128)(2,1)S(1)}, u32[]{:S(2)}, u32[]{:S(2)}) collective-permute-start(bf16[8,128,128]{2,1,0:T(8,128)(2,1)S(1)} %get-tuple-element.55.refs_8_), channel_id=1, source_target_pairs={{0,8},{1,9},{2,10},{3,11},{4,12},{5,13},{6,14},{7,15},{8,0},{9,1},... | collective-permute-start | bytes 786440 | tf_op jit(solution)/shard_map/ppermute | solution.py:37
  51.1 10.3 %collective-permute-start.7 = (bf16[8,144,128]{2,1,0:T(8,128)(2,1)S(1)}, bf16[8,144,128]{2,1,0:T(8,128)(2,1)S(1)}, u32[]{:S(2)}, u32[]{:S(2)}) collective-permute-start(bf16[8,144,128]{2,1,0:T(8,128)(2,1)S(1)} %all-to-all-done.1.refs_0_.refs_8_), channel_id=1, source_target_pairs={{0,4},{1,5},{2,6},{3,7},{4,8},{5,9},{6,10},{7,11},{8,12},{9,13},{1... | collective-permute-start | bytes 884744 | tf_op jit(solution)/shard_map/ppermute | solution.py:37
  51.2 11.9 %collective-permute-start.8 = (bf16[8,144,128]{2,1,0:T(8,128)(2,1)S(1)}, bf16[8,144,128]{2,1,0:T(8,128)(2,1)S(1)}, u32[]{:S(2)}, u32[]{:S(2)}) collective-permute-start(bf16[8,144,128]{2,1,0:T(8,128)(2,1)S(1)} %all-to-all-done.1.refs_0_.refs_8_), channel_id=1, source_target_pairs={{0,12},{1,13},{2,14},{3,15},{4,0},{5,1},{6,2},{7,3},{8,4},{9,5},{1... | collective-permute-start | bytes 884744 | tf_op jit(solution)/shard_map/ppermute | solution.py:37
  54.3 9.2 %collective-permute-start.9 = (bf16[8,144,128]{2,1,0:T(8,128)(2,1)S(1)}, bf16[8,144,128]{2,1,0:T(8,128)(2,1)S(1)}, u32[]{:S(2)}, u32[]{:S(2)}) collective-permute-start(bf16[8,144,128]{2,1,0:T(8,128)(2,1)S(1)} %all-to-all-done.1.refs_0_.refs_8_), channel_id=1, source_target_pairs={{0,8},{1,9},{2,10},{3,11},{4,12},{5,13},{6,14},{7,15},{8,0},{9,1},... | collective-permute-start | bytes 884744 | tf_op jit(solution)/shard_map/ppermute | solution.py:37
  55.8 11.3 %all-to-all-start.2 = ((bf16[8,128,128]{2,1,0:T(8,128)(2,1)}), bf16[8,128,128]{2,1,0:T(8,128)(2,1)S(1)}, u32[]{:S(2)}, u32[]{:S(2)}) async-start(bf16[8,128,128]{2,1,0:T(8,128)(2,1)} %shard_map.78), calls=%async_computation.2 | async-start | bytes 524288 | tf_op jit(solution)/shard_map/all_to_all | solution.py:447
  64.0 3.2 %collective-permute-start.10 = (f32[136,128]{1,0:T(8,128)S(1)}, f32[136,128]{1,0:T(8,128)S(1)}, u32[]{:S(2)}, u32[]{:S(2)}) collective-permute-start(f32[136,128]{1,0:T(8,128)S(1)} %get-tuple-element.60), channel_id=1, source_target_pairs={{0,32},{1,33},{2,34},{3,35},{4,36},{5,37},{6,38},{7,39},{8,40},{9,... | collective-permute-start | bytes 208904 | tf_op jit(solution)/shard_map/ppermute | solution.py:37
  68.0 5.4 %collective-permute-start.14 = (bf16[128,128]{1,0:T(8,128)(2,1)S(1)}, bf16[128,128]{1,0:T(8,128)(2,1)S(1)}, u32[]{:S(2)}, u32[]{:S(2)}) collective-permute-start(bf16[128,128]{1,0:T(8,128)(2,1)S(1)} %get-tuple-element.62), channel_id=1, source_target_pairs={{0,64},{1,65},{2,66},{3,67},{4,68},{5,69},{6,70},{7,71},{8,72},{9,... | collective-permute-start | bytes 98312 | tf_op jit(solution)/shard_map/ppermute | solution.py:37
  83.7 9.8 %collective-permute-start.15 = (bf16[8,144,128]{2,1,0:T(8,128)(2,1)S(1)}, bf16[8,144,128]{2,1,0:T(8,128)(2,1)S(1)}, u32[]{:S(2)}, u32[]{:S(2)}) collective-permute-start(bf16[8,144,128]{2,1,0:T(8,128)(2,1)S(1)} %all_to_all.36.refs_0_.refs_12_), channel_id=1, source_target_pairs={{0,4},{1,5},{2,6},{3,7},{4,8},{5,9},{6,10},{7,11},{8,12},{9,13},{1... | collective-permute-start | bytes 884744 | tf_op jit(solution)/shard_map/ppermute | solution.py:37
  84.7 9.8 %collective-permute-start.16 = (bf16[8,144,128]{2,1,0:T(8,128)(2,1)S(1)}, bf16[8,144,128]{2,1,0:T(8,128)(2,1)S(1)}, u32[]{:S(2)}, u32[]{:S(2)}) collective-permute-start(bf16[8,144,128]{2,1,0:T(8,128)(2,1)S(1)} %all_to_all.36.refs_0_.refs_12_), channel_id=1, source_target_pairs={{0,12},{1,13},{2,14},{3,15},{4,0},{5,1},{6,2},{7,3},{8,4},{9,5},{1... | collective-permute-start | bytes 884744 | tf_op jit(solution)/shard_map/ppermute | solution.py:37
  87.0 8.6 %collective-permute-start.17 = (bf16[8,144,128]{2,1,0:T(8,128)(2,1)S(1)}, bf16[8,144,128]{2,1,0:T(8,128)(2,1)S(1)}, u32[]{:S(2)}, u32[]{:S(2)}) collective-permute-start(bf16[8,144,128]{2,1,0:T(8,128)(2,1)S(1)} %all_to_all.36.refs_0_.refs_12_), channel_id=1, source_target_pairs={{0,8},{1,9},{2,10},{3,11},{4,12},{5,13},{6,14},{7,15},{8,0},{9,1},... | collective-permute-start | bytes 884744 | tf_op jit(solution)/shard_map/ppermute | solution.py:37
  88.0 5.4 %collective-permute-start.18 = (bf16[128,128]{1,0:T(8,128)(2,1)S(1)}, bf16[128,128]{1,0:T(8,128)(2,1)S(1)}, u32[]{:S(2)}, u32[]{:S(2)}) collective-permute-start(bf16[128,128]{1,0:T(8,128)(2,1)S(1)} %broadcast_select_fusion.3), channel_id=1, source_target_pairs={{0,64},{1,65},{2,66},{3,67},{4,68},{5,69},{6,70},{7,71},{8,72},{9,... | collective-permute-start | bytes 98312 | tf_op jit(solution)/shard_map/ppermute | solution.py:37
  96.1 1.3 collective-permute-start.19
  98.3 7.1 %collective-permute-start.20 = (bf16[128,128]{1,0:T(8,128)(2,1)S(1)}, bf16[128,128]{1,0:T(8,128)(2,1)S(1)}, u32[]{:S(2)}, u32[]{:S(2)}) collective-permute-start(bf16[128,128]{1,0:T(8,128)(2,1)S(1)} %shard_map.85), channel_id=1, source_target_pairs={{0,64},{1,65},{2,66},{3,67},{4,68},{5,69},{6,70},{7,71},{8,72},{9,... | collective-permute-start | bytes 98312 | tf_op jit(solution)/shard_map/ppermute | solution.py:37
  101.9 9.6 %all-to-all-start.4 = ((f32[16,8,128]{2,1,0:T(8,128)}), f32[16,8,128]{2,1,0:T(8,128)S(1)}, u32[]{:S(2)}, u32[]{:S(2)}) async-start(f32[16,8,128]{2,1,0:T(8,128)} %get-tuple-element.71), calls=%async_computation.4 | async-start | bytes 131072 | tf_op jit(solution)/shard_map/all_to_all | solution.py:561
  105.4 10.1 %collective-permute-start.21 = (bf16[3,128,128]{2,1,0:T(8,128)(2,1)S(1)}, bf16[3,128,128]{2,1,0:T(8,128)(2,1)S(1)}, u32[]{:S(2)}, u32[]{:S(2)}) collective-permute-start(bf16[3,128,128]{2,1,0:T(8,128)(2,1)S(1)} %get-tuple-element.97), channel_id=1, source_target_pairs={{0,16},{1,17},{2,18},{3,19},{4,20},{5,21},{6,22},{7,23},{8,24},{9,... | collective-permute-start | bytes 294920 | tf_op jit(solution)/shard_map/ppermute | solution.py:37
  111.5 4.9 %collective-permute-start.25 = (f32[8,128]{1,0:T(8,128)S(1)}, f32[8,128]{1,0:T(8,128)S(1)}, u32[]{:S(2)}, u32[]{:S(2)}) collective-permute-start(f32[8,128]{1,0:T(8,128)S(1)} %shard_map.86.refs_0_), channel_id=1, source_target_pairs={{0,4},{1,5},{2,6},{3,7},{4,8},{5,9},{6,10},{7,11},{8,12},{9,13},{1... | collective-permute-start | bytes 12296 | tf_op jit(solution)/shard_map/ppermute | solution.py:37
  113.0 3.6 %collective-permute-start.26 = (f32[8,128]{1,0:T(8,128)S(1)}, f32[8,128]{1,0:T(8,128)S(1)}, u32[]{:S(2)}, u32[]{:S(2)}) collective-permute-start(f32[8,128]{1,0:T(8,128)S(1)} %shard_map.86.refs_0_), channel_id=1, source_target_pairs={{0,12},{1,13},{2,14},{3,15},{4,0},{5,1},{6,2},{7,3},{8,4},{9,5},{1... | collective-permute-start | bytes 12296 | tf_op jit(solution)/shard_map/ppermute | solution.py:37
  114.8 5.1 %collective-permute-start.27 = (f32[8,128]{1,0:T(8,128)S(1)}, f32[8,128]{1,0:T(8,128)S(1)}, u32[]{:S(2)}, u32[]{:S(2)}) collective-permute-start(f32[8,128]{1,0:T(8,128)S(1)} %shard_map.86.refs_0_), channel_id=1, source_target_pairs={{0,8},{1,9},{2,10},{3,11},{4,12},{5,13},{6,14},{7,15},{8,0},{9,1},... | collective-permute-start | bytes 12296 | tf_op jit(solution)/shard_map/ppermute | solution.py:37
  120.1 1.3 collective-permute-start.28
  122.2 9.7 %collective-permute-start.29 = (bf16[8,144,128]{2,1,0:T(8,128)(2,1)S(1)}, bf16[8,144,128]{2,1,0:T(8,128)(2,1)S(1)}, u32[]{:S(2)}, u32[]{:S(2)}) collective-permute-start(bf16[8,144,128]{2,1,0:T(8,128)(2,1)S(1)} %get-tuple-element.76), channel_id=1, source_target_pairs={{0,4},{1,5},{2,6},{3,7},{4,8},{5,9},{6,10},{7,11},{8,12},{9,13},{1... | collective-permute-start | bytes 884744 | tf_op jit(solution)/shard_map/ppermute | solution.py:37
  122.5 13.9 %collective-permute-start.30 = (bf16[8,144,128]{2,1,0:T(8,128)(2,1)S(1)}, bf16[8,144,128]{2,1,0:T(8,128)(2,1)S(1)}, u32[]{:S(2)}, u32[]{:S(2)}) collective-permute-start(bf16[8,144,128]{2,1,0:T(8,128)(2,1)S(1)} %get-tuple-element.77), channel_id=1, source_target_pairs={{0,12},{1,13},{2,14},{3,15},{4,0},{5,1},{6,2},{7,3},{8,4},{9,5},{1... | collective-permute-start | bytes 884744 | tf_op jit(solution)/shard_map/ppermute | solution.py:37
  125.5 10.9 %collective-permute-start.31 = (bf16[8,144,128]{2,1,0:T(8,128)(2,1)S(1)}, bf16[8,144,128]{2,1,0:T(8,128)(2,1)S(1)}, u32[]{:S(2)}, u32[]{:S(2)}) collective-permute-start(bf16[8,144,128]{2,1,0:T(8,128)(2,1)S(1)} %get-tuple-element.78), channel_id=1, source_target_pairs={{0,8},{1,9},{2,10},{3,11},{4,12},{5,13},{6,14},{7,15},{8,0},{9,1},... | collective-permute-start | bytes 884744 | tf_op jit(solution)/shard_map/ppermute | solution.py:37
  125.5 11.8 %collective-permute-start.22 = (bf16[2,3,128,128]{3,2,1,0:T(8,128)(2,1)S(1)}, bf16[2,3,128,128]{3,2,1,0:T(8,128)(2,1)S(1)}, u32[]{:S(2)}, u32[]{:S(2)}) collective-permute-start(bf16[2,3,128,128]{3,2,1,0:T(8,128)(2,1)S(1)} %pad_maximum_fusion.refs_9_.refs_0_), channel_id=1, source_target_pairs={{0,1},{1,2},{2,3},{3,0},{4,5},{5,6},{6,7},{7,4},{8,9},{9,10},{10,1... | collective-permute-start | bytes 589832 | tf_op jit(solution)/shard_map/ppermute | solution.py:37
  126.1 11.2 %collective-permute-start.23 = (bf16[2,3,128,128]{3,2,1,0:T(8,128)(2,1)S(1)}, bf16[2,3,128,128]{3,2,1,0:T(8,128)(2,1)S(1)}, u32[]{:S(2)}, u32[]{:S(2)}) collective-permute-start(bf16[2,3,128,128]{3,2,1,0:T(8,128)(2,1)S(1)} %pad_maximum_fusion.refs_9_.refs_0_), channel_id=1, source_target_pairs={{0,3},{1,0},{2,1},{3,2},{4,7},{5,4},{6,5},{7,6},{8,11},{9,8},{10,9... | collective-permute-start | bytes 589832 | tf_op jit(solution)/shard_map/ppermute | solution.py:37
  131.9 7.2 %collective-permute-start.24 = (bf16[2,3,128,128]{3,2,1,0:T(8,128)(2,1)S(1)}, bf16[2,3,128,128]{3,2,1,0:T(8,128)(2,1)S(1)}, u32[]{:S(2)}, u32[]{:S(2)}) collective-permute-start(bf16[2,3,128,128]{3,2,1,0:T(8,128)(2,1)S(1)} %pad_maximum_fusion.refs_9_.refs_0_), channel_id=1, source_target_pairs={{0,2},{1,3},{2,0},{3,1},{4,6},{5,7},{6,4},{7,5},{8,10},{9,11},{10,... | collective-permute-start | bytes 589832 | tf_op jit(solution)/shard_map/ppermute | solution.py:37
  139.1 32.8 %collective-permute-start.32 = (bf16[8,3,128,128]{3,2,1,0:T(8,128)(2,1)S(1)}, bf16[8,3,128,128]{3,2,1,0:T(8,128)(2,1)}, u32[]{:S(2)}, u32[]{:S(2)}) collective-permute-start(bf16[8,3,128,128]{3,2,1,0:T(8,128)(2,1)S(1)} %shard_map.91.refs_6_.refs_0_), channel_id=1, source_target_pairs={{0,4},{1,5},{2,6},{3,7},{4,8},{5,9},{6,10},{7,11},{8,12},{9,13},{1... | collective-permute-start | bytes 2359304 | tf_op jit(solution)/shard_map/ppermute | solution.py:37
  139.2 32.7 %collective-permute-start.33 = (bf16[8,3,128,128]{3,2,1,0:T(8,128)(2,1)S(1)}, bf16[8,3,128,128]{3,2,1,0:T(8,128)(2,1)}, u32[]{:S(2)}, u32[]{:S(2)}) collective-permute-start(bf16[8,3,128,128]{3,2,1,0:T(8,128)(2,1)S(1)} %shard_map.91.refs_6_.refs_0_), channel_id=1, source_target_pairs={{0,12},{1,13},{2,14},{3,15},{4,0},{5,1},{6,2},{7,3},{8,4},{9,5},{1... | collective-permute-start | bytes 2359304 | tf_op jit(solution)/shard_map/ppermute | solution.py:37
  142.4 29.5 %collective-permute-start.34 = (bf16[8,3,128,128]{3,2,1,0:T(8,128)(2,1)S(1)}, bf16[8,3,128,128]{3,2,1,0:T(8,128)(2,1)}, u32[]{:S(2)}, u32[]{:S(2)}) collective-permute-start(bf16[8,3,128,128]{3,2,1,0:T(8,128)(2,1)S(1)} %shard_map.91.refs_6_.refs_0_), channel_id=1, source_target_pairs={{0,8},{1,9},{2,10},{3,11},{4,12},{5,13},{6,14},{7,15},{8,0},{9,1},... | collective-permute-start | bytes 2359304 | tf_op jit(solution)/shard_map/ppermute | solution.py:37
  142.8 17.7 %all-to-all-start.5 = ((bf16[8,144,128]{2,1,0:T(8,128)(2,1)}), bf16[8,144,128]{2,1,0:T(8,128)(2,1)}, u32[]{:S(2)}, u32[]{:S(2)}) async-start(bf16[8,144,128]{2,1,0:T(8,128)(2,1)} %shard_map.90.refs_4_.refs_1_), calls=%async_computation.5 | async-start | bytes 589824 | tf_op jit(solution)/shard_map/all_to_all | solution.py:447
  162.6 5.5 %collective-permute-start.35 = (bf16[128,128]{1,0:T(8,128)(2,1)S(1)}, bf16[128,128]{1,0:T(8,128)(2,1)S(1)}, u32[]{:S(2)}, u32[]{:S(2)}) collective-permute-start(bf16[128,128]{1,0:T(8,128)(2,1)S(1)} %shard_map.93), channel_id=1, source_target_pairs={{0,64},{1,65},{2,66},{3,67},{4,68},{5,69},{6,70},{7,71},{8,72},{9,... | collective-permute-start | bytes 98312 | tf_op jit(solution)/shard_map/ppermute | solution.py:37
  177.4 34.8 %collective-permute-start.37 = (bf16[32,128,256]{2,1,0:T(8,128)(2,1)}, bf16[32,128,256]{2,1,0:T(8,128)(2,1)}, u32[]{:S(2)}, u32[]{:S(2)}) collective-permute-start(bf16[32,128,256]{2,1,0:T(8,128)(2,1)} %get-tuple-element.83), channel_id=1, source_target_pairs={{0,32},{1,33},{2,34},{3,35},{4,36},{5,37},{6,38},{7,39},{8,40},{9,... | collective-permute-start | bytes 6291464 | tf_op jit(solution)/shard_map/ppermute | solution.py:37
  177.5 10.6 %collective-permute-start.39 = (bf16[8,144,128]{2,1,0:T(8,128)(2,1)}, bf16[8,144,128]{2,1,0:T(8,128)(2,1)S(1)}, u32[]{:S(2)}, u32[]{:S(2)}) collective-permute-start(bf16[8,144,128]{2,1,0:T(8,128)(2,1)} %get-tuple-element.87), channel_id=1, source_target_pairs={{0,4},{1,5},{2,6},{3,7},{4,8},{5,9},{6,10},{7,11},{8,12},{9,13},{1... | collective-permute-start | bytes 884744 | tf_op jit(solution)/shard_map/ppermute | solution.py:37
  178.2 10.3 %collective-permute-start.40 = (bf16[8,144,128]{2,1,0:T(8,128)(2,1)}, bf16[8,144,128]{2,1,0:T(8,128)(2,1)S(1)}, u32[]{:S(2)}, u32[]{:S(2)}) collective-permute-start(bf16[8,144,128]{2,1,0:T(8,128)(2,1)} %get-tuple-element.88), channel_id=1, source_target_pairs={{0,12},{1,13},{2,14},{3,15},{4,0},{5,1},{6,2},{7,3},{8,4},{9,5},{1... | collective-permute-start | bytes 884744 | tf_op jit(solution)/shard_map/ppermute | solution.py:37
  180.8 9.2 %collective-permute-start.41 = (bf16[8,144,128]{2,1,0:T(8,128)(2,1)}, bf16[8,144,128]{2,1,0:T(8,128)(2,1)S(1)}, u32[]{:S(2)}, u32[]{:S(2)}) collective-permute-start(bf16[8,144,128]{2,1,0:T(8,128)(2,1)} %get-tuple-element.89), channel_id=1, source_target_pairs={{0,8},{1,9},{2,10},{3,11},{4,12},{5,13},{6,14},{7,15},{8,0},{9,1},... | collective-permute-start | bytes 884744 | tf_op jit(solution)/shard_map/ppermute | solution.py:37
  186.8 7.6 %collective-permute-start.45 = (f32[128,128]{1,0:T(8,128)}, f32[128,128]{1,0:T(8,128)}, u32[]{:S(2)}, u32[]{:S(2)}) collective-permute-start(f32[128,128]{1,0:T(8,128)} %get-tuple-element.91.refs_4_), channel_id=1, source_target_pairs={{0,32},{1,33},{2,34},{3,35},{4,36},{5,37},{6,38},{7,39},{8,40},{9,... | collective-permute-start | bytes 196616 | tf_op jit(solution)/shard_map/ppermute | solution.py:37
  190.9 10.9 %all-to-all-start.6 = ((bf16[8,144,128]{2,1,0:T(8,128)(2,1)}), bf16[8,144,128]{2,1,0:T(8,128)(2,1)S(1)}, u32[]{:S(2)}, u32[]{:S(2)}) async-start(bf16[8,144,128]{2,1,0:T(8,128)(2,1)} %shard_map.99), calls=%async_computation.6 | async-start | bytes 589824 | tf_op jit(solution)/shard_map/all_to_all | solution.py:447
  196.8 8.6 %collective-permute-start.46 = (bf16[128,128]{1,0:T(8,128)(2,1)S(1)}, bf16[128,128]{1,0:T(8,128)(2,1)S(1)}, u32[]{:S(2)}, u32[]{:S(2)}) collective-permute-start(bf16[128,128]{1,0:T(8,128)(2,1)S(1)} %get-tuple-element.99), channel_id=1, source_target_pairs={{0,32},{1,33},{2,34},{3,35},{4,36},{5,37},{6,38},{7,39},{8,40},{9,... | collective-permute-start | bytes 98312 | tf_op jit(solution)/shard_map/ppermute | solution.py:37
  197.9 9.5 %collective-permute-start.38 = (bf16[128,256]{1,0:T(8,128)(2,1)S(1)}, bf16[128,256]{1,0:T(8,128)(2,1)S(1)}, u32[]{:S(2)}, u32[]{:S(2)}) collective-permute-start(bf16[128,256]{1,0:T(8,128)(2,1)S(1)} %get-tuple-element.94), channel_id=1, source_target_pairs={{0,64},{1,65},{2,66},{3,67},{4,68},{5,69},{6,70},{7,71},{8,72},{9,... | collective-permute-start | bytes 196616 | tf_op jit(solution)/shard_map/ppermute | solution.py:37
  202.8 4.6 %collective-permute-start.42 = (bf16[128,128]{1,0:T(8,128)(2,1)S(1)}, bf16[128,128]{1,0:T(8,128)(2,1)S(1)}, u32[]{:S(2)}, u32[]{:S(2)}) collective-permute-start(bf16[128,128]{1,0:T(8,128)(2,1)S(1)} %shard_map.100.refs_4_), channel_id=1, source_target_pairs={{32,0},{33,1},{34,2},{35,3},{36,4},{37,5},{38,6},{39,7},{40,8},{41... | collective-permute-start | bytes 98312 | tf_op jit(solution)/shard_map/ppermute | solution.py:41
  204.1 7.3 %collective-permute-start.43 = (bf16[128,128]{1,0:T(8,128)(2,1)S(1)}, bf16[128,128]{1,0:T(8,128)(2,1)S(1)}, u32[]{:S(2)}, u32[]{:S(2)}) collective-permute-start(bf16[128,128]{1,0:T(8,128)(2,1)S(1)} %shard_map.100.refs_4_), channel_id=1, source_target_pairs={{64,0},{65,1},{66,2},{67,3},{68,4},{69,5},{70,6},{71,7},{72,8},{73... | collective-permute-start | bytes 98312 | tf_op jit(solution)/shard_map/ppermute | solution.py:41
  205.5 6.7 %collective-permute-start.44 = (bf16[128,128]{1,0:T(8,128)(2,1)S(1)}, bf16[128,128]{1,0:T(8,128)(2,1)S(1)}, u32[]{:S(2)}, u32[]{:S(2)}) collective-permute-start(bf16[128,128]{1,0:T(8,128)(2,1)S(1)} %shard_map.100.refs_4_), channel_id=1, source_target_pairs={{96,0},{97,1},{98,2},{99,3},{100,4},{101,5},{102,6},{103,7},{104,8... | collective-permute-start | bytes 98312 | tf_op jit(solution)/shard_map/ppermute | solution.py:41
  (50 other events, 438.5 us)

commit v3 on v2

--- a/solution.py
+++ b/solution.py
@@ -49,10 +49,6 @@
     return (1 - zh, c, zl, y, x)
 
 
-def other_both(zh, c, zl, y, x):
-    return (1 - zh, 1 - c, zl, y, x)
-
-
 def other_zl(zh, c, zl, y, x):
     return (zh, c, 1 - zl, y, x)
 
@@ -77,8 +73,9 @@
     return p // 2, p % 2
 
 
-def block_index(sign):
+def block_index(sign, other=False):
     _, c = place()
+    c = 1 - c if other else c
     dp = lax.axis_index("dp")
     y, x = (dp // 4) % 4, dp % 4
     b = jnp.where(c == 0, y, x)
@@ -194,12 +191,13 @@
     send_ref[M : M + 8, :] = sums
 
 
-def last_forward_kernel(f_ref, w_ref, keep_ref, send_ref):
+def last_forward_kernel(v0, v1, v2, v3, w_ref, keep_ref, send_ref):
     _, c = place()
+    index = step_index()
     total = jnp.zeros((M, 2 * H), F32)
-    for ch in range(4):
-        f = jnp.concatenate([f_ref[8 * ch + j] for j in range(8)], axis=1)
-        w = w_ref[8 * ch : 8 * ch + 8].reshape(8 * 128, 2 * H)
+    for ib, ref in enumerate((v0, v1, v2, v3)):
+        f = jnp.concatenate([ref[at, 0] for at in range(8)], axis=1)
+        w = jnp.concatenate([w_ref[index(ib, at // 2, at % 2)] for at in range(8)], axis=0)
         total = total + jnp.dot(f, w, preferred_element_type=F32)
     first = c == 0
     keep_ref[...] = jnp.where(first, total[:, :H], total[:, H:])
@@ -242,25 +240,36 @@
         sums_ref[j] = sums
 
 
-def last_combine_kernel(keep_ref, recv_ref, x_ref, s_ref, next_ref):
+def last_combine_kernel(keep_ref, recv_ref, x_ref, s_ref, shown_ref, send_ref):
+    zh, c = place()
     p = keep_ref[...] + recv_ref[...]
-    next_ref[...] = (x_ref[...].astype(F32) + to_cols(s_ref[0:1, :]) * p).astype(BF16)
+    x = x_ref[...]
+    new = (x.astype(F32) + to_cols(s_ref[0:1, :]) * p).astype(BF16)
+    shown_ref[...] = jnp.where((zh ^ c) == 0, new, x)
+    send_ref[...] = jnp.where((zh ^ c) == 0, x, new)
 
 
 def turned(left, right):
     return jnp.concatenate([jnp.transpose(left), jnp.transpose(right)], axis=0)
 
 
-def backward_kernel(mine_ref, theirs_ref, s_ref, w_ref, o0, o1, o2, o3, gs_ref):
-    _, c = place()
+def backward_kernel(mine_ref, theirs_ref, s_ref, w_ref, *refs):
+    extra_refs = refs[:-5] if len(refs) == 5 else refs[:2]
+    o0, o1, o2, o3 = refs[len(extra_refs) : len(extra_refs) + 4]
+    zh, c = place()
     first = c == 0
     a = mine_ref[0:M, :]
     b = theirs_ref[0:M, :]
     left = jnp.where(first, a, b)
     right = jnp.where(first, b, a)
     scale = to_cols(s_ref[0:1, :])
-    gs_ref[:, :H] = (left.astype(F32) * scale).astype(BF16)
-    gs_ref[:, H:] = (right.astype(F32) * scale).astype(BF16)
+    scaled = jnp.concatenate([left.astype(F32) * scale, right.astype(F32) * scale], axis=1).astype(BF16)
+    if extra_refs:
+        high = jnp.where(first, extra_refs[0][...], extra_refs[1][...])
+        refs[-2][...] = jnp.where(zh == 0, scaled, high)
+        refs[-1][...] = jnp.where(zh == 0, high, scaled)
+    else:
+        refs[-1][...] = scaled
     extra = extra_rows(read_extra(mine_ref[M:R, :]) + read_extra(theirs_ref[M:R, :]))
     gt = turned(left, right)
     index = block_index(1)
@@ -311,12 +320,16 @@
     out[...] = jnp.sum(r[...], axis=0)
 
 
-def last_grad_kernel(s0, s1, s2, s3, g_ref, gn_ref, x_ref, p_ref, out_ref, s_ref):
+def last_grad_kernel(s0, s1, s2, s3, cot_ref, gn_ref, x_ref, p_ref, out_ref, s_ref, gs_ref):
     total = s0[...] + s1[...] + s2[...] + s3[...]
     scale = lax.rsqrt(total[0:1, :] / D + EPS)
     s_ref[...] = jnp.broadcast_to(scale, (8, M))
     mix = scale * scale * scale * total[1:2, :] / D
-    g = g_ref[...].astype(F32) + to_cols(scale) * gn_ref[...] - to_cols(mix) * x_ref[...].astype(F32)
+    _, c = place()
+    column = to_cols(scale)
+    left, right = cot_ref[:, :H].astype(F32), cot_ref[:, H:].astype(F32)
+    gs_ref[...] = jnp.concatenate([left * column, right * column], axis=1).astype(BF16)
+    g = jnp.where(c == 0, left, right) + column * gn_ref[...] - to_cols(mix) * x_ref[...].astype(F32)
     g = g.astype(BF16)
     out_ref[0:M, :] = g
     out_ref[M:R, :] = extra_rows(to_rows(g.astype(F32) * p_ref[...]))
@@ -343,56 +356,52 @@
 
 def order_kernel(*refs):
     v, g0, g1, g2 = refs[0:4], refs[4:8], refs[8:12], refs[12:16]
-    f3_ref, keep_ref, send_ref = refs[16:]
+    keep, send = refs[16:20], refs[20:24]
     zh, c = place()
-    index = step_index()
-    other = block_index(-1)
-
-    def fill(first, second, q0_ref, q1_ref):
+    dp = lax.axis_index("dp")
+    zl, y, x = dp // 16, (dp // 4) % 4, dp % 4
+    a = jnp.where(c == 0, x, y)
+
+    def at(ia, iz):
+        return (zl if iz == 0 else 1 - zl) * 4 + lax.rem(a + 4 - SHIFTS[ia], 4)
+
+    def fill(first, second, q0, q1):
         for ib in range(4):
+            for i in range(8):
+                q0[ib][i, :, :M] = jnp.transpose(first[ib][i, 0:M, :])
+                if second is not None:
+                    q1[ib][i, :, :M] = jnp.transpose(second[ib][i, 0:M, :])
             for ia in range(4):
                 for iz in range(2):
-                    j = index(ib, ia, iz)
-                    at = ia * 2 + iz
-                    last = v[ib][at, 0]
-                    f3_ref[j] = last
-                    q0_ref[j, :, M:] = v[ib][at, 1]
-                    q1_ref[j, :, M:] = v[ib][at, 2]
+                    i = at(ia, iz)
+                    q0[ib][i, :, M:] = v[ib][ia * 2 + iz, 1]
+                    q1[ib][i, :, M:] = v[ib][ia * 2 + iz, 2]
                     if second is None:
-                        q1_ref[j, :, :M] = jnp.transpose(last)
-            for i in range(8):
-                j = other(ib, i)
-                q0_ref[j, :, :M] = jnp.transpose(first[ib][i, 0:M, :])
-                if second is not None:
-                    q1_ref[j, :, :M] = jnp.transpose(second[ib][i, 0:M, :])
-
-    for a in range(2):
-        for b in range(2):
-            q0, q1 = (keep_ref, send_ref) if b == 0 else (send_ref, keep_ref)
-            first, second = (g0, g1) if a == 0 else (g2, None)
-            pl.when(jnp.logical_and(zh == a, c == b))(functools.partial(fill, first, second, q0, q1))
-
-
-def weight_grad_kernel(
-    keep_ref, recv_ref, local_ref, far_ref, mine_ref, core_ref, far0_ref, far1_ref, factor_ref, out_ref, buf, sem
-):
+                        q1[ib][i, :, :M] = jnp.transpose(v[ib][ia * 2 + iz, 0])
+
+    for half in range(2):
+        for core in range(2):
+            q0, q1 = (keep, send) if core == 0 else (send, keep)
+            first, second = (g0, g1) if half == 0 else (g2, None)
+            pl.when(jnp.logical_and(zh == half, c == core))(functools.partial(fill, first, second, q0, q1))
+
+
+def weight_grad_kernel(*refs):
+    keep, recv = refs[0:4], refs[4:8]
+    local_ref, far_ref, late_ref, far_late_ref, factor_ref, out_ref, buf, sem = refs[8:]
     zh, c = place()
     late = (zh + c) == 0
-    local = jnp.where(late, jnp.concatenate([mine_ref[...], core_ref[...]], axis=1), local_ref[...])
-    far = jnp.where(late, jnp.concatenate([far0_ref[...], far1_ref[...]], axis=1), far_ref[...])
+    local = jnp.where(late, late_ref[...], local_ref[...])
+    far = jnp.where(late, far_late_ref[...], far_ref[...])
     g = jnp.concatenate([local, far], axis=0)
-    count = 4
-    copies = []
-    for i in range(N // count):
-        part = pl.ds(i * count, count)
-        for ref, which in ((keep_ref, c), (recv_ref, 1 - c)):
-            value = jnp.dot(ref[part].reshape(count * H, 2 * M), g, preferred_element_type=F32)
-            value = value.reshape(count, H, 2 * H) * factor_ref[part, which]
-            buf[part, which] = value.astype(BF16)
-        copies.append(pltpu.make_async_copy(buf.at[part], out_ref.at[part], sem.at[i]))
-        copies[-1].start()
-    for copy in copies:
-        copy.wait()
+    for features, which, index in ((keep, c, block_index(-1)), (recv, 1 - c, block_index(-1, True))):
+        for ib, ref in enumerate(features):
+            value = jnp.dot(ref[...].reshape(8 * H, 2 * M), g, preferred_element_type=F32).reshape(8, H, 2 * H)
+            for i in range(8):
+                j = index(ib, i)
+                buf[j, which] = (value[i] * factor_ref[j, which]).astype(BF16)
+                pltpu.make_async_copy(buf.at[j, which], out_ref.at[j, which], sem).start()
+    pltpu.make_async_copy(buf, out_ref, sem).wait()
 
 
 def call(kernel, out, specs, args, scratch=(), flops=0, bytes_accessed=0, limit=4, out_specs=None, deps=()):
@@ -556,30 +565,30 @@
         [VM] * 5,
         (keep, recv, x2, gain[3], gn3),
     )
-    (send3,) = call(choose_kernel, [(block, BF16)], [VM] * 2, (ft3, ft1), deps=(x3,))
+    (sums,) = call(add_kernel, [((8, M), F32)], [VM], (lax.all_to_all(spread, BOTH, 0, 0, axis_index_groups=CORES),))
+    (send3,) = call(choose_kernel, [(block, BF16)], [VM] * 2, (ft3, ft1), deps=(sums,))
     mirror1 = move(send3, other_zh)
-    (sums,) = call(add_kernel, [((8, M), F32)], [VM], (lax.all_to_all(spread, BOTH, 0, 0, axis_index_groups=CORES),), deps=(mirror1,))
     first_rows = gather_z(jnp.stack([f3, mirror0, mirror1]))
     w2 = load(2, x3)
     sums = [sums] + [move(sums, along_y(k)) for k in SHIFTS[1:]]
 
-    g3 = half(cot, c)
-    mine2, s3 = call(
+    mine2, s3, gs3 = call(
         last_grad_kernel,
-        [((R, H), BF16), ((8, M), F32)],
+        [((R, H), BF16), ((8, M), F32), ((M, 2 * H), BF16)],
         [VM] * 8,
-        (*sums, g3, gn3, x3, p2),
-        deps=(w2, first_rows),
-    )
-
-    def backward(weight, mine, s):
+        (*sums, cot, gn3, x3, p2),
+        deps=(w2, mirror1),
+    )
+
+    def backward(weight, mine, s, *deps, extra=()):
         theirs = move(mine, other_core)
-        *parts, gs = call(
-            backward_kernel, [wide] * 4 + [((M, 2 * H), BF16)], [VM] * 4, (mine, theirs, s, weight), **MATMUL
-        )
-        return parts, gs
+        outs = [wide] * 4 + [((M, 2 * H), BF16)] * (2 if extra else 1)
+        args = (mine, theirs, s, weight, *extra)
+        *parts, last = call(backward_kernel, outs, [VM] * len(args), args, deps=deps, **MATMUL)
+        return (parts[:4], *parts[4:], last)
 
     parts2, gs2 = backward(w2, mine2, s2)
+    factor = jnp.repeat(jnp.exp2(-exponents[0].astype(F32)), H, axis=1).reshape(N, 2, 1, 2 * H)
     got2, row2 = scatter(parts2)
     w1 = load(1, row2)
     joined = gather_first(first_rows, row2)
@@ -589,51 +598,39 @@
         [(block, BF16)],
         [VM] * 5,
         (got2, gain[2], mine2, s2, x2),
-        deps=(w1, joined),
-    )
-    back1 = move(back1, other_zh)
-    (mine1,) = call(dots_kernel, [((R, H), BF16)], [VM] * 2, (back1, p1))
-    parts1, gs1 = backward(w1, mine1, s1)
-
-    f3_all, keep_t, send_t = call(
-        order_kernel,
-        [((N, M, H), BF16), ((N, H, 2 * M), BF16), ((N, H, 2 * M), BF16)],
-        [VM] * 16,
-        (*v, *g0, *g1, *g2),
-        limit=14,
-        deps=(gs1,),
-    )
-    recv_t = move(send_t, other_core)
-    keep, send = call(last_forward_kernel, [(block, F32)] * 2, [VM] * 2, (f3_all, load(3, gs1)), **MATMUL)
-    got1, row1 = scatter(parts1, send)
+        deps=(w1,),
+    )
+    moved1 = move(back1, other_zh)
+    (mine1,) = call(dots_kernel, [((R, H), BF16)], [VM] * 2, (moved1, p1), deps=(factor,))
+    parts1, local, far = backward(w1, mine1, s1, extra=(gs2, gs3))
+    gs1 = local
+    keep, send = call(last_forward_kernel, [(block, F32)] * 2, [VM] * 5, (*v, load(3, gs1)), deps=(gs1,), **MATMUL)
+    got1, _ = scatter(parts1, keep)
+    far = move(far, other_zh)
+    turned_features = call(
+        order_kernel, [((8, H, 2 * M), BF16)] * 8, [VM] * 16, (*v, *g0, *g1, *g2), limit=14, deps=(gs1,)
+    )
+    kept, received = turned_features[:4], [move(t, other_core) for t in turned_features[4:]]
+
     recv = move(send, other_core)
-    (x4,) = call(last_combine_kernel, [(block, BF16)], [VM] * 4, (keep, recv, x3, s3))
-    is_first = e == 0
-    shown = jnp.where(is_first, x4, x3)
-    got = move(jnp.where(is_first, x3, x4), other_core)
+    shown, got = call(last_combine_kernel, [(block, BF16)] * 2, [VM] * 4, (keep, recv, x3, s3))
+    got = move(got, other_core)
     last = jnp.where(c == 0, jnp.concatenate([shown, got], 1), jnp.concatenate([got, shown], 1))
 
-    gs3 = (cot.astype(F32) * s3[0][:, None]).astype(BF16)
-    high = jnp.where(c == 0, gs2, gs3)
-    local = jnp.where(zh == 0, gs1, high)
-    far = move(jnp.where(zh == 0, high, gs1), other_zh)
-    factor = jnp.repeat(jnp.exp2(-exponents[0].astype(F32)), H, axis=1).reshape(N, 2, 1, 2 * H)
     (mine0,) = call(
         grad_kernel,
         [(block, BF16)],
         [VM] * 6,
         (got1, gain[1], mine1, s1, x1, s0),
-        deps=(factor, local),
-    )
-    far0 = move_some(mine0, other_zh, [(1, 0)])
-    far1 = move_some(mine0, other_both, [(1, 1)])
-    core = move_some(mine0, other_core, [(0, 1)])
+    )
+    late = jnp.concatenate([mine0, move_some(mine0, other_core, [(0, 1), (1, 1)])], axis=1)
+    far_late = move_some(late, other_zh, [(1, 0)])
     (total,) = call(
         weight_grad_kernel,
         [((N, 2, H, 2 * H), BF16)],
-        [VM] * 9,
-        (keep_t, recv_t, local, far, mine0, core, far0, far1, factor),
-        scratch=[pltpu.VMEM((N, 2, H, 2 * H), BF16), pltpu.SemaphoreType.DMA((8,))],
+        [VM] * 13,
+        (*kept, *received, local, far, late, far_late, factor),
+        scratch=[pltpu.VMEM((N, 2, H, 2 * H), BF16), pltpu.SemaphoreType.DMA],
         out_specs=[HBM],
         flops=2 * 256 * 256 * D,
         bytes_accessed=8 << 20,

time: 218 us -> 217 us (level)
  waiting for transfers between devices: 65.3 us -> 50.7 us
  blocking collectives: 23.4 us -> 32.1 us
  starting transfers between devices: 72.3 us -> 77.3 us
    all_to_all x4, waiting for transfers between devices: 23.8 us -> 13.1 us  [exchange(): return lax.all_to_all(value, BOTH, 0, 0, axis_index_groups=PLANES)]
    all_to_all x0 -> x1, blocking collectives: none -> 8.69 us  [on_device(): lax.all_to_all(spread, BOTH, 0, 0, axis_index_groups=CORES)]
    ppermute x44 -> x47, starting transfers between devices: 50 us -> 56 us  [move(): return lax.ppermute(value, BOTH, pairs(fn))]
    all_to_all x4, starting transfers between devices: 14.9 us -> 18.8 us  [exchange(): return lax.all_to_all(value, BOTH, 0, 0, axis_index_groups=PLANES)]
    all_to_all x1 -> x0, starting transfers between devices: 3.5 us -> none  [on_device(): lax.all_to_all(spread, BOTH, 0, 0, axis_index_groups=CORES)]
    ppermute x44 -> x47, waiting for transfers between devices: 34.2 us -> 31.1 us  [move(): return lax.ppermute(value, BOTH, pairs(fn))]
    all_to_all x1 -> x0, waiting for transfers between devices: 2.45 us -> none  [on_device(): lax.all_to_all(spread, BOTH, 0, 0, axis_index_groups=CORES)]
    ppermute x3 -> x2, waiting for transfers between devices: 4.79 us -> 6.54 us  [move_some(): lax.ppermute(value, BOTH, [(i, j) for i, j in pairs(fn) if (i // 64, i //...]
  transfers between devices with their start and end apart: 52 -> 53, of which waited for: 28 -> 25; matrix products, arithmetic and copies ran while one was open for 2% -> 1% of each run, Pallas kernels for 12% -> 14%
where the time goes in v3:
time: 217 us; the launch traced here: 213 us
  starting transfers between devices  77.3 us (36%)
  waiting for transfers between devices  50.7 us (23%)
  Pallas kernels  36.4 us (17%)
  blocking collectives  32.1 us (15%)
  local copies, waits for them, and re-layouts  14 us (6%)
    ppermute x47, starting transfers between devices, move(): return lax.ppermute(value, BOTH, pairs(fn))  56 us
    pallas_call x35, Pallas kernels, call(): pl.pallas_call(body, out_shape=[jax.ShapeDtypeStruct(s, d) for s, d in ou...  36.4 us
    ppermute x47, waiting for transfers between devices, move(): return lax.ppermute(value, BOTH, pairs(fn))  31.1 us
    all_to_all x2, blocking collectives, exchange(): return lax.all_to_all(value, BOTH, 0, 0, axis_index_groups=PLANES)  23.4 us
    all_to_all x4, starting transfers between devices, exchange(): return lax.all_to_all(value, BOTH, 0, 0, axis_index_groups=PLANES)  18.8 us
    all_to_all x4, waiting for transfers between devices, exchange(): return lax.all_to_all(value, BOTH, 0, 0, axis_index_groups=PLANES)  13.1 us
    unnamed x104, local copies, waits for them, and re-layouts  12.1 us
    all_to_all x1, blocking collectives, on_device(): lax.all_to_all(spread, BOTH, 0, 0, axis_index_groups=CORES)  8.69 us
  transfers between devices with their start and end apart: 53, of which 25 were waited for; matrix products, arithmetic and copies ran while one was open for 1% of the time, Pallas kernels for 14%

profile of v3, /device:TPU:0, one launch (start us, length us, event | category | flops | bytes accessed | tf_op | source)
XLA Modules:
  0.0 213.5 jit_solution(5366680398569121970)
XLA Ops:
  4.6 3.4 %copy-done.2 = bf16[2,1,8192,256]{3,2,1,0:T(8,128)(2,1)S(1)} copy-done((bf16[2,1,8192,256]{3,2,1,0:T(8,128)(2,1)S(1)}, bf16[2,1,8192,256]{3,2,1,0:T(8,128)(2,1)}, u32[]{:S(2)}) %copy-start.2) | copy-done | bytes 8388632
  9.2 13.2 %all_to_all.35.refs_0_.refs_4_ = bf16[8,144,128]{2,1,0:T(8,128)(2,1)S(1)} all-to-all(bf16[8,144,128]{2,1,0:T(8,128)(2,1)S(1)} %get-tuple-element.57), channel_id=1, replica_groups={{0,1,2,3,16,17,18,19},{4,5,6,7,20,21,22,23},{8,9,10,11,24,25,26,27},{12..., dimensions={0} | all-to-all | bytes 589824 | tf_op jit(solution)/shard_map/all_to_all | solution.py:456
  22.4 1.6 collective-permute-start.1
  24.0 1.7 collective-permute-start.2
  25.6 2.0 collective-permute-start.3
  27.6 3.4 %shard_map.70.refs_0_ = bf16[24,32,128,256]{3,2,1,0:T(8,128)(2,1)} custom-call(bf16[2,32,128,256]{3,2,1,0:T(8,128)(2,1)S(1)} %get-tuple-element.59.refs_0_, bf16[2,32,128,256]{3,2,1,0:T(8,128)(2,1)S(1)} %collective-permute-done.5.refs_1_), custom_call_target="tpu_custom_call" | custom-call | tf_op jit(solution)/shard_map/pallas_call | solution.py:413
  31.0 1.6 shard_map.72.refs_1_
  32.6 1.6 shard_map.71.refs_4_
  39.4 3.4 %all-to-all-start.1 = ((bf16[8,144,128]{2,1,0:T(8,128)(2,1)}), bf16[8,144,128]{2,1,0:T(8,128)(2,1)S(1)}, u32[]{:S(2)}, u32[]{:S(2)}) async-start(bf16[8,144,128]{2,1,0:T(8,128)(2,1)} %get-tuple-element.67.refs_1_), calls=%async_computation.1 | async-start | bytes 589824 | tf_op jit(solution)/shard_map/all_to_all | solution.py:456
  42.9 2.6 %collective-permute-start.12 = (bf16[8,128,128]{2,1,0:T(8,128)(2,1)S(1)}, bf16[8,128,128]{2,1,0:T(8,128)(2,1)S(1)}, u32[]{:S(2)}, u32[]{:S(2)}) collective-permute-start(bf16[8,128,128]{2,1,0:T(8,128)(2,1)S(1)} %get-tuple-element.63.refs_7_), channel_id=1, source_target_pairs={{0,12},{1,13},{2,14},{3,15},{4,0},{5,1},{6,2},{7,3},{8,4},{9,5},{1... | collective-permute-start | bytes 786440 | tf_op jit(solution)/shard_map/ppermute | solution.py:37
  45.8 5.3 %all-to-all-done.1.refs_0_.refs_8_ = bf16[8,144,128]{2,1,0:T(8,128)(2,1)S(1)} async-done(((bf16[8,144,128]{2,1,0:T(8,128)(2,1)}), bf16[8,144,128]{2,1,0:T(8,128)(2,1)S(1)}, u32[]{:S(2)}, u32[]{:S(2)}) %all-to-all-start.1) | async-done | bytes 294944 | tf_op jit(solution)/shard_map/all_to_all | solution.py:456
  51.3 3.1 %collective-permute-start.8 = (bf16[8,144,128]{2,1,0:T(8,128)(2,1)S(1)}, bf16[8,144,128]{2,1,0:T(8,128)(2,1)S(1)}, u32[]{:S(2)}, u32[]{:S(2)}) collective-permute-start(bf16[8,144,128]{2,1,0:T(8,128)(2,1)S(1)} %all-to-all-done.1.refs_0_.refs_8_), channel_id=1, source_target_pairs={{0,12},{1,13},{2,14},{3,15},{4,0},{5,1},{6,2},{7,3},{8,4},{9,5},{1... | collective-permute-start | bytes 884744 | tf_op jit(solution)/shard_map/ppermute | solution.py:37
  55.1 1.8 shard_map.78
  56.8 4.1 %all-to-all-start.2 = ((bf16[8,128,128]{2,1,0:T(8,128)(2,1)}), bf16[8,128,128]{2,1,0:T(8,128)(2,1)S(1)}, u32[]{:S(2)}, u32[]{:S(2)}) async-start(bf16[8,128,128]{2,1,0:T(8,128)(2,1)} %shard_map.78), calls=%async_computation.2 | async-start | bytes 524288 | tf_op jit(solution)/shard_map/all_to_all | solution.py:456
  60.9 1.6 shard_map.76.refs_4_
  63.8 4.4 %all-to-all-done.2.refs_0_ = bf16[8,128,128]{2,1,0:T(8,128)(2,1)S(1)} async-done(((bf16[8,128,128]{2,1,0:T(8,128)(2,1)}), bf16[8,128,128]{2,1,0:T(8,128)(2,1)S(1)}, u32[]{:S(2)}, u32[]{:S(2)}) %all-to-all-start.2) | async-done | bytes 262176 | tf_op jit(solution)/shard_map/all_to_all | solution.py:456
  69.1 3.5 %collective-permute-start.14 = (bf16[128,128]{1,0:T(8,128)(2,1)S(1)}, bf16[128,128]{1,0:T(8,128)(2,1)S(1)}, u32[]{:S(2)}, u32[]{:S(2)}) collective-permute-start(bf16[128,128]{1,0:T(8,128)(2,1)S(1)} %get-tuple-element.71), channel_id=1, source_target_pairs={{0,64},{1,65},{2,66},{3,67},{4,68},{5,69},{6,70},{7,71},{8,72},{9,... | collective-permute-start | bytes 98312 | tf_op jit(solution)/shard_map/ppermute | solution.py:37
  72.6 1.9 collective-permute-done.14.refs_0_.refs_2_.refs_4_
  74.7 10.2 %all_to_all.36.refs_0_.refs_12_ = bf16[8,144,128]{2,1,0:T(8,128)(2,1)S(1)} all-to-all(bf16[8,144,128]{2,1,0:T(8,128)(2,1)S(1)} %get-tuple-element.72.refs_1_), channel_id=1, replica_groups={{0,1,2,3,16,17,18,19},{4,5,6,7,20,21,22,23},{8,9,10,11,24,25,26,27},{12..., dimensions={0} | all-to-all | bytes 589824 | tf_op jit(solution)/shard_map/all_to_all | solution.py:456
  85.7 2.4 %collective-permute-start.16 = (bf16[8,144,128]{2,1,0:T(8,128)(2,1)S(1)}, bf16[8,144,128]{2,1,0:T(8,128)(2,1)S(1)}, u32[]{:S(2)}, u32[]{:S(2)}) collective-permute-start(bf16[8,144,128]{2,1,0:T(8,128)(2,1)S(1)} %all_to_all.36.refs_0_.refs_12_), channel_id=1, source_target_pairs={{0,12},{1,13},{2,14},{3,15},{4,0},{5,1},{6,2},{7,3},{8,4},{9,5},{1... | collective-permute-start | bytes 884744 | tf_op jit(solution)/shard_map/ppermute | solution.py:37
  89.1 3.5 %collective-permute-start.18 = (bf16[128,128]{1,0:T(8,128)(2,1)S(1)}, bf16[128,128]{1,0:T(8,128)(2,1)S(1)}, u32[]{:S(2)}, u32[]{:S(2)}) collective-permute-start(bf16[128,128]{1,0:T(8,128)(2,1)S(1)} %broadcast_select_fusion), channel_id=1, source_target_pairs={{0,64},{1,65},{2,66},{3,67},{4,68},{5,69},{6,70},{7,71},{8,72},{9,... | collective-permute-start | bytes 98312 | tf_op jit(solution)/shard_map/ppermute | solution.py:37
  92.6 1.6 shard_map.82.refs_4_
  98.9 8.7 %all_to_all.37.refs_0_ = f32[16,8,128]{2,1,0:T(8,128)S(1)} all-to-all(f32[16,8,128]{2,1,0:T(8,128)S(1)} %get-tuple-element.79), channel_id=1, replica_groups={{0,1,2,3,16,17,18,19,32,33,34,35,48,49,50,51},{4,5,6,7,20,21,22,23,36,3..., dimensions={0} | all-to-all | bytes 131072 | tf_op jit(solution)/shard_map/all_to_all | solution.py:568
  107.7 3.6 %collective-permute-start.20 = (bf16[128,128]{1,0:T(8,128)(2,1)S(1)}, bf16[128,128]{1,0:T(8,128)(2,1)S(1)}, u32[]{:S(2)}, u32[]{:S(2)}) collective-permute-start(bf16[128,128]{1,0:T(8,128)(2,1)S(1)} %shard_map.86), channel_id=1, source_target_pairs={{0,64},{1,65},{2,66},{3,67},{4,68},{5,69},{6,70},{7,71},{8,72},{9,... | collective-permute-start | bytes 98312 | tf_op jit(solution)/shard_map/ppermute | solution.py:37
  111.3 1.4 collective-permute-start.25
  112.7 1.8 collective-permute-start.26
  115.1 1.6 shard_map.87.refs_8_.refs_3_
  116.8 2.8 %collective-permute-done.27.refs_3_ = f32[8,128]{1,0:T(8,128)S(1)} collective-permute-done((f32[8,128]{1,0:T(8,128)S(1)}, f32[8,128]{1,0:T(8,128)S(1)}, u32[]{:S(2)}, u32[]{:S(2)}) %collective-permute-start.27) | collective-permute-done | bytes 4128 | tf_op jit(solution)/shard_map/ppermute | solution.py:37
  123.6 3.0 %collective-permute-start.30 = (bf16[8,144,128]{2,1,0:T(8,128)(2,1)S(1)}, bf16[8,144,128]{2,1,0:T(8,128)(2,1)S(1)}, u32[]{:S(2)}, u32[]{:S(2)}) collective-permute-start(bf16[8,144,128]{2,1,0:T(8,128)(2,1)S(1)} %get-tuple-element.86), channel_id=1, source_target_pairs={{0,12},{1,13},{2,14},{3,15},{4,0},{5,1},{6,2},{7,3},{8,4},{9,5},{1... | collective-permute-start | bytes 884744 | tf_op jit(solution)/shard_map/ppermute | solution.py:37
  126.6 1.7 collective-permute-done.21
  129.2 2.5 %collective-permute-start.23 = (bf16[2,3,128,128]{3,2,1,0:T(8,128)(2,1)S(1)}, bf16[2,3,128,128]{3,2,1,0:T(8,128)(2,1)S(1)}, u32[]{:S(2)}, u32[]{:S(2)}) collective-permute-start(bf16[2,3,128,128]{3,2,1,0:T(8,128)(2,1)S(1)} %pad_maximum_fusion.refs_0_), channel_id=1, source_target_pairs={{0,3},{1,0},{2,1},{3,2},{4,7},{5,4},{6,5},{7,6},{8,11},{9,8},{10,9... | collective-permute-start | bytes 589832 | tf_op jit(solution)/shard_map/ppermute | solution.py:37
  133.8 3.5 %collective-permute-done.31.refs_3_ = bf16[8,144,128]{2,1,0:T(8,128)(2,1)S(1)} collective-permute-done((bf16[8,144,128]{2,1,0:T(8,128)(2,1)S(1)}, bf16[8,144,128]{2,1,0:T(8,128)(2,1)S(1)}, u32[]{:S(2)}, u32[]{:S(2)}) %collective-permute-start.31) | collective-permute-done | bytes 294944 | tf_op jit(solution)/shard_map/ppermute | solution.py:37
  139.2 4.5 %all-to-all-start.5 = ((bf16[8,144,128]{2,1,0:T(8,128)(2,1)}), bf16[8,144,128]{2,1,0:T(8,128)(2,1)}, u32[]{:S(2)}, u32[]{:S(2)}) async-start(bf16[8,144,128]{2,1,0:T(8,128)(2,1)} %shard_map.90.refs_4_.refs_1_), calls=%async_computation.5 | async-start | bytes 589824 | tf_op jit(solution)/shard_map/all_to_all | solution.py:456
  143.6 2.8 %collective-permute-start.33 = (bf16[8,3,128,128]{3,2,1,0:T(8,128)(2,1)S(1)}, bf16[8,3,128,128]{3,2,1,0:T(8,128)(2,1)}, u32[]{:S(2)}, u32[]{:S(2)}) collective-permute-start(bf16[8,3,128,128]{3,2,1,0:T(8,128)(2,1)S(1)} %shard_map.91.refs_0_), channel_id=1, source_target_pairs={{0,12},{1,13},{2,14},{3,15},{4,0},{5,1},{6,2},{7,3},{8,4},{9,5},{1... | collective-permute-start | bytes 2359304 | tf_op jit(solution)/shard_map/ppermute | solution.py:37
  147.3 1.6 shard_map.92.refs_5_.refs_3_
  148.9 3.3 %all-to-all-done.5.refs_0_ = bf16[8,144,128]{2,1,0:T(8,128)(2,1)} async-done(((bf16[8,144,128]{2,1,0:T(8,128)(2,1)}), bf16[8,144,128]{2,1,0:T(8,128)(2,1)}, u32[]{:S(2)}, u32[]{:S(2)}) %all-to-all-start.5) | async-done | bytes 294944 | tf_op jit(solution)/shard_map/all_to_all | solution.py:456
  152.9 1.7 shard_map.93
  154.7 1.7 collective-permute-start.35
  156.5 3.8 %collective-permute-done.35.refs_0_ = bf16[128,128]{1,0:T(8,128)(2,1)S(1)} collective-permute-done((bf16[128,128]{1,0:T(8,128)(2,1)}, bf16[128,128]{1,0:T(8,128)(2,1)S(1)}, u32[]{:S(2)}, u32[]{:S(2)}) %collective-permute-start.35) | collective-permute-done | bytes 32800 | tf_op jit(solution)/shard_map/ppermute | solution.py:37
  166.5 2.0 collective-permute-start.43
  169.8 1.7 shard_map.97.refs_4_
  172.1 4.0 %shard_map.96 = (bf16[8,128,256]{2,1,0:T(8,128)(2,1)S(1)}, bf16[8,128,256]{2,1,0:T(8,128)(2,1)S(1)}, bf16[8,128,256]{2,1,0:T(8,128)(2,1)S(1)}, bf16[8,128,256]{2...) custom-call(bf16[8,3,128,128]{3,2,1,0:T(8,128)(2,1)S(1)} %shard_map., ...), custom_call_target="tpu_custom_call" | custom-call | tf_op jit(solution)/shard_map/pallas_call | solution.py:413
  177.1 2.0 shard_map.98
  181.4 6.8 %all-to-all-start.6 = ((bf16[8,144,128]{2,1,0:T(8,128)(2,1)}), bf16[8,144,128]{2,1,0:T(8,128)(2,1)S(1)}, u32[]{:S(2)}, u32[]{:S(2)}) async-start(bf16[8,144,128]{2,1,0:T(8,128)(2,1)} %shard_map.99), calls=%async_computation.6 | async-start | bytes 589824 | tf_op jit(solution)/shard_map/all_to_all | solution.py:456
  188.2 4.2 %collective-permute-start.41 = (bf16[128,256]{1,0:T(8,128)(2,1)S(1)}, bf16[128,256]{1,0:T(8,128)(2,1)S(1)}, u32[]{:S(2)}, u32[]{:S(2)}) collective-permute-start(bf16[128,256]{1,0:T(8,128)(2,1)S(1)} %copy-done.48), channel_id=1, source_target_pairs={{0,64},{1,65},{2,66},{3,67},{4,68},{5,69},{6,70},{7,71},{8,72},{9,... | collective-permute-start | bytes 196616 | tf_op jit(solution)/shard_map/ppermute | solution.py:37
  192.4 3.9 %collective-permute-done.41.refs_9_ = bf16[128,256]{1,0:T(8,128)(2,1)S(1)} collective-permute-done((bf16[128,256]{1,0:T(8,128)(2,1)S(1)}, bf16[128,256]{1,0:T(8,128)(2,1)S(1)}, u32[]{:S(2)}, u32[]{:S(2)}) %collective-permute-start.41) | collective-permute-done | bytes 65568 | tf_op jit(solution)/shard_map/ppermute | solution.py:37
  203.9 5.7 %collective-permute-done.46.refs_11_ = bf16[128,256]{1,0:T(8,128)(2,1)S(1)} collective-permute-done((bf16[128,256]{1,0:T(8,128)(2,1)S(1)}, bf16[128,256]{1,0:T(8,128)(2,1)S(1)}, u32[]{:S(2)}, u32[]{:S(2)}) %collective-permute-start.46) | collective-permute-done | bytes 65568 | tf_op jit(solution)/shard_map/ppermute | solution.py:41
  209.6 3.7 %shard_map.101 = bf16[32,2,128,256]{3,2,1,0:T(8,128)(2,1)} custom-call(bf16[8,128,256]{2,1,0:T(8,128)(2,1)S(1)} %get-tuple-element.93.refs_0_, bf16[8,128,256]{2,1,0:T(8,128)(2,1)S(1)} %get-tuple-element.94.refs_1_, bf16[8,128,256]{2,1,0:T(8,128)(2,1)S(1)} %get-tuple-element.95.refs_2_, bf16[8,128,256]{2,1,0:T(8,128)(2,1)S(1)} %copy-done.26, ...), custom_call_target="tpu_custom_call" | custom-call | flops 1073741824 | bytes 8388608 | tf_op jit(solution)/shard_map/pallas_call | solution.py:413
  (214 shorter events, 49.9 us)
Async XLA Ops:
  3.3 1.3 collective-permute-start.4
  8.9 18.7 %collective-permute-start.5 = (bf16[2,32,128,256]{3,2,1,0:T(8,128)(2,1)S(1)}, bf16[2,32,128,256]{3,2,1,0:T(8,128)(2,1)S(1)}, u32[]{:S(2)}, u32[]{:S(2)}) collective-permute-start(bf16[2,32,128,256]{3,2,1,0:T(8,128)(2,1)S(1)} %get-tuple-element.60), channel_id=1, source_target_pairs={{0,32},{1,33},{2,34},{3,35},{4,36},{5,37},{6,38},{7,39},{8,40},{9,... | collective-permute-start | bytes 12582920 | tf_op jit(solution)/shard_map/ppermute | solution.py:37
  22.4 13.3 %collective-permute-start.1 = (bf16[8,144,128]{2,1,0:T(8,128)(2,1)S(1)}, bf16[8,144,128]{2,1,0:T(8,128)(2,1)S(1)}, u32[]{:S(2)}, u32[]{:S(2)}) collective-permute-start(bf16[8,144,128]{2,1,0:T(8,128)(2,1)S(1)} %all_to_all.35.refs_0_.refs_4_), channel_id=1, source_target_pairs={{0,4},{1,5},{2,6},{3,7},{4,8},{5,9},{6,10},{7,11},{8,12},{9,13},{1... | collective-permute-start | bytes 884744 | tf_op jit(solution)/shard_map/ppermute | solution.py:37
  24.0 11.8 %collective-permute-start.2 = (bf16[8,144,128]{2,1,0:T(8,128)(2,1)S(1)}, bf16[8,144,128]{2,1,0:T(8,128)(2,1)S(1)}, u32[]{:S(2)}, u32[]{:S(2)}) collective-permute-start(bf16[8,144,128]{2,1,0:T(8,128)(2,1)S(1)} %all_to_all.35.refs_0_.refs_4_), channel_id=1, source_target_pairs={{0,12},{1,13},{2,14},{3,15},{4,0},{5,1},{6,2},{7,3},{8,4},{9,5},{1... | collective-permute-start | bytes 884744 | tf_op jit(solution)/shard_map/ppermute | solution.py:37
  25.6 10.1 %collective-permute-start.3 = (bf16[8,144,128]{2,1,0:T(8,128)(2,1)S(1)}, bf16[8,144,128]{2,1,0:T(8,128)(2,1)S(1)}, u32[]{:S(2)}, u32[]{:S(2)}) collective-permute-start(bf16[8,144,128]{2,1,0:T(8,128)(2,1)S(1)} %all_to_all.35.refs_0_.refs_4_), channel_id=1, source_target_pairs={{0,8},{1,9},{2,10},{3,11},{4,12},{5,13},{6,14},{7,15},{8,0},{9,1},... | collective-permute-start | bytes 884744 | tf_op jit(solution)/shard_map/ppermute | solution.py:37
  35.0 19.4 %collective-permute-start.11 = (bf16[8,128,128]{2,1,0:T(8,128)(2,1)S(1)}, bf16[8,128,128]{2,1,0:T(8,128)(2,1)S(1)}, u32[]{:S(2)}, u32[]{:S(2)}) collective-permute-start(bf16[8,128,128]{2,1,0:T(8,128)(2,1)S(1)} %get-tuple-element.62.refs_6_), channel_id=1, source_target_pairs={{0,4},{1,5},{2,6},{3,7},{4,8},{5,9},{6,10},{7,11},{8,12},{9,13},{1... | collective-permute-start | bytes 786440 | tf_op jit(solution)/shard_map/ppermute | solution.py:37
  39.4 11.7 %all-to-all-start.1 = ((bf16[8,144,128]{2,1,0:T(8,128)(2,1)}), bf16[8,144,128]{2,1,0:T(8,128)(2,1)S(1)}, u32[]{:S(2)}, u32[]{:S(2)}) async-start(bf16[8,144,128]{2,1,0:T(8,128)(2,1)} %get-tuple-element.67.refs_1_), calls=%async_computation.1 | async-start | bytes 589824 | tf_op jit(solution)/shard_map/all_to_all | solution.py:456
  42.9 12.2 %collective-permute-start.12 = (bf16[8,128,128]{2,1,0:T(8,128)(2,1)S(1)}, bf16[8,128,128]{2,1,0:T(8,128)(2,1)S(1)}, u32[]{:S(2)}, u32[]{:S(2)}) collective-permute-start(bf16[8,128,128]{2,1,0:T(8,128)(2,1)S(1)} %get-tuple-element.63.refs_7_), channel_id=1, source_target_pairs={{0,12},{1,13},{2,14},{3,15},{4,0},{5,1},{6,2},{7,3},{8,4},{9,5},{1... | collective-permute-start | bytes 786440 | tf_op jit(solution)/shard_map/ppermute | solution.py:37
  45.5 9.6 %collective-permute-start.13 = (bf16[8,128,128]{2,1,0:T(8,128)(2,1)S(1)}, bf16[8,128,128]{2,1,0:T(8,128)(2,1)}, u32[]{:S(2)}, u32[]{:S(2)}) collective-permute-start(bf16[8,128,128]{2,1,0:T(8,128)(2,1)S(1)} %get-tuple-element.64.refs_8_), channel_id=1, source_target_pairs={{0,8},{1,9},{2,10},{3,11},{4,12},{5,13},{6,14},{7,15},{8,0},{9,1},... | collective-permute-start | bytes 786440 | tf_op jit(solution)/shard_map/ppermute | solution.py:37
  51.2 11.3 %collective-permute-start.7 = (bf16[8,144,128]{2,1,0:T(8,128)(2,1)S(1)}, bf16[8,144,128]{2,1,0:T(8,128)(2,1)S(1)}, u32[]{:S(2)}, u32[]{:S(2)}) collective-permute-start(bf16[8,144,128]{2,1,0:T(8,128)(2,1)S(1)} %all-to-all-done.1.refs_0_.refs_8_), channel_id=1, source_target_pairs={{0,4},{1,5},{2,6},{3,7},{4,8},{5,9},{6,10},{7,11},{8,12},{9,13},{1... | collective-permute-start | bytes 884744 | tf_op jit(solution)/shard_map/ppermute | solution.py:37
  51.3 11.9 %collective-permute-start.8 = (bf16[8,144,128]{2,1,0:T(8,128)(2,1)S(1)}, bf16[8,144,128]{2,1,0:T(8,128)(2,1)S(1)}, u32[]{:S(2)}, u32[]{:S(2)}) collective-permute-start(bf16[8,144,128]{2,1,0:T(8,128)(2,1)S(1)} %all-to-all-done.1.refs_0_.refs_8_), channel_id=1, source_target_pairs={{0,12},{1,13},{2,14},{3,15},{4,0},{5,1},{6,2},{7,3},{8,4},{9,5},{1... | collective-permute-start | bytes 884744 | tf_op jit(solution)/shard_map/ppermute | solution.py:37
  54.4 8.8 %collective-permute-start.9 = (bf16[8,144,128]{2,1,0:T(8,128)(2,1)S(1)}, bf16[8,144,128]{2,1,0:T(8,128)(2,1)S(1)}, u32[]{:S(2)}, u32[]{:S(2)}) collective-permute-start(bf16[8,144,128]{2,1,0:T(8,128)(2,1)S(1)} %all-to-all-done.1.refs_0_.refs_8_), channel_id=1, source_target_pairs={{0,8},{1,9},{2,10},{3,11},{4,12},{5,13},{6,14},{7,15},{8,0},{9,1},... | collective-permute-start | bytes 884744 | tf_op jit(solution)/shard_map/ppermute | solution.py:37
  56.8 11.4 %all-to-all-start.2 = ((bf16[8,128,128]{2,1,0:T(8,128)(2,1)}), bf16[8,128,128]{2,1,0:T(8,128)(2,1)S(1)}, u32[]{:S(2)}, u32[]{:S(2)}) async-start(bf16[8,128,128]{2,1,0:T(8,128)(2,1)} %shard_map.78), calls=%async_computation.2 | async-start | bytes 524288 | tf_op jit(solution)/shard_map/all_to_all | solution.py:456
  63.7 4.6 %collective-permute-start.10 = (f32[136,128]{1,0:T(8,128)S(1)}, f32[136,128]{1,0:T(8,128)S(1)}, u32[]{:S(2)}, u32[]{:S(2)}) collective-permute-start(f32[136,128]{1,0:T(8,128)S(1)} %get-tuple-element.69), channel_id=1, source_target_pairs={{0,32},{1,33},{2,34},{3,35},{4,36},{5,37},{6,38},{7,39},{8,40},{9,... | collective-permute-start | bytes 208904 | tf_op jit(solution)/shard_map/ppermute | solution.py:37
  69.1 5.4 %collective-permute-start.14 = (bf16[128,128]{1,0:T(8,128)(2,1)S(1)}, bf16[128,128]{1,0:T(8,128)(2,1)S(1)}, u32[]{:S(2)}, u32[]{:S(2)}) collective-permute-start(bf16[128,128]{1,0:T(8,128)(2,1)S(1)} %get-tuple-element.71), channel_id=1, source_target_pairs={{0,64},{1,65},{2,66},{3,67},{4,68},{5,69},{6,70},{7,71},{8,72},{9,... | collective-permute-start | bytes 98312 | tf_op jit(solution)/shard_map/ppermute | solution.py:37
  84.8 9.7 %collective-permute-start.15 = (bf16[8,144,128]{2,1,0:T(8,128)(2,1)S(1)}, bf16[8,144,128]{2,1,0:T(8,128)(2,1)S(1)}, u32[]{:S(2)}, u32[]{:S(2)}) collective-permute-start(bf16[8,144,128]{2,1,0:T(8,128)(2,1)S(1)} %all_to_all.36.refs_0_.refs_12_), channel_id=1, source_target_pairs={{0,4},{1,5},{2,6},{3,7},{4,8},{5,9},{6,10},{7,11},{8,12},{9,13},{1... | collective-permute-start | bytes 884744 | tf_op jit(solution)/shard_map/ppermute | solution.py:37
  85.7 9.9 %collective-permute-start.16 = (bf16[8,144,128]{2,1,0:T(8,128)(2,1)S(1)}, bf16[8,144,128]{2,1,0:T(8,128)(2,1)S(1)}, u32[]{:S(2)}, u32[]{:S(2)}) collective-permute-start(bf16[8,144,128]{2,1,0:T(8,128)(2,1)S(1)} %all_to_all.36.refs_0_.refs_12_), channel_id=1, source_target_pairs={{0,12},{1,13},{2,14},{3,15},{4,0},{5,1},{6,2},{7,3},{8,4},{9,5},{1... | collective-permute-start | bytes 884744 | tf_op jit(solution)/shard_map/ppermute | solution.py:37
  88.1 8.7 %collective-permute-start.17 = (bf16[8,144,128]{2,1,0:T(8,128)(2,1)S(1)}, bf16[8,144,128]{2,1,0:T(8,128)(2,1)S(1)}, u32[]{:S(2)}, u32[]{:S(2)}) collective-permute-start(bf16[8,144,128]{2,1,0:T(8,128)(2,1)S(1)} %all_to_all.36.refs_0_.refs_12_), channel_id=1, source_target_pairs={{0,8},{1,9},{2,10},{3,11},{4,12},{5,13},{6,14},{7,15},{8,0},{9,1},... | collective-permute-start | bytes 884744 | tf_op jit(solution)/shard_map/ppermute | solution.py:37
  89.1 5.4 %collective-permute-start.18 = (bf16[128,128]{1,0:T(8,128)(2,1)S(1)}, bf16[128,128]{1,0:T(8,128)(2,1)S(1)}, u32[]{:S(2)}, u32[]{:S(2)}) collective-permute-start(bf16[128,128]{1,0:T(8,128)(2,1)S(1)} %broadcast_select_fusion), channel_id=1, source_target_pairs={{0,64},{1,65},{2,66},{3,67},{4,68},{5,69},{6,70},{7,71},{8,72},{9,... | collective-permute-start | bytes 98312 | tf_op jit(solution)/shard_map/ppermute | solution.py:37
  97.3 1.3 collective-permute-start.19
  107.7 12.0 %collective-permute-start.20 = (bf16[128,128]{1,0:T(8,128)(2,1)S(1)}, bf16[128,128]{1,0:T(8,128)(2,1)S(1)}, u32[]{:S(2)}, u32[]{:S(2)}) collective-permute-start(bf16[128,128]{1,0:T(8,128)(2,1)S(1)} %shard_map.86), channel_id=1, source_target_pairs={{0,64},{1,65},{2,66},{3,67},{4,68},{5,69},{6,70},{7,71},{8,72},{9,... | collective-permute-start | bytes 98312 | tf_op jit(solution)/shard_map/ppermute | solution.py:37
  111.3 5.5 %collective-permute-start.25 = (f32[8,128]{1,0:T(8,128)S(1)}, f32[8,128]{1,0:T(8,128)S(1)}, u32[]{:S(2)}, u32[]{:S(2)}) collective-permute-start(f32[8,128]{1,0:T(8,128)S(1)} %shard_map.85.refs_2_.refs_0_), channel_id=1, source_target_pairs={{0,4},{1,5},{2,6},{3,7},{4,8},{5,9},{6,10},{7,11},{8,12},{9,13},{1... | collective-permute-start | bytes 12296 | tf_op jit(solution)/shard_map/ppermute | solution.py:37
  112.7 4.1 %collective-permute-start.26 = (f32[8,128]{1,0:T(8,128)S(1)}, f32[8,128]{1,0:T(8,128)S(1)}, u32[]{:S(2)}, u32[]{:S(2)}) collective-permute-start(f32[8,128]{1,0:T(8,128)S(1)} %shard_map.85.refs_2_.refs_0_), channel_id=1, source_target_pairs={{0,12},{1,13},{2,14},{3,15},{4,0},{5,1},{6,2},{7,3},{8,4},{9,5},{1... | collective-permute-start | bytes 12296 | tf_op jit(solution)/shard_map/ppermute | solution.py:37
  114.5 5.1 %collective-permute-start.27 = (f32[8,128]{1,0:T(8,128)S(1)}, f32[8,128]{1,0:T(8,128)S(1)}, u32[]{:S(2)}, u32[]{:S(2)}) collective-permute-start(f32[8,128]{1,0:T(8,128)S(1)} %shard_map.85.refs_2_.refs_0_), channel_id=1, source_target_pairs={{0,8},{1,9},{2,10},{3,11},{4,12},{5,13},{6,14},{7,15},{8,0},{9,1},... | collective-permute-start | bytes 12296 | tf_op jit(solution)/shard_map/ppermute | solution.py:37
  123.1 8.6 %collective-permute-start.29 = (bf16[8,144,128]{2,1,0:T(8,128)(2,1)S(1)}, bf16[8,144,128]{2,1,0:T(8,128)(2,1)S(1)}, u32[]{:S(2)}, u32[]{:S(2)}) collective-permute-start(bf16[8,144,128]{2,1,0:T(8,128)(2,1)S(1)} %get-tuple-element.85), channel_id=1, source_target_pairs={{0,4},{1,5},{2,6},{3,7},{4,8},{5,9},{6,10},{7,11},{8,12},{9,13},{1... | collective-permute-start | bytes 884744 | tf_op jit(solution)/shard_map/ppermute | solution.py:37
  123.3 5.0 %collective-permute-start.21 = (bf16[3,128,128]{2,1,0:T(8,128)(2,1)S(1)}, bf16[3,128,128]{2,1,0:T(8,128)(2,1)S(1)}, u32[]{:S(2)}, u32[]{:S(2)}) collective-permute-start(bf16[3,128,128]{2,1,0:T(8,128)(2,1)S(1)} %get-tuple-element.113), channel_id=1, source_target_pairs={{0,16},{1,17},{2,18},{3,19},{4,20},{5,21},{6,22},{7,23},{8,24},{9,... | collective-permute-start | bytes 294920 | tf_op jit(solution)/shard_map/ppermute | solution.py:37
  123.6 10.2 %collective-permute-start.30 = (bf16[8,144,128]{2,1,0:T(8,128)(2,1)S(1)}, bf16[8,144,128]{2,1,0:T(8,128)(2,1)S(1)}, u32[]{:S(2)}, u32[]{:S(2)}) collective-permute-start(bf16[8,144,128]{2,1,0:T(8,128)(2,1)S(1)} %get-tuple-element.86), channel_id=1, source_target_pairs={{0,12},{1,13},{2,14},{3,15},{4,0},{5,1},{6,2},{7,3},{8,4},{9,5},{1... | collective-permute-start | bytes 884744 | tf_op jit(solution)/shard_map/ppermute | solution.py:37
  126.6 10.7 %collective-permute-start.31 = (bf16[8,144,128]{2,1,0:T(8,128)(2,1)S(1)}, bf16[8,144,128]{2,1,0:T(8,128)(2,1)S(1)}, u32[]{:S(2)}, u32[]{:S(2)}) collective-permute-start(bf16[8,144,128]{2,1,0:T(8,128)(2,1)S(1)} %get-tuple-element.87), channel_id=1, source_target_pairs={{0,8},{1,9},{2,10},{3,11},{4,12},{5,13},{6,14},{7,15},{8,0},{9,1},... | collective-permute-start | bytes 884744 | tf_op jit(solution)/shard_map/ppermute | solution.py:37
  128.3 9.9 %collective-permute-start.22 = (bf16[2,3,128,128]{3,2,1,0:T(8,128)(2,1)S(1)}, bf16[2,3,128,128]{3,2,1,0:T(8,128)(2,1)S(1)}, u32[]{:S(2)}, u32[]{:S(2)}) collective-permute-start(bf16[2,3,128,128]{3,2,1,0:T(8,128)(2,1)S(1)} %pad_maximum_fusion.refs_0_), channel_id=1, source_target_pairs={{0,1},{1,2},{2,3},{3,0},{4,5},{5,6},{6,7},{7,4},{8,9},{9,10},{10,1... | collective-permute-start | bytes 589832 | tf_op jit(solution)/shard_map/ppermute | solution.py:37
  129.2 9.0 %collective-permute-start.23 = (bf16[2,3,128,128]{3,2,1,0:T(8,128)(2,1)S(1)}, bf16[2,3,128,128]{3,2,1,0:T(8,128)(2,1)S(1)}, u32[]{:S(2)}, u32[]{:S(2)}) collective-permute-start(bf16[2,3,128,128]{3,2,1,0:T(8,128)(2,1)S(1)} %pad_maximum_fusion.refs_0_), channel_id=1, source_target_pairs={{0,3},{1,0},{2,1},{3,2},{4,7},{5,4},{6,5},{7,6},{8,11},{9,8},{10,9... | collective-permute-start | bytes 589832 | tf_op jit(solution)/shard_map/ppermute | solution.py:37
  131.7 7.2 %collective-permute-start.24 = (bf16[2,3,128,128]{3,2,1,0:T(8,128)(2,1)S(1)}, bf16[2,3,128,128]{3,2,1,0:T(8,128)(2,1)S(1)}, u32[]{:S(2)}, u32[]{:S(2)}) collective-permute-start(bf16[2,3,128,128]{3,2,1,0:T(8,128)(2,1)S(1)} %pad_maximum_fusion.refs_0_), channel_id=1, source_target_pairs={{0,2},{1,3},{2,0},{3,1},{4,6},{5,7},{6,4},{7,5},{8,10},{9,11},{10,... | collective-permute-start | bytes 589832 | tf_op jit(solution)/shard_map/ppermute | solution.py:37
  138.9 29.6 %collective-permute-start.32 = (bf16[8,3,128,128]{3,2,1,0:T(8,128)(2,1)S(1)}, bf16[8,3,128,128]{3,2,1,0:T(8,128)(2,1)}, u32[]{:S(2)}, u32[]{:S(2)}) collective-permute-start(bf16[8,3,128,128]{3,2,1,0:T(8,128)(2,1)S(1)} %shard_map.91.refs_0_), channel_id=1, source_target_pairs={{0,4},{1,5},{2,6},{3,7},{4,8},{5,9},{6,10},{7,11},{8,12},{9,13},{1... | collective-permute-start | bytes 2359304 | tf_op jit(solution)/shard_map/ppermute | solution.py:37
  139.2 13.1 %all-to-all-start.5 = ((bf16[8,144,128]{2,1,0:T(8,128)(2,1)}), bf16[8,144,128]{2,1,0:T(8,128)(2,1)}, u32[]{:S(2)}, u32[]{:S(2)}) async-start(bf16[8,144,128]{2,1,0:T(8,128)(2,1)} %shard_map.90.refs_4_.refs_1_), calls=%async_computation.5 | async-start | bytes 589824 | tf_op jit(solution)/shard_map/all_to_all | solution.py:456
  143.6 27.9 %collective-permute-start.33 = (bf16[8,3,128,128]{3,2,1,0:T(8,128)(2,1)S(1)}, bf16[8,3,128,128]{3,2,1,0:T(8,128)(2,1)}, u32[]{:S(2)}, u32[]{:S(2)}) collective-permute-start(bf16[8,3,128,128]{3,2,1,0:T(8,128)(2,1)S(1)} %shard_map.91.refs_0_), channel_id=1, source_target_pairs={{0,12},{1,13},{2,14},{3,15},{4,0},{5,1},{6,2},{7,3},{8,4},{9,5},{1... | collective-permute-start | bytes 2359304 | tf_op jit(solution)/shard_map/ppermute | solution.py:37
  146.4 25.1 %collective-permute-start.34 = (bf16[8,3,128,128]{3,2,1,0:T(8,128)(2,1)S(1)}, bf16[8,3,128,128]{3,2,1,0:T(8,128)(2,1)}, u32[]{:S(2)}, u32[]{:S(2)}) collective-permute-start(bf16[8,3,128,128]{3,2,1,0:T(8,128)(2,1)S(1)} %shard_map.91.refs_0_), channel_id=1, source_target_pairs={{0,8},{1,9},{2,10},{3,11},{4,12},{5,13},{6,14},{7,15},{8,0},{9,1},... | collective-permute-start | bytes 2359304 | tf_op jit(solution)/shard_map/ppermute | solution.py:37
  154.7 5.6 %collective-permute-start.35 = (bf16[128,128]{1,0:T(8,128)(2,1)}, bf16[128,128]{1,0:T(8,128)(2,1)S(1)}, u32[]{:S(2)}, u32[]{:S(2)}) collective-permute-start(bf16[128,128]{1,0:T(8,128)(2,1)} %shard_map.93), channel_id=1, source_target_pairs={{0,64},{1,65},{2,66},{3,67},{4,68},{5,69},{6,70},{7,71},{8,72},{9,... | collective-permute-start | bytes 98312 | tf_op jit(solution)/shard_map/ppermute | solution.py:37
  161.4 1.3 collective-permute-start.36
  165.2 11.4 %collective-permute-start.42 = (bf16[8,144,128]{2,1,0:T(8,128)(2,1)S(1)}, bf16[8,144,128]{2,1,0:T(8,128)(2,1)S(1)}, u32[]{:S(2)}, u32[]{:S(2)}) collective-permute-start(bf16[8,144,128]{2,1,0:T(8,128)(2,1)S(1)} %get-tuple-element.103), channel_id=1, source_target_pairs={{0,4},{1,5},{2,6},{3,7},{4,8},{5,9},{6,10},{7,11},{8,12},{9,13},{1... | collective-permute-start | bytes 884744 | tf_op jit(solution)/shard_map/ppermute | solution.py:37
  166.5 10.1 %collective-permute-start.43 = (bf16[8,144,128]{2,1,0:T(8,128)(2,1)S(1)}, bf16[8,144,128]{2,1,0:T(8,128)(2,1)S(1)}, u32[]{:S(2)}, u32[]{:S(2)}) collective-permute-start(bf16[8,144,128]{2,1,0:T(8,128)(2,1)S(1)} %get-tuple-element.104), channel_id=1, source_target_pairs={{0,12},{1,13},{2,14},{3,15},{4,0},{5,1},{6,2},{7,3},{8,4},{9,5},{1... | collective-permute-start | bytes 884744 | tf_op jit(solution)/shard_map/ppermute | solution.py:37
  168.5 11.3 %collective-permute-start.44 = (bf16[8,144,128]{2,1,0:T(8,128)(2,1)S(1)}, bf16[8,144,128]{2,1,0:T(8,128)(2,1)S(1)}, u32[]{:S(2)}, u32[]{:S(2)}) collective-permute-start(bf16[8,144,128]{2,1,0:T(8,128)(2,1)S(1)} %get-tuple-element.105), channel_id=1, source_target_pairs={{0,8},{1,9},{2,10},{3,11},{4,12},{5,13},{6,14},{7,15},{8,0},{9,1},... | collective-permute-start | bytes 884744 | tf_op jit(solution)/shard_map/ppermute | solution.py:37
  176.1 33.5 %collective-permute-start.37 = (bf16[8,128,256]{2,1,0:T(8,128)(2,1)}, bf16[8,128,256]{2,1,0:T(8,128)(2,1)S(1)}, u32[]{:S(2)}, u32[]{:S(2)}) collective-permute-start(bf16[8,128,256]{2,1,0:T(8,128)(2,1)} %get-tuple-element.97), channel_id=1, source_target_pairs={{0,32},{1,33},{2,34},{3,35},{4,36},{5,37},{6,38},{7,39},{8,40},{9,... | collective-permute-start | bytes 1572872 | tf_op jit(solution)/shard_map/ppermute | solution.py:37
  176.1 33.5 %collective-permute-start.38 = (bf16[8,128,256]{2,1,0:T(8,128)(2,1)}, bf16[8,128,256]{2,1,0:T(8,128)(2,1)}, u32[]{:S(2)}, u32[]{:S(2)}) collective-permute-start(bf16[8,128,256]{2,1,0:T(8,128)(2,1)} %get-tuple-element.98), channel_id=1, source_target_pairs={{0,32},{1,33},{2,34},{3,35},{4,36},{5,37},{6,38},{7,39},{8,40},{9,... | collective-permute-start | bytes 1572872 | tf_op jit(solution)/shard_map/ppermute | solution.py:37
  176.6 33.0 %collective-permute-start.39 = (bf16[8,128,256]{2,1,0:T(8,128)(2,1)}, bf16[8,128,256]{2,1,0:T(8,128)(2,1)}, u32[]{:S(2)}, u32[]{:S(2)}) collective-permute-start(bf16[8,128,256]{2,1,0:T(8,128)(2,1)} %get-tuple-element.99), channel_id=1, source_target_pairs={{0,32},{1,33},{2,34},{3,35},{4,36},{5,37},{6,38},{7,39},{8,40},{9,... | collective-permute-start | bytes 1572872 | tf_op jit(solution)/shard_map/ppermute | solution.py:37
  176.6 33.0 %collective-permute-start.40 = (bf16[8,128,256]{2,1,0:T(8,128)(2,1)}, bf16[8,128,256]{2,1,0:T(8,128)(2,1)}, u32[]{:S(2)}, u32[]{:S(2)}) collective-permute-start(bf16[8,128,256]{2,1,0:T(8,128)(2,1)} %get-tuple-element.100), channel_id=1, source_target_pairs={{0,32},{1,33},{2,34},{3,35},{4,36},{5,37},{6,38},{7,39},{8,40},{9,... | collective-permute-start | bytes 1572872 | tf_op jit(solution)/shard_map/ppermute | solution.py:37
  181.4 15.0 %all-to-all-start.6 = ((bf16[8,144,128]{2,1,0:T(8,128)(2,1)}), bf16[8,144,128]{2,1,0:T(8,128)(2,1)S(1)}, u32[]{:S(2)}, u32[]{:S(2)}) async-start(bf16[8,144,128]{2,1,0:T(8,128)(2,1)} %shard_map.99), calls=%async_computation.6 | async-start | bytes 589824 | tf_op jit(solution)/shard_map/all_to_all | solution.py:456
  188.2 8.2 %collective-permute-start.41 = (bf16[128,256]{1,0:T(8,128)(2,1)S(1)}, bf16[128,256]{1,0:T(8,128)(2,1)S(1)}, u32[]{:S(2)}, u32[]{:S(2)}) collective-permute-start(bf16[128,256]{1,0:T(8,128)(2,1)S(1)} %copy-done.48), channel_id=1, source_target_pairs={{0,64},{1,65},{2,66},{3,67},{4,68},{5,69},{6,70},{7,71},{8,72},{9,... | collective-permute-start | bytes 196616 | tf_op jit(solution)/shard_map/ppermute | solution.py:37
  197.6 3.1 %collective-permute-start.45 = (bf16[128,128]{1,0:T(8,128)(2,1)S(1)}, bf16[128,128]{1,0:T(8,128)(2,1)S(1)}, u32[]{:S(2)}, u32[]{:S(2)}) collective-permute-start(bf16[128,128]{1,0:T(8,128)(2,1)S(1)} %shard_map.100), channel_id=1, source_target_pairs={{32,0},{33,1},{34,2},{35,3},{36,4},{37,5},{38,6},{39,7},{40,8},{41... | collective-permute-start | bytes 98312 | tf_op jit(solution)/shard_map/ppermute | solution.py:41
  201.9 7.7 %collective-permute-start.46 = (bf16[128,256]{1,0:T(8,128)(2,1)S(1)}, bf16[128,256]{1,0:T(8,128)(2,1)S(1)}, u32[]{:S(2)}, u32[]{:S(2)}) collective-permute-start(bf16[128,256]{1,0:T(8,128)(2,1)S(1)} %pad_maximum_fusion.2.refs_10_), channel_id=1, source_target_pairs={{64,0},{65,1},{66,2},{67,3},{68,4},{69,5},{70,6},{71,7},{72,8},{73... | collective-permute-start | bytes 196616 | tf_op jit(solution)/shard_map/ppermute | solution.py:41
  (57 other events, 497.2 us)

commit v4 on v3

--- a/solution.py
+++ b/solution.py
@@ -545,7 +545,7 @@
         return keep, move(send, other_core)
 
     outs = [(block, BF16), (block, F32), ((8, M), F32)]
-    keep, recv = forward(load(0), g0, first_parts)
+    keep, recv = forward(load(0), g0, ())
     x1, _, s0, out1, ft1 = call(
         combine_kernel, outs + [wide, (block, BF16)], [VM] * 4, (keep, recv, x0, gain[1])
     )

time: 217 us -> 213 us (0.982); the launches traced: 213 us -> 212 us
  starting transfers between devices: 77.3 us -> 72.2 us
  waiting for transfers between devices: 50.7 us -> 53 us
    ppermute x47, starting transfers between devices: 56 us -> 53 us  [move(): return lax.ppermute(value, BOTH, pairs(fn))]
    unnamed x104 -> x108, local copies, waits for them, and re-layouts: 12.1 us -> 12.4 us
where the time goes in v4:
time: 213 us; the launch traced here: 212 us
  starting transfers between devices  72.2 us (34%)
  waiting for transfers between devices  53 us (25%)
  Pallas kernels  37.2 us (17%)
  blocking collectives  32 us (15%)
  local copies, waits for them, and re-layouts  14.3 us (7%)
    ppermute x47, starting transfers between devices, move(): return lax.ppermute(value, BOTH, pairs(fn))  53 us
    pallas_call x35, Pallas kernels, call(): pl.pallas_call(body, out_shape=[jax.ShapeDtypeStruct(s, d) for s, d in ou...  37.2 us
    ppermute x47, waiting for transfers between devices, move(): return lax.ppermute(value, BOTH, pairs(fn))  33.2 us
    all_to_all x2, blocking collectives, exchange(): return lax.all_to_all(value, BOTH, 0, 0, axis_index_groups=PLANES)  23.4 us
    all_to_all x4, starting transfers between devices, exchange(): return lax.all_to_all(value, BOTH, 0, 0, axis_index_groups=PLANES)  16.6 us
    all_to_all x4, waiting for transfers between devices, exchange(): return lax.all_to_all(value, BOTH, 0, 0, axis_index_groups=PLANES)  13.3 us
    unnamed x108, local copies, waits for them, and re-layouts  12.4 us
    all_to_all x1, blocking collectives, on_device(): lax.all_to_all(spread, BOTH, 0, 0, axis_index_groups=CORES)  8.69 us
  transfers between devices with their start and end apart: 53, of which 25 were waited for; matrix products, arithmetic and copies ran while one was open for 1% of the time, Pallas kernels for 14%

profile of v4, /device:TPU:0, one launch (start us, length us, event | category | flops | bytes accessed | tf_op | source)
XLA Modules:
  0.0 211.8 jit_solution(9925639819976577480)
XLA Ops:
  4.6 3.4 %copy-done.2 = bf16[2,1,8192,256]{3,2,1,0:T(8,128)(2,1)S(1)} copy-done((bf16[2,1,8192,256]{3,2,1,0:T(8,128)(2,1)S(1)}, bf16[2,1,8192,256]{3,2,1,0:T(8,128)(2,1)}, u32[]{:S(2)}) %copy-start.2) | copy-done | bytes 8388632
  9.2 13.2 %all_to_all.35.refs_0_.refs_4_ = bf16[8,144,128]{2,1,0:T(8,128)(2,1)S(1)} all-to-all(bf16[8,144,128]{2,1,0:T(8,128)(2,1)S(1)} %get-tuple-element.57), channel_id=1, replica_groups={{0,1,2,3,16,17,18,19},{4,5,6,7,20,21,22,23},{8,9,10,11,24,25,26,27},{12..., dimensions={0} | all-to-all | bytes 589824 | tf_op jit(solution)/shard_map/all_to_all | solution.py:456
  22.4 1.6 collective-permute-start.1
  24.0 1.7 collective-permute-start.2
  25.6 2.0 collective-permute-start.3
  27.6 3.4 %shard_map.70.refs_0_ = bf16[24,32,128,256]{3,2,1,0:T(8,128)(2,1)} custom-call(bf16[2,32,128,256]{3,2,1,0:T(8,128)(2,1)S(1)} %get-tuple-element.59.refs_0_, bf16[2,32,128,256]{3,2,1,0:T(8,128)(2,1)S(1)} %collective-permute-done.5.refs_1_), custom_call_target="tpu_custom_call" | custom-call | tf_op jit(solution)/shard_map/pallas_call | solution.py:413
  31.0 1.6 shard_map.76.refs_1_
  32.6 1.6 shard_map.71.refs_4_
  34.2 1.6 shard_map.77
  40.5 3.4 %all-to-all-start.1 = ((bf16[8,144,128]{2,1,0:T(8,128)(2,1)}), bf16[8,144,128]{2,1,0:T(8,128)(2,1)S(1)}, u32[]{:S(2)}, u32[]{:S(2)}) async-start(bf16[8,144,128]{2,1,0:T(8,128)(2,1)} %get-tuple-element.63.refs_1_), calls=%async_computation.1 | async-start | bytes 589824 | tf_op jit(solution)/shard_map/all_to_all | solution.py:456
  43.9 2.6 %collective-permute-start.12 = (bf16[8,128,128]{2,1,0:T(8,128)(2,1)}, bf16[8,128,128]{2,1,0:T(8,128)(2,1)S(1)}, u32[]{:S(2)}, u32[]{:S(2)}) collective-permute-start(bf16[8,128,128]{2,1,0:T(8,128)(2,1)} %get-tuple-element.69), channel_id=1, source_target_pairs={{0,12},{1,13},{2,14},{3,15},{4,0},{5,1},{6,2},{7,3},{8,4},{9,5},{1... | collective-permute-start | bytes 786440 | tf_op jit(solution)/shard_map/ppermute | solution.py:37
  46.9 5.1 %all-to-all-done.1.refs_0_.refs_8_ = bf16[8,144,128]{2,1,0:T(8,128)(2,1)S(1)} async-done(((bf16[8,144,128]{2,1,0:T(8,128)(2,1)}), bf16[8,144,128]{2,1,0:T(8,128)(2,1)S(1)}, u32[]{:S(2)}, u32[]{:S(2)}) %all-to-all-start.1) | async-done | bytes 294944 | tf_op jit(solution)/shard_map/all_to_all | solution.py:456
  52.3 3.0 %collective-permute-start.8 = (bf16[8,144,128]{2,1,0:T(8,128)(2,1)S(1)}, bf16[8,144,128]{2,1,0:T(8,128)(2,1)S(1)}, u32[]{:S(2)}, u32[]{:S(2)}) collective-permute-start(bf16[8,144,128]{2,1,0:T(8,128)(2,1)S(1)} %all-to-all-done.1.refs_0_.refs_8_), channel_id=1, source_target_pairs={{0,12},{1,13},{2,14},{3,15},{4,0},{5,1},{6,2},{7,3},{8,4},{9,5},{1... | collective-permute-start | bytes 884744 | tf_op jit(solution)/shard_map/ppermute | solution.py:37
  55.9 1.8 shard_map.78
  57.7 4.5 %all-to-all-start.2 = ((bf16[8,128,128]{2,1,0:T(8,128)(2,1)}), bf16[8,128,128]{2,1,0:T(8,128)(2,1)S(1)}, u32[]{:S(2)}, u32[]{:S(2)}) async-start(bf16[8,128,128]{2,1,0:T(8,128)(2,1)} %shard_map.78), calls=%async_computation.2 | async-start | bytes 524288 | tf_op jit(solution)/shard_map/all_to_all | solution.py:456
  62.2 1.6 shard_map.74.refs_4_
  64.6 4.9 %all-to-all-done.2.refs_0_ = bf16[8,128,128]{2,1,0:T(8,128)(2,1)S(1)} async-done(((bf16[8,128,128]{2,1,0:T(8,128)(2,1)}), bf16[8,128,128]{2,1,0:T(8,128)(2,1)S(1)}, u32[]{:S(2)}, u32[]{:S(2)}) %all-to-all-start.2) | async-done | bytes 262176 | tf_op jit(solution)/shard_map/all_to_all | solution.py:456
  70.4 3.6 %collective-permute-start.14 = (bf16[128,128]{1,0:T(8,128)(2,1)S(1)}, bf16[128,128]{1,0:T(8,128)(2,1)S(1)}, u32[]{:S(2)}, u32[]{:S(2)}) collective-permute-start(bf16[128,128]{1,0:T(8,128)(2,1)S(1)} %get-tuple-element.71), channel_id=1, source_target_pairs={{0,64},{1,65},{2,66},{3,67},{4,68},{5,69},{6,70},{7,71},{8,72},{9,... | collective-permute-start | bytes 98312 | tf_op jit(solution)/shard_map/ppermute | solution.py:37
  73.9 1.9 collective-permute-done.14.refs_0_.refs_2_.refs_4_
  76.0 10.2 %all_to_all.36.refs_0_.refs_12_ = bf16[8,144,128]{2,1,0:T(8,128)(2,1)S(1)} all-to-all(bf16[8,144,128]{2,1,0:T(8,128)(2,1)S(1)} %get-tuple-element.72.refs_1_), channel_id=1, replica_groups={{0,1,2,3,16,17,18,19},{4,5,6,7,20,21,22,23},{8,9,10,11,24,25,26,27},{12..., dimensions={0} | all-to-all | bytes 589824 | tf_op jit(solution)/shard_map/all_to_all | solution.py:456
  86.9 2.6 %collective-permute-start.16 = (bf16[8,144,128]{2,1,0:T(8,128)(2,1)S(1)}, bf16[8,144,128]{2,1,0:T(8,128)(2,1)S(1)}, u32[]{:S(2)}, u32[]{:S(2)}) collective-permute-start(bf16[8,144,128]{2,1,0:T(8,128)(2,1)S(1)} %all_to_all.36.refs_0_.refs_12_), channel_id=1, source_target_pairs={{0,12},{1,13},{2,14},{3,15},{4,0},{5,1},{6,2},{7,3},{8,4},{9,5},{1... | collective-permute-start | bytes 884744 | tf_op jit(solution)/shard_map/ppermute | solution.py:37
  90.3 3.6 %collective-permute-start.18 = (bf16[128,128]{1,0:T(8,128)(2,1)S(1)}, bf16[128,128]{1,0:T(8,128)(2,1)S(1)}, u32[]{:S(2)}, u32[]{:S(2)}) collective-permute-start(bf16[128,128]{1,0:T(8,128)(2,1)S(1)} %broadcast_select_fusion), channel_id=1, source_target_pairs={{0,64},{1,65},{2,66},{3,67},{4,68},{5,69},{6,70},{7,71},{8,72},{9,... | collective-permute-start | bytes 98312 | tf_op jit(solution)/shard_map/ppermute | solution.py:37
  93.9 1.6 shard_map.82.refs_4_
  100.2 8.7 %all_to_all.37.refs_0_ = f32[16,8,128]{2,1,0:T(8,128)S(1)} all-to-all(f32[16,8,128]{2,1,0:T(8,128)S(1)} %get-tuple-element.79), channel_id=1, replica_groups={{0,1,2,3,16,17,18,19,32,33,34,35,48,49,50,51},{4,5,6,7,20,21,22,23,36,3..., dimensions={0} | all-to-all | bytes 131072 | tf_op jit(solution)/shard_map/all_to_all | solution.py:568
  108.9 3.6 %collective-permute-start.20 = (bf16[128,128]{1,0:T(8,128)(2,1)S(1)}, bf16[128,128]{1,0:T(8,128)(2,1)S(1)}, u32[]{:S(2)}, u32[]{:S(2)}) collective-permute-start(bf16[128,128]{1,0:T(8,128)(2,1)S(1)} %shard_map.86), channel_id=1, source_target_pairs={{0,64},{1,65},{2,66},{3,67},{4,68},{5,69},{6,70},{7,71},{8,72},{9,... | collective-permute-start | bytes 98312 | tf_op jit(solution)/shard_map/ppermute | solution.py:37
  112.6 1.4 collective-permute-start.25
  114.0 1.8 collective-permute-start.26
  116.5 1.6 shard_map.87.refs_8_.refs_3_
  118.1 2.8 %collective-permute-done.27.refs_3_ = f32[8,128]{1,0:T(8,128)S(1)} collective-permute-done((f32[8,128]{1,0:T(8,128)S(1)}, f32[8,128]{1,0:T(8,128)S(1)}, u32[]{:S(2)}, u32[]{:S(2)}) %collective-permute-start.27) | collective-permute-done | bytes 4128 | tf_op jit(solution)/shard_map/ppermute | solution.py:37
  124.9 3.0 %collective-permute-start.30 = (bf16[8,144,128]{2,1,0:T(8,128)(2,1)S(1)}, bf16[8,144,128]{2,1,0:T(8,128)(2,1)S(1)}, u32[]{:S(2)}, u32[]{:S(2)}) collective-permute-start(bf16[8,144,128]{2,1,0:T(8,128)(2,1)S(1)} %get-tuple-element.86), channel_id=1, source_target_pairs={{0,12},{1,13},{2,14},{3,15},{4,0},{5,1},{6,2},{7,3},{8,4},{9,5},{1... | collective-permute-start | bytes 884744 | tf_op jit(solution)/shard_map/ppermute | solution.py:37
  127.9 1.7 collective-permute-done.21
  130.5 2.5 %collective-permute-start.23 = (bf16[2,3,128,128]{3,2,1,0:T(8,128)(2,1)S(1)}, bf16[2,3,128,128]{3,2,1,0:T(8,128)(2,1)S(1)}, u32[]{:S(2)}, u32[]{:S(2)}) collective-permute-start(bf16[2,3,128,128]{3,2,1,0:T(8,128)(2,1)S(1)} %pad_maximum_fusion.refs_0_), channel_id=1, source_target_pairs={{0,3},{1,0},{2,1},{3,2},{4,7},{5,4},{6,5},{7,6},{8,11},{9,8},{10,9... | collective-permute-start | bytes 589832 | tf_op jit(solution)/shard_map/ppermute | solution.py:37
  135.1 3.5 %collective-permute-done.31.refs_3_ = bf16[8,144,128]{2,1,0:T(8,128)(2,1)S(1)} collective-permute-done((bf16[8,144,128]{2,1,0:T(8,128)(2,1)S(1)}, bf16[8,144,128]{2,1,0:T(8,128)(2,1)S(1)}, u32[]{:S(2)}, u32[]{:S(2)}) %collective-permute-start.31) | collective-permute-done | bytes 294944 | tf_op jit(solution)/shard_map/ppermute | solution.py:37
  140.5 4.5 %all-to-all-start.5 = ((bf16[8,144,128]{2,1,0:T(8,128)(2,1)}), bf16[8,144,128]{2,1,0:T(8,128)(2,1)}, u32[]{:S(2)}, u32[]{:S(2)}) async-start(bf16[8,144,128]{2,1,0:T(8,128)(2,1)} %shard_map.90.refs_4_.refs_1_), calls=%async_computation.5 | async-start | bytes 589824 | tf_op jit(solution)/shard_map/all_to_all | solution.py:456
  145.0 2.8 %collective-permute-start.33 = (bf16[8,3,128,128]{3,2,1,0:T(8,128)(2,1)S(1)}, bf16[8,3,128,128]{3,2,1,0:T(8,128)(2,1)}, u32[]{:S(2)}, u32[]{:S(2)}) collective-permute-start(bf16[8,3,128,128]{3,2,1,0:T(8,128)(2,1)S(1)} %shard_map.91.refs_0_), channel_id=1, source_target_pairs={{0,12},{1,13},{2,14},{3,15},{4,0},{5,1},{6,2},{7,3},{8,4},{9,5},{1... | collective-permute-start | bytes 2359304 | tf_op jit(solution)/shard_map/ppermute | solution.py:37
  148.7 1.6 shard_map.92.refs_5_.refs_3_
  150.3 3.3 %all-to-all-done.5.refs_0_ = bf16[8,144,128]{2,1,0:T(8,128)(2,1)} async-done(((bf16[8,144,128]{2,1,0:T(8,128)(2,1)}), bf16[8,144,128]{2,1,0:T(8,128)(2,1)}, u32[]{:S(2)}, u32[]{:S(2)}) %all-to-all-start.5) | async-done | bytes 294944 | tf_op jit(solution)/shard_map/all_to_all | solution.py:456
  154.3 1.7 shard_map.93
  156.0 1.6 collective-permute-start.35
  157.7 4.0 %collective-permute-done.35.refs_0_ = bf16[128,128]{1,0:T(8,128)(2,1)S(1)} collective-permute-done((bf16[128,128]{1,0:T(8,128)(2,1)}, bf16[128,128]{1,0:T(8,128)(2,1)S(1)}, u32[]{:S(2)}, u32[]{:S(2)}) %collective-permute-start.35) | collective-permute-done | bytes 32800 | tf_op jit(solution)/shard_map/ppermute | solution.py:37
  167.8 2.0 collective-permute-start.43
  171.1 1.7 shard_map.97.refs_4_
  173.4 4.0 %shard_map.96 = (bf16[8,128,256]{2,1,0:T(8,128)(2,1)S(1)}, bf16[8,128,256]{2,1,0:T(8,128)(2,1)S(1)}, bf16[8,128,256]{2,1,0:T(8,128)(2,1)S(1)}, bf16[8,128,256]{2...) custom-call(bf16[8,3,128,128]{3,2,1,0:T(8,128)(2,1)S(1)} %shard_map., ...), custom_call_target="tpu_custom_call" | custom-call | tf_op jit(solution)/shard_map/pallas_call | solution.py:413
  178.5 2.0 shard_map.98
  182.7 4.2 %all-to-all-start.6 = ((bf16[8,144,128]{2,1,0:T(8,128)(2,1)}), bf16[8,144,128]{2,1,0:T(8,128)(2,1)S(1)}, u32[]{:S(2)}, u32[]{:S(2)}) async-start(bf16[8,144,128]{2,1,0:T(8,128)(2,1)} %shard_map.99), calls=%async_computation.6 | async-start | bytes 589824 | tf_op jit(solution)/shard_map/all_to_all | solution.py:456
  188.2 6.4 %collective-permute-done.41.refs_9_ = bf16[128,256]{1,0:T(8,128)(2,1)S(1)} collective-permute-done((bf16[128,256]{1,0:T(8,128)(2,1)S(1)}, bf16[128,256]{1,0:T(8,128)(2,1)S(1)}, u32[]{:S(2)}, u32[]{:S(2)}) %collective-permute-start.41) | collective-permute-done | bytes 65568 | tf_op jit(solution)/shard_map/ppermute | solution.py:37
  202.2 5.7 %collective-permute-done.46.refs_11_ = bf16[128,256]{1,0:T(8,128)(2,1)S(1)} collective-permute-done((bf16[128,256]{1,0:T(8,128)(2,1)S(1)}, bf16[128,256]{1,0:T(8,128)(2,1)S(1)}, u32[]{:S(2)}, u32[]{:S(2)}) %collective-permute-start.46) | collective-permute-done | bytes 65568 | tf_op jit(solution)/shard_map/ppermute | solution.py:41
  208.0 3.7 %shard_map.101 = bf16[32,2,128,256]{3,2,1,0:T(8,128)(2,1)} custom-call(bf16[8,128,256]{2,1,0:T(8,128)(2,1)S(1)} %get-tuple-element.93.refs_0_, bf16[8,128,256]{2,1,0:T(8,128)(2,1)S(1)} %get-tuple-element.94.refs_1_, bf16[8,128,256]{2,1,0:T(8,128)(2,1)S(1)} %get-tuple-element.95.refs_2_, bf16[8,128,256]{2,1,0:T(8,128)(2,1)S(1)} %copy-done.26, ...), custom_call_target="tpu_custom_call" | custom-call | flops 1073741824 | bytes 8388608 | tf_op jit(solution)/shard_map/pallas_call | solution.py:413
  (218 shorter events, 50.1 us)
Async XLA Ops:
  8.9 18.7 %collective-permute-start.5 = (bf16[2,32,128,256]{3,2,1,0:T(8,128)(2,1)S(1)}, bf16[2,32,128,256]{3,2,1,0:T(8,128)(2,1)S(1)}, u32[]{:S(2)}, u32[]{:S(2)}) collective-permute-start(bf16[2,32,128,256]{3,2,1,0:T(8,128)(2,1)S(1)} %get-tuple-element.60), channel_id=1, source_target_pairs={{0,32},{1,33},{2,34},{3,35},{4,36},{5,37},{6,38},{7,39},{8,40},{9,... | collective-permute-start | bytes 12582920 | tf_op jit(solution)/shard_map/ppermute | solution.py:37
  22.4 14.1 %collective-permute-start.1 = (bf16[8,144,128]{2,1,0:T(8,128)(2,1)S(1)}, bf16[8,144,128]{2,1,0:T(8,128)(2,1)S(1)}, u32[]{:S(2)}, u32[]{:S(2)}) collective-permute-start(bf16[8,144,128]{2,1,0:T(8,128)(2,1)S(1)} %all_to_all.35.refs_0_.refs_4_), channel_id=1, source_target_pairs={{0,4},{1,5},{2,6},{3,7},{4,8},{5,9},{6,10},{7,11},{8,12},{9,13},{1... | collective-permute-start | bytes 884744 | tf_op jit(solution)/shard_map/ppermute | solution.py:37
  24.0 12.5 %collective-permute-start.2 = (bf16[8,144,128]{2,1,0:T(8,128)(2,1)S(1)}, bf16[8,144,128]{2,1,0:T(8,128)(2,1)S(1)}, u32[]{:S(2)}, u32[]{:S(2)}) collective-permute-start(bf16[8,144,128]{2,1,0:T(8,128)(2,1)S(1)} %all_to_all.35.refs_0_.refs_4_), channel_id=1, source_target_pairs={{0,12},{1,13},{2,14},{3,15},{4,0},{5,1},{6,2},{7,3},{8,4},{9,5},{1... | collective-permute-start | bytes 884744 | tf_op jit(solution)/shard_map/ppermute | solution.py:37
  25.6 10.9 %collective-permute-start.3 = (bf16[8,144,128]{2,1,0:T(8,128)(2,1)S(1)}, bf16[8,144,128]{2,1,0:T(8,128)(2,1)S(1)}, u32[]{:S(2)}, u32[]{:S(2)}) collective-permute-start(bf16[8,144,128]{2,1,0:T(8,128)(2,1)S(1)} %all_to_all.35.refs_0_.refs_4_), channel_id=1, source_target_pairs={{0,8},{1,9},{2,10},{3,11},{4,12},{5,13},{6,14},{7,15},{8,0},{9,1},... | collective-permute-start | bytes 884744 | tf_op jit(solution)/shard_map/ppermute | solution.py:37
  35.8 19.4 %collective-permute-start.11 = (bf16[8,128,128]{2,1,0:T(8,128)(2,1)S(1)}, bf16[8,128,128]{2,1,0:T(8,128)(2,1)S(1)}, u32[]{:S(2)}, u32[]{:S(2)}) collective-permute-start(bf16[8,128,128]{2,1,0:T(8,128)(2,1)S(1)} %get-tuple-element.68), channel_id=1, source_target_pairs={{0,4},{1,5},{2,6},{3,7},{4,8},{5,9},{6,10},{7,11},{8,12},{9,13},{1... | collective-permute-start | bytes 786440 | tf_op jit(solution)/shard_map/ppermute | solution.py:37
  37.0 1.3 collective-permute-start.6
  40.5 11.5 %all-to-all-start.1 = ((bf16[8,144,128]{2,1,0:T(8,128)(2,1)}), bf16[8,144,128]{2,1,0:T(8,128)(2,1)S(1)}, u32[]{:S(2)}, u32[]{:S(2)}) async-start(bf16[8,144,128]{2,1,0:T(8,128)(2,1)} %get-tuple-element.63.refs_1_), calls=%async_computation.1 | async-start | bytes 589824 | tf_op jit(solution)/shard_map/all_to_all | solution.py:456
  43.9 12.0 %collective-permute-start.12 = (bf16[8,128,128]{2,1,0:T(8,128)(2,1)}, bf16[8,128,128]{2,1,0:T(8,128)(2,1)S(1)}, u32[]{:S(2)}, u32[]{:S(2)}) collective-permute-start(bf16[8,128,128]{2,1,0:T(8,128)(2,1)} %get-tuple-element.69), channel_id=1, source_target_pairs={{0,12},{1,13},{2,14},{3,15},{4,0},{5,1},{6,2},{7,3},{8,4},{9,5},{1... | collective-permute-start | bytes 786440 | tf_op jit(solution)/shard_map/ppermute | solution.py:37
  46.5 9.4 %collective-permute-start.13 = (bf16[8,128,128]{2,1,0:T(8,128)(2,1)}, bf16[8,128,128]{2,1,0:T(8,128)(2,1)}, u32[]{:S(2)}, u32[]{:S(2)}) collective-permute-start(bf16[8,128,128]{2,1,0:T(8,128)(2,1)} %get-tuple-element.70), channel_id=1, source_target_pairs={{0,8},{1,9},{2,10},{3,11},{4,12},{5,13},{6,14},{7,15},{8,0},{9,1},... | collective-permute-start | bytes 786440 | tf_op jit(solution)/shard_map/ppermute | solution.py:37
  52.0 11.8 %collective-permute-start.7 = (bf16[8,144,128]{2,1,0:T(8,128)(2,1)S(1)}, bf16[8,144,128]{2,1,0:T(8,128)(2,1)S(1)}, u32[]{:S(2)}, u32[]{:S(2)}) collective-permute-start(bf16[8,144,128]{2,1,0:T(8,128)(2,1)S(1)} %all-to-all-done.1.refs_0_.refs_8_), channel_id=1, source_target_pairs={{0,4},{1,5},{2,6},{3,7},{4,8},{5,9},{6,10},{7,11},{8,12},{9,13},{1... | collective-permute-start | bytes 884744 | tf_op jit(solution)/shard_map/ppermute | solution.py:37
  52.3 11.8 %collective-permute-start.8 = (bf16[8,144,128]{2,1,0:T(8,128)(2,1)S(1)}, bf16[8,144,128]{2,1,0:T(8,128)(2,1)S(1)}, u32[]{:S(2)}, u32[]{:S(2)}) collective-permute-start(bf16[8,144,128]{2,1,0:T(8,128)(2,1)S(1)} %all-to-all-done.1.refs_0_.refs_8_), channel_id=1, source_target_pairs={{0,12},{1,13},{2,14},{3,15},{4,0},{5,1},{6,2},{7,3},{8,4},{9,5},{1... | collective-permute-start | bytes 884744 | tf_op jit(solution)/shard_map/ppermute | solution.py:37
  55.2 8.8 %collective-permute-start.9 = (bf16[8,144,128]{2,1,0:T(8,128)(2,1)S(1)}, bf16[8,144,128]{2,1,0:T(8,128)(2,1)S(1)}, u32[]{:S(2)}, u32[]{:S(2)}) collective-permute-start(bf16[8,144,128]{2,1,0:T(8,128)(2,1)S(1)} %all-to-all-done.1.refs_0_.refs_8_), channel_id=1, source_target_pairs={{0,8},{1,9},{2,10},{3,11},{4,12},{5,13},{6,14},{7,15},{8,0},{9,1},... | collective-permute-start | bytes 884744 | tf_op jit(solution)/shard_map/ppermute | solution.py:37
  57.7 11.8 %all-to-all-start.2 = ((bf16[8,128,128]{2,1,0:T(8,128)(2,1)}), bf16[8,128,128]{2,1,0:T(8,128)(2,1)S(1)}, u32[]{:S(2)}, u32[]{:S(2)}) async-start(bf16[8,128,128]{2,1,0:T(8,128)(2,1)} %shard_map.78), calls=%async_computation.2 | async-start | bytes 524288 | tf_op jit(solution)/shard_map/all_to_all | solution.py:456
  64.5 5.1 %collective-permute-start.10 = (f32[136,128]{1,0:T(8,128)S(1)}, f32[136,128]{1,0:T(8,128)S(1)}, u32[]{:S(2)}, u32[]{:S(2)}) collective-permute-start(f32[136,128]{1,0:T(8,128)S(1)} %get-tuple-element.65), channel_id=1, source_target_pairs={{0,32},{1,33},{2,34},{3,35},{4,36},{5,37},{6,38},{7,39},{8,40},{9,... | collective-permute-start | bytes 208904 | tf_op jit(solution)/shard_map/ppermute | solution.py:37
  70.4 5.5 %collective-permute-start.14 = (bf16[128,128]{1,0:T(8,128)(2,1)S(1)}, bf16[128,128]{1,0:T(8,128)(2,1)S(1)}, u32[]{:S(2)}, u32[]{:S(2)}) collective-permute-start(bf16[128,128]{1,0:T(8,128)(2,1)S(1)} %get-tuple-element.71), channel_id=1, source_target_pairs={{0,64},{1,65},{2,66},{3,67},{4,68},{5,69},{6,70},{7,71},{8,72},{9,... | collective-permute-start | bytes 98312 | tf_op jit(solution)/shard_map/ppermute | solution.py:37
  86.1 9.6 %collective-permute-start.15 = (bf16[8,144,128]{2,1,0:T(8,128)(2,1)S(1)}, bf16[8,144,128]{2,1,0:T(8,128)(2,1)S(1)}, u32[]{:S(2)}, u32[]{:S(2)}) collective-permute-start(bf16[8,144,128]{2,1,0:T(8,128)(2,1)S(1)} %all_to_all.36.refs_0_.refs_12_), channel_id=1, source_target_pairs={{0,4},{1,5},{2,6},{3,7},{4,8},{5,9},{6,10},{7,11},{8,12},{9,13},{1... | collective-permute-start | bytes 884744 | tf_op jit(solution)/shard_map/ppermute | solution.py:37
  86.9 10.0 %collective-permute-start.16 = (bf16[8,144,128]{2,1,0:T(8,128)(2,1)S(1)}, bf16[8,144,128]{2,1,0:T(8,128)(2,1)S(1)}, u32[]{:S(2)}, u32[]{:S(2)}) collective-permute-start(bf16[8,144,128]{2,1,0:T(8,128)(2,1)S(1)} %all_to_all.36.refs_0_.refs_12_), channel_id=1, source_target_pairs={{0,12},{1,13},{2,14},{3,15},{4,0},{5,1},{6,2},{7,3},{8,4},{9,5},{1... | collective-permute-start | bytes 884744 | tf_op jit(solution)/shard_map/ppermute | solution.py:37
  89.4 8.7 %collective-permute-start.17 = (bf16[8,144,128]{2,1,0:T(8,128)(2,1)S(1)}, bf16[8,144,128]{2,1,0:T(8,128)(2,1)S(1)}, u32[]{:S(2)}, u32[]{:S(2)}) collective-permute-start(bf16[8,144,128]{2,1,0:T(8,128)(2,1)S(1)} %all_to_all.36.refs_0_.refs_12_), channel_id=1, source_target_pairs={{0,8},{1,9},{2,10},{3,11},{4,12},{5,13},{6,14},{7,15},{8,0},{9,1},... | collective-permute-start | bytes 884744 | tf_op jit(solution)/shard_map/ppermute | solution.py:37
  90.3 5.5 %collective-permute-start.18 = (bf16[128,128]{1,0:T(8,128)(2,1)S(1)}, bf16[128,128]{1,0:T(8,128)(2,1)S(1)}, u32[]{:S(2)}, u32[]{:S(2)}) collective-permute-start(bf16[128,128]{1,0:T(8,128)(2,1)S(1)} %broadcast_select_fusion), channel_id=1, source_target_pairs={{0,64},{1,65},{2,66},{3,67},{4,68},{5,69},{6,70},{7,71},{8,72},{9,... | collective-permute-start | bytes 98312 | tf_op jit(solution)/shard_map/ppermute | solution.py:37
  98.6 1.3 collective-permute-start.19
  108.9 12.0 %collective-permute-start.20 = (bf16[128,128]{1,0:T(8,128)(2,1)S(1)}, bf16[128,128]{1,0:T(8,128)(2,1)S(1)}, u32[]{:S(2)}, u32[]{:S(2)}) collective-permute-start(bf16[128,128]{1,0:T(8,128)(2,1)S(1)} %shard_map.86), channel_id=1, source_target_pairs={{0,64},{1,65},{2,66},{3,67},{4,68},{5,69},{6,70},{7,71},{8,72},{9,... | collective-permute-start | bytes 98312 | tf_op jit(solution)/shard_map/ppermute | solution.py:37
  112.6 5.5 %collective-permute-start.25 = (f32[8,128]{1,0:T(8,128)S(1)}, f32[8,128]{1,0:T(8,128)S(1)}, u32[]{:S(2)}, u32[]{:S(2)}) collective-permute-start(f32[8,128]{1,0:T(8,128)S(1)} %shard_map.85.refs_2_.refs_0_), channel_id=1, source_target_pairs={{0,4},{1,5},{2,6},{3,7},{4,8},{5,9},{6,10},{7,11},{8,12},{9,13},{1... | collective-permute-start | bytes 12296 | tf_op jit(solution)/shard_map/ppermute | solution.py:37
  114.0 4.1 %collective-permute-start.26 = (f32[8,128]{1,0:T(8,128)S(1)}, f32[8,128]{1,0:T(8,128)S(1)}, u32[]{:S(2)}, u32[]{:S(2)}) collective-permute-start(f32[8,128]{1,0:T(8,128)S(1)} %shard_map.85.refs_2_.refs_0_), channel_id=1, source_target_pairs={{0,12},{1,13},{2,14},{3,15},{4,0},{5,1},{6,2},{7,3},{8,4},{9,5},{1... | collective-permute-start | bytes 12296 | tf_op jit(solution)/shard_map/ppermute | solution.py:37
  115.8 5.1 %collective-permute-start.27 = (f32[8,128]{1,0:T(8,128)S(1)}, f32[8,128]{1,0:T(8,128)S(1)}, u32[]{:S(2)}, u32[]{:S(2)}) collective-permute-start(f32[8,128]{1,0:T(8,128)S(1)} %shard_map.85.refs_2_.refs_0_), channel_id=1, source_target_pairs={{0,8},{1,9},{2,10},{3,11},{4,12},{5,13},{6,14},{7,15},{8,0},{9,1},... | collective-permute-start | bytes 12296 | tf_op jit(solution)/shard_map/ppermute | solution.py:37
  124.4 8.6 %collective-permute-start.29 = (bf16[8,144,128]{2,1,0:T(8,128)(2,1)S(1)}, bf16[8,144,128]{2,1,0:T(8,128)(2,1)S(1)}, u32[]{:S(2)}, u32[]{:S(2)}) collective-permute-start(bf16[8,144,128]{2,1,0:T(8,128)(2,1)S(1)} %get-tuple-element.85), channel_id=1, source_target_pairs={{0,4},{1,5},{2,6},{3,7},{4,8},{5,9},{6,10},{7,11},{8,12},{9,13},{1... | collective-permute-start | bytes 884744 | tf_op jit(solution)/shard_map/ppermute | solution.py:37
  124.6 5.0 %collective-permute-start.21 = (bf16[3,128,128]{2,1,0:T(8,128)(2,1)S(1)}, bf16[3,128,128]{2,1,0:T(8,128)(2,1)S(1)}, u32[]{:S(2)}, u32[]{:S(2)}) collective-permute-start(bf16[3,128,128]{2,1,0:T(8,128)(2,1)S(1)} %get-tuple-element.113), channel_id=1, source_target_pairs={{0,16},{1,17},{2,18},{3,19},{4,20},{5,21},{6,22},{7,23},{8,24},{9,... | collective-permute-start | bytes 294920 | tf_op jit(solution)/shard_map/ppermute | solution.py:37
  124.9 10.2 %collective-permute-start.30 = (bf16[8,144,128]{2,1,0:T(8,128)(2,1)S(1)}, bf16[8,144,128]{2,1,0:T(8,128)(2,1)S(1)}, u32[]{:S(2)}, u32[]{:S(2)}) collective-permute-start(bf16[8,144,128]{2,1,0:T(8,128)(2,1)S(1)} %get-tuple-element.86), channel_id=1, source_target_pairs={{0,12},{1,13},{2,14},{3,15},{4,0},{5,1},{6,2},{7,3},{8,4},{9,5},{1... | collective-permute-start | bytes 884744 | tf_op jit(solution)/shard_map/ppermute | solution.py:37
  127.9 10.7 %collective-permute-start.31 = (bf16[8,144,128]{2,1,0:T(8,128)(2,1)S(1)}, bf16[8,144,128]{2,1,0:T(8,128)(2,1)S(1)}, u32[]{:S(2)}, u32[]{:S(2)}) collective-permute-start(bf16[8,144,128]{2,1,0:T(8,128)(2,1)S(1)} %get-tuple-element.87), channel_id=1, source_target_pairs={{0,8},{1,9},{2,10},{3,11},{4,12},{5,13},{6,14},{7,15},{8,0},{9,1},... | collective-permute-start | bytes 884744 | tf_op jit(solution)/shard_map/ppermute | solution.py:37
  129.7 9.9 %collective-permute-start.22 = (bf16[2,3,128,128]{3,2,1,0:T(8,128)(2,1)S(1)}, bf16[2,3,128,128]{3,2,1,0:T(8,128)(2,1)S(1)}, u32[]{:S(2)}, u32[]{:S(2)}) collective-permute-start(bf16[2,3,128,128]{3,2,1,0:T(8,128)(2,1)S(1)} %pad_maximum_fusion.refs_0_), channel_id=1, source_target_pairs={{0,1},{1,2},{2,3},{3,0},{4,5},{5,6},{6,7},{7,4},{8,9},{9,10},{10,1... | collective-permute-start | bytes 589832 | tf_op jit(solution)/shard_map/ppermute | solution.py:37
  130.5 9.0 %collective-permute-start.23 = (bf16[2,3,128,128]{3,2,1,0:T(8,128)(2,1)S(1)}, bf16[2,3,128,128]{3,2,1,0:T(8,128)(2,1)S(1)}, u32[]{:S(2)}, u32[]{:S(2)}) collective-permute-start(bf16[2,3,128,128]{3,2,1,0:T(8,128)(2,1)S(1)} %pad_maximum_fusion.refs_0_), channel_id=1, source_target_pairs={{0,3},{1,0},{2,1},{3,2},{4,7},{5,4},{6,5},{7,6},{8,11},{9,8},{10,9... | collective-permute-start | bytes 589832 | tf_op jit(solution)/shard_map/ppermute | solution.py:37
  133.0 7.2 %collective-permute-start.24 = (bf16[2,3,128,128]{3,2,1,0:T(8,128)(2,1)S(1)}, bf16[2,3,128,128]{3,2,1,0:T(8,128)(2,1)S(1)}, u32[]{:S(2)}, u32[]{:S(2)}) collective-permute-start(bf16[2,3,128,128]{3,2,1,0:T(8,128)(2,1)S(1)} %pad_maximum_fusion.refs_0_), channel_id=1, source_target_pairs={{0,2},{1,3},{2,0},{3,1},{4,6},{5,7},{6,4},{7,5},{8,10},{9,11},{10,... | collective-permute-start | bytes 589832 | tf_op jit(solution)/shard_map/ppermute | solution.py:37
  140.2 29.6 %collective-permute-start.32 = (bf16[8,3,128,128]{3,2,1,0:T(8,128)(2,1)S(1)}, bf16[8,3,128,128]{3,2,1,0:T(8,128)(2,1)}, u32[]{:S(2)}, u32[]{:S(2)}) collective-permute-start(bf16[8,3,128,128]{3,2,1,0:T(8,128)(2,1)S(1)} %shard_map.91.refs_0_), channel_id=1, source_target_pairs={{0,4},{1,5},{2,6},{3,7},{4,8},{5,9},{6,10},{7,11},{8,12},{9,13},{1... | collective-permute-start | bytes 2359304 | tf_op jit(solution)/shard_map/ppermute | solution.py:37
  140.5 13.1 %all-to-all-start.5 = ((bf16[8,144,128]{2,1,0:T(8,128)(2,1)}), bf16[8,144,128]{2,1,0:T(8,128)(2,1)}, u32[]{:S(2)}, u32[]{:S(2)}) async-start(bf16[8,144,128]{2,1,0:T(8,128)(2,1)} %shard_map.90.refs_4_.refs_1_), calls=%async_computation.5 | async-start | bytes 589824 | tf_op jit(solution)/shard_map/all_to_all | solution.py:456
  145.0 27.9 %collective-permute-start.33 = (bf16[8,3,128,128]{3,2,1,0:T(8,128)(2,1)S(1)}, bf16[8,3,128,128]{3,2,1,0:T(8,128)(2,1)}, u32[]{:S(2)}, u32[]{:S(2)}) collective-permute-start(bf16[8,3,128,128]{3,2,1,0:T(8,128)(2,1)S(1)} %shard_map.91.refs_0_), channel_id=1, source_target_pairs={{0,12},{1,13},{2,14},{3,15},{4,0},{5,1},{6,2},{7,3},{8,4},{9,5},{1... | collective-permute-start | bytes 2359304 | tf_op jit(solution)/shard_map/ppermute | solution.py:37
  147.8 25.1 %collective-permute-start.34 = (bf16[8,3,128,128]{3,2,1,0:T(8,128)(2,1)S(1)}, bf16[8,3,128,128]{3,2,1,0:T(8,128)(2,1)}, u32[]{:S(2)}, u32[]{:S(2)}) collective-permute-start(bf16[8,3,128,128]{3,2,1,0:T(8,128)(2,1)S(1)} %shard_map.91.refs_0_), channel_id=1, source_target_pairs={{0,8},{1,9},{2,10},{3,11},{4,12},{5,13},{6,14},{7,15},{8,0},{9,1},... | collective-permute-start | bytes 2359304 | tf_op jit(solution)/shard_map/ppermute | solution.py:37
  156.0 5.6 %collective-permute-start.35 = (bf16[128,128]{1,0:T(8,128)(2,1)}, bf16[128,128]{1,0:T(8,128)(2,1)S(1)}, u32[]{:S(2)}, u32[]{:S(2)}) collective-permute-start(bf16[128,128]{1,0:T(8,128)(2,1)} %shard_map.93), channel_id=1, source_target_pairs={{0,64},{1,65},{2,66},{3,67},{4,68},{5,69},{6,70},{7,71},{8,72},{9,... | collective-permute-start | bytes 98312 | tf_op jit(solution)/shard_map/ppermute | solution.py:37
  162.8 1.3 collective-permute-start.36
  166.5 11.4 %collective-permute-start.42 = (bf16[8,144,128]{2,1,0:T(8,128)(2,1)S(1)}, bf16[8,144,128]{2,1,0:T(8,128)(2,1)S(1)}, u32[]{:S(2)}, u32[]{:S(2)}) collective-permute-start(bf16[8,144,128]{2,1,0:T(8,128)(2,1)S(1)} %get-tuple-element.103), channel_id=1, source_target_pairs={{0,4},{1,5},{2,6},{3,7},{4,8},{5,9},{6,10},{7,11},{8,12},{9,13},{1... | collective-permute-start | bytes 884744 | tf_op jit(solution)/shard_map/ppermute | solution.py:37
  167.8 10.1 %collective-permute-start.43 = (bf16[8,144,128]{2,1,0:T(8,128)(2,1)S(1)}, bf16[8,144,128]{2,1,0:T(8,128)(2,1)S(1)}, u32[]{:S(2)}, u32[]{:S(2)}) collective-permute-start(bf16[8,144,128]{2,1,0:T(8,128)(2,1)S(1)} %get-tuple-element.104), channel_id=1, source_target_pairs={{0,12},{1,13},{2,14},{3,15},{4,0},{5,1},{6,2},{7,3},{8,4},{9,5},{1... | collective-permute-start | bytes 884744 | tf_op jit(solution)/shard_map/ppermute | solution.py:37
  169.8 11.4 %collective-permute-start.44 = (bf16[8,144,128]{2,1,0:T(8,128)(2,1)S(1)}, bf16[8,144,128]{2,1,0:T(8,128)(2,1)S(1)}, u32[]{:S(2)}, u32[]{:S(2)}) collective-permute-start(bf16[8,144,128]{2,1,0:T(8,128)(2,1)S(1)} %get-tuple-element.105), channel_id=1, source_target_pairs={{0,8},{1,9},{2,10},{3,11},{4,12},{5,13},{6,14},{7,15},{8,0},{9,1},... | collective-permute-start | bytes 884744 | tf_op jit(solution)/shard_map/ppermute | solution.py:37
  177.4 30.5 %collective-permute-start.37 = (bf16[8,128,256]{2,1,0:T(8,128)(2,1)}, bf16[8,128,256]{2,1,0:T(8,128)(2,1)S(1)}, u32[]{:S(2)}, u32[]{:S(2)}) collective-permute-start(bf16[8,128,256]{2,1,0:T(8,128)(2,1)} %get-tuple-element.97), channel_id=1, source_target_pairs={{0,32},{1,33},{2,34},{3,35},{4,36},{5,37},{6,38},{7,39},{8,40},{9,... | collective-permute-start | bytes 1572872 | tf_op jit(solution)/shard_map/ppermute | solution.py:37
  177.4 30.5 %collective-permute-start.38 = (bf16[8,128,256]{2,1,0:T(8,128)(2,1)}, bf16[8,128,256]{2,1,0:T(8,128)(2,1)}, u32[]{:S(2)}, u32[]{:S(2)}) collective-permute-start(bf16[8,128,256]{2,1,0:T(8,128)(2,1)} %get-tuple-element.98), channel_id=1, source_target_pairs={{0,32},{1,33},{2,34},{3,35},{4,36},{5,37},{6,38},{7,39},{8,40},{9,... | collective-permute-start | bytes 1572872 | tf_op jit(solution)/shard_map/ppermute | solution.py:37
  177.9 30.0 %collective-permute-start.39 = (bf16[8,128,256]{2,1,0:T(8,128)(2,1)}, bf16[8,128,256]{2,1,0:T(8,128)(2,1)}, u32[]{:S(2)}, u32[]{:S(2)}) collective-permute-start(bf16[8,128,256]{2,1,0:T(8,128)(2,1)} %get-tuple-element.99), channel_id=1, source_target_pairs={{0,32},{1,33},{2,34},{3,35},{4,36},{5,37},{6,38},{7,39},{8,40},{9,... | collective-permute-start | bytes 1572872 | tf_op jit(solution)/shard_map/ppermute | solution.py:37
  178.0 30.0 %collective-permute-start.40 = (bf16[8,128,256]{2,1,0:T(8,128)(2,1)}, bf16[8,128,256]{2,1,0:T(8,128)(2,1)}, u32[]{:S(2)}, u32[]{:S(2)}) collective-permute-start(bf16[8,128,256]{2,1,0:T(8,128)(2,1)} %get-tuple-element.100), channel_id=1, source_target_pairs={{0,32},{1,33},{2,34},{3,35},{4,36},{5,37},{6,38},{7,39},{8,40},{9,... | collective-permute-start | bytes 1572872 | tf_op jit(solution)/shard_map/ppermute | solution.py:37
  182.7 11.9 %all-to-all-start.6 = ((bf16[8,144,128]{2,1,0:T(8,128)(2,1)}), bf16[8,144,128]{2,1,0:T(8,128)(2,1)S(1)}, u32[]{:S(2)}, u32[]{:S(2)}) async-start(bf16[8,144,128]{2,1,0:T(8,128)(2,1)} %shard_map.99), calls=%async_computation.6 | async-start | bytes 589824 | tf_op jit(solution)/shard_map/all_to_all | solution.py:456
  187.0 7.7 %collective-permute-start.41 = (bf16[128,256]{1,0:T(8,128)(2,1)S(1)}, bf16[128,256]{1,0:T(8,128)(2,1)S(1)}, u32[]{:S(2)}, u32[]{:S(2)}) collective-permute-start(bf16[128,256]{1,0:T(8,128)(2,1)S(1)} %copy-done.50), channel_id=1, source_target_pairs={{0,64},{1,65},{2,66},{3,67},{4,68},{5,69},{6,70},{7,71},{8,72},{9,... | collective-permute-start | bytes 196616 | tf_op jit(solution)/shard_map/ppermute | solution.py:37
  195.9 3.1 %collective-permute-start.45 = (bf16[128,128]{1,0:T(8,128)(2,1)S(1)}, bf16[128,128]{1,0:T(8,128)(2,1)S(1)}, u32[]{:S(2)}, u32[]{:S(2)}) collective-permute-start(bf16[128,128]{1,0:T(8,128)(2,1)S(1)} %shard_map.100), channel_id=1, source_target_pairs={{32,0},{33,1},{34,2},{35,3},{36,4},{37,5},{38,6},{39,7},{40,8},{41... | collective-permute-start | bytes 98312 | tf_op jit(solution)/shard_map/ppermute | solution.py:41
  200.3 7.7 %collective-permute-start.46 = (bf16[128,256]{1,0:T(8,128)(2,1)S(1)}, bf16[128,256]{1,0:T(8,128)(2,1)S(1)}, u32[]{:S(2)}, u32[]{:S(2)}) collective-permute-start(bf16[128,256]{1,0:T(8,128)(2,1)S(1)} %pad_maximum_fusion.2.refs_10_), channel_id=1, source_target_pairs={{64,0},{65,1},{66,2},{67,3},{68,4},{69,5},{70,6},{71,7},{72,8},{73... | collective-permute-start | bytes 196616 | tf_op jit(solution)/shard_map/ppermute | solution.py:41
  (59 other events, 558.0 us)
